TPU v7x, 32 devices: a whole 2x2x4 slice. The times are simulated.
32 devices in a mesh: ctx: 8 (over z, core), fsdp: 4 (over y, x).
Axes of the slice: x: 2, y: 2, z: 4, core: 2. Of those that a mesh axis runs over, the one named last changes fastest.
Arguments:
- tokens: bfloat16 [16, 1536, 768], P('fsdp', 'ctx'), may hold values from -6 to 6
- lengths: int32 [16], P('fsdp'), may hold values from 384 to 1536, as said below
- cotangent: bfloat16 [16, 1536, 768], P('fsdp', 'ctx'), may hold values from -6 to 6
- qkv_weight: bfloat16 [768, 2304], P('fsdp'), may hold values from -0.21875 to 0.21875
- qkv_bias: bfloat16 [2304], P('fsdp'), may hold values from -3 to 3
- out_weight: bfloat16 [768, 768], P('fsdp'), may hold values from -0.875 to 0.875
- out_bias: bfloat16 [768], P('fsdp'), may hold values from -2 to 2
- up_weight: bfloat16 [768, 3072], P('fsdp'), may hold values from -0.21875 to 0.21875
- up_bias: bfloat16 [3072], P('fsdp'), may hold values from -3 to 3
- down_weight: bfloat16 [3072, 768], P('fsdp'), may hold values from -0.109375 to 0.109375
- down_bias: bfloat16 [768], P('fsdp'), may hold values from -2 to 2
- attn_gain: bfloat16 [768], P('fsdp'), may hold values from 0.099609375 to 1.8984375
- attn_shift: bfloat16 [768], P('fsdp'), may hold values from -2 to 2
- mlp_gain: bfloat16 [768], P('fsdp'), may hold values from 0.099609375 to 1.8984375
- mlp_shift: bfloat16 [768], P('fsdp'), may hold values from -2 to 2
Outputs:
- layer_out: bfloat16 [16, 1536, 768], P('fsdp', 'ctx')
- tokens_grad: float32 [16, 1536, 768], P('fsdp', 'ctx')
- qkv_weight_grad: float32 [768, 2304], P('fsdp')
- qkv_bias_grad: float32 [2304], P('fsdp')
- out_weight_grad: float32 [768, 768], P('fsdp')
- out_bias_grad: float32 [768], P('fsdp')
- up_weight_grad: float32 [768, 3072], P('fsdp')
- up_bias_grad: float32 [3072], P('fsdp')
- down_weight_grad: float32 [3072, 768], P('fsdp')
- down_bias_grad: float32 [768], P('fsdp')
- attn_gain_grad: float32 [768], P('fsdp')
- attn_shift_grad: float32 [768], P('fsdp')
- mlp_gain_grad: float32 [768], P('fsdp')
- mlp_shift_grad: float32 [768], P('fsdp')
Inputs may be any that keep to these rules, and one draw needn't show every extreme that they name: `lengths`: in each group of 4 sequences on one index of fsdp, one sequence chosen by the seed has length 1536.
All inputs are finite; a program needn't handle non-finite values.
Results may differ from a plain program's by a relative error of at most 0.02.
Values may be sent and summed in bfloat16 or wider, within the bound.
No kernel may reach another device: no remote copies, remote signals or barrier semaphores. Data moves between devices by JAX's collectives and lax.ppermute only.
A program may use at most 256 MiB of HBM per device.

v0:
```python
import math

import jax
import jax.numpy as jnp
from jax import lax
from jax.sharding import PartitionSpec as P

D = 768
HEADS = 12
HEAD_DIM = 64
ROTARY = 16


norm_eps = 1e-05
masked_score = -1e30
rope_base = 10000.0
inv_sqrt_two = 0.7071067811865476
inv_sqrt_tau = 0.3989422804014327


def from_behind(x, axis, by):
    devices = lax.axis_size(axis)
    pairs = [(i, i + by) for i in range(devices) if 0 <= i + by < devices]
    return lax.ppermute(x, axis, pairs)


def passed_along(value, axis, steps):
    count = lax.axis_size(axis)
    pairs = [(source, (source + steps) % count) for source in range(count)]
    return lax.ppermute(value, axis, pairs)


def tables(positions):
    half_rot = ROTARY // 2
    frequency = rope_base ** (-2.0 * jnp.arange(half_rot, dtype=jnp.float32) / ROTARY)
    angles = positions.astype(jnp.float32)[:, None] * frequency[None, :]
    return (jnp.cos(angles)[:, None, :], jnp.sin(angles)[:, None, :])


def rotate(field, cosine, sine):
    half_rot = ROTARY // 2
    first_half = field[..., :half_rot]
    second_half = field[..., half_rot:ROTARY]
    return jnp.concatenate(
        [
            first_half * cosine - second_half * sine,
            second_half * cosine + first_half * sine,
            field[..., ROTARY:],
        ],
        -1,
    )


def permitted(query_pos, key_pos, seq_lengths):
    causal = key_pos[None, :] <= query_pos[:, None]
    live = key_pos[None, None, :] < seq_lengths[:, None, None]
    return (causal[None] & live)[:, None]


def score_grads(
    queries, grad_mixed, row_lse, row_delta, query_pos, keys_part, values_part, key_pos, seq_lengths
):
    att_scale = HEAD_DIM ** (-0.5)
    allowed = permitted(query_pos, key_pos, seq_lengths)
    scores = (
        jnp.einsum("sqhd,skhd->shqk", queries, keys_part, preferred_element_type=jnp.float32)
        * att_scale
    )
    scores = jnp.where(allowed, scores, masked_score)
    probs = jnp.where(allowed, jnp.exp(scores - row_lse[..., None]), 0.0)
    grad_probs = jnp.einsum(
        "sqhd,skhd->shqk", grad_mixed, values_part, preferred_element_type=jnp.float32
    )
    grad_scores = (probs * (grad_probs - row_delta[..., None])).astype(jnp.bfloat16)
    return (grad_scores, probs.astype(jnp.bfloat16))


def local(
    tokens,
    lengths,
    cotangent,
    qkv_weight,
    qkv_bias,
    out_weight,
    out_bias,
    up_weight,
    up_bias,
    down_weight,
    down_bias,
    attn_gain,
    attn_shift,
    mlp_gain,
    mlp_shift,
):
    (
        full_qkv,
        full_qkv_bias,
        full_out,
        full_out_bias,
        full_up,
        full_up_bias,
        full_down,
        full_down_bias,
        full_attn_gain,
        full_attn_shift,
        full_mlp_gain,
        full_mlp_shift,
    ) = (
        lax.all_gather(qkv_weight, "fsdp", axis=0, tiled=True),
        lax.all_gather(qkv_bias, "fsdp", axis=0, tiled=True),
        lax.all_gather(out_weight, "fsdp", axis=0, tiled=True),
        lax.all_gather(out_bias, "fsdp", axis=0, tiled=True),
        lax.all_gather(up_weight, "fsdp", axis=0, tiled=True),
        lax.all_gather(up_bias, "fsdp", axis=0, tiled=True),
        lax.all_gather(down_weight, "fsdp", axis=0, tiled=True),
        lax.all_gather(down_bias, "fsdp", axis=0, tiled=True),
        lax.all_gather(attn_gain, "fsdp", axis=0, tiled=True),
        lax.all_gather(attn_shift, "fsdp", axis=0, tiled=True),
        lax.all_gather(mlp_gain, "fsdp", axis=0, tiled=True),
        lax.all_gather(mlp_shift, "fsdp", axis=0, tiled=True),
    )
    seqs_here = tokens.shape[0]
    width = tokens.shape[1]
    row_count = seqs_here * width
    att_scale = HEAD_DIM ** (-0.5)
    ctx_size = lax.axis_size("ctx")
    ctx_here = lax.axis_index("ctx")
    query_pos = ctx_here * width + jnp.arange(width, dtype=jnp.int32)
    cosine, sine = tables(query_pos)
    tok_rows = tokens.reshape(row_count, D).astype(jnp.float32)
    center = tok_rows - jnp.mean(tok_rows, -1, keepdims=True)
    inv_spread = lax.rsqrt(jnp.mean(center * center, -1, keepdims=True) + norm_eps)
    normed = center * inv_spread
    attn_in = (normed * full_attn_gain + full_attn_shift).astype(jnp.bfloat16)
    mlp_in = (normed * full_mlp_gain + full_mlp_shift).astype(jnp.bfloat16)
    projected = jnp.dot(attn_in, full_qkv, preferred_element_type=jnp.float32) + full_qkv_bias
    head_shape = (seqs_here, width, HEADS, HEAD_DIM)
    queries = rotate(projected[:, :D].reshape(head_shape), cosine, sine).astype(jnp.bfloat16)
    keys_own = rotate(projected[:, D : 2 * D].reshape(head_shape), cosine, sine).astype(
        jnp.bfloat16
    )
    values_own = projected[:, 2 * D :].reshape(head_shape).astype(jnp.bfloat16)
    stat_shape = (seqs_here, HEADS, width)
    init_state = (
        jnp.full(stat_shape, masked_score, jnp.float32),
        jnp.zeros(stat_shape, jnp.float32),
        jnp.zeros((seqs_here, HEADS, width, HEAD_DIM), jnp.float32),
    )
    keys_piece = lax.all_gather(keys_own, "ctx", axis=1, tiled=True)
    values_piece = lax.all_gather(values_own, "ctx", axis=1, tiled=True)
    piece_len = keys_piece.shape[1]
    part_len = math.gcd(piece_len, width)

    def inner(part_index, running):
        best_score, denom, accum = running
        offset = part_index * part_len
        keys_part = lax.dynamic_slice_in_dim(keys_piece, offset, part_len, 1)
        values_part = lax.dynamic_slice_in_dim(values_piece, offset, part_len, 1)
        key_pos = offset + jnp.arange(part_len, dtype=jnp.int32)
        allowed = permitted(query_pos, key_pos, lengths)
        scores = (
            jnp.einsum("sqhd,skhd->shqk", queries, keys_part, preferred_element_type=jnp.float32)
            * att_scale
        )
        scores = jnp.where(allowed, scores, masked_score)
        new_best = jnp.maximum(best_score, jnp.max(scores, -1))
        weights = jnp.where(allowed, jnp.exp(scores - new_best[..., None]), 0.0)
        fading = jnp.exp(best_score - new_best)
        denom = denom * fading + jnp.sum(weights, -1)
        accum = accum * fading[..., None] + jnp.einsum(
            "shqk,skhd->shqd",
            weights.astype(jnp.bfloat16),
            values_part,
            preferred_element_type=jnp.float32,
        )
        return (new_best, denom, accum)

    best_score, denom, accum = lax.fori_loop(0, piece_len // part_len, inner, init_state)
    row_lse = best_score + jnp.log(denom)
    mixed_f = accum / denom[..., None]
    mixed = mixed_f.astype(jnp.bfloat16)
    out_heads = full_out.reshape(HEADS, HEAD_DIM, D)
    attn_out = (
        jnp.einsum("shqd,hde->sqe", mixed, out_heads, preferred_element_type=jnp.float32)
        + full_out_bias
    )
    pre_act = jnp.dot(mlp_in, full_up, preferred_element_type=jnp.float32) + full_up_bias
    hidden = jax.nn.gelu(pre_act, approximate=False).astype(jnp.bfloat16)
    mlp_out = jnp.dot(hidden, full_down, preferred_element_type=jnp.float32) + full_down_bias
    layer_out = (
        tokens.astype(jnp.float32) + attn_out + mlp_out.reshape(seqs_here, width, D)
    ).astype(jnp.bfloat16)
    grad_rows = cotangent.reshape(row_count, D)
    grad_float = grad_rows.astype(jnp.float32)
    down_grad = jnp.einsum("rf,rd->fd", hidden, grad_rows, preferred_element_type=jnp.float32)
    down_bias_grad = jnp.sum(grad_float, 0)
    grad_hidden = jnp.einsum("rd,fd->rf", grad_rows, full_down, preferred_element_type=jnp.float32)
    slope = (
        0.5 * (1.0 + lax.erf(pre_act * inv_sqrt_two))
        + pre_act * jnp.exp(-0.5 * pre_act * pre_act) * inv_sqrt_tau
    )
    grad_pre = (grad_hidden * slope).astype(jnp.bfloat16)
    up_bias_grad = jnp.sum(grad_pre.astype(jnp.float32), 0)
    up_grad = jnp.einsum("rd,rf->df", mlp_in, grad_pre, preferred_element_type=jnp.float32)
    grad_mlp_in = jnp.einsum("rf,df->rd", grad_pre, full_up, preferred_element_type=jnp.float32)
    out_grad = jnp.einsum(
        "shqd,sqe->hde", mixed, cotangent, preferred_element_type=jnp.float32
    ).reshape(D, D)
    grad_mixed = jnp.einsum(
        "sqe,hde->sqhd", cotangent, out_heads, preferred_element_type=jnp.float32
    ).astype(jnp.bfloat16)
    row_delta = jnp.einsum(
        "sqhd,shqd->shq", grad_mixed.astype(jnp.float32), mixed_f, precision=lax.Precision.HIGHEST
    )
    zeros_heads = jnp.zeros(head_shape, jnp.float32)

    def turn(turn_index, state):
        keys_now, values_now, carry_k, carry_v, carry_q = state
        source = (ctx_here - turn_index) % ctx_size
        key_pos = source * width + jnp.arange(width, dtype=jnp.int32)
        grad_scores, probs = score_grads(
            queries,
            grad_mixed,
            row_lse,
            row_delta,
            query_pos,
            keys_now,
            values_now,
            key_pos,
            lengths,
        )
        carry_q = (
            carry_q
            + jnp.einsum(
                "shqk,skhd->sqhd", grad_scores, keys_now, preferred_element_type=jnp.float32
            )
            * att_scale
        )
        carry_k = (
            carry_k
            + jnp.einsum(
                "shqk,sqhd->skhd", grad_scores, queries, preferred_element_type=jnp.float32
            )
            * att_scale
        )
        carry_v = carry_v + jnp.einsum(
            "shqk,sqhd->skhd", probs, grad_mixed, preferred_element_type=jnp.float32
        )
        keys_now, values_now = from_behind((keys_now, values_now), "ctx", 1)
        carry_k, carry_v = (
            passed_along(carry_k.astype(jnp.bfloat16), "ctx", 1).astype(carry_k.dtype),
            passed_along(carry_v.astype(jnp.bfloat16), "ctx", 1).astype(carry_v.dtype),
        )
        return (keys_now, values_now, carry_k, carry_v, carry_q)

    final_state = lax.fori_loop(
        0, ctx_size, turn, (keys_own, values_own, zeros_heads, zeros_heads, zeros_heads)
    )
    grad_k = final_state[2]
    grad_v = final_state[3]
    grad_q = final_state[4]
    back_q = rotate(grad_q, cosine, -sine).reshape(seqs_here, width, D)
    back_k = rotate(grad_k, cosine, -sine).reshape(seqs_here, width, D)
    grad_proj = (
        jnp.concatenate([back_q, back_k, grad_v.reshape(seqs_here, width, D)], -1)
        .reshape(row_count, 3 * D)
        .astype(jnp.bfloat16)
    )
    qkv_bias_grad = jnp.sum(grad_proj.astype(jnp.float32), 0)
    qkv_grad = jnp.einsum("rd,re->de", attn_in, grad_proj, preferred_element_type=jnp.float32)
    grad_attn_in = jnp.einsum("re,de->rd", grad_proj, full_qkv, preferred_element_type=jnp.float32)
    attn_gain_grad = jnp.sum(grad_attn_in * normed, 0)
    attn_shift_grad = jnp.sum(grad_attn_in, 0)
    mlp_gain_grad = jnp.sum(grad_mlp_in * normed, 0)
    mlp_shift_grad = jnp.sum(grad_mlp_in, 0)
    grad_normed = grad_attn_in * full_attn_gain + grad_mlp_in * full_mlp_gain
    tokens_grad = grad_float + inv_spread * (
        grad_normed
        - jnp.mean(grad_normed, -1, keepdims=True)
        - normed * jnp.mean(grad_normed * normed, -1, keepdims=True)
    )
    tokens_grad = tokens_grad.reshape(seqs_here, width, D)
    summed = (
        lax.psum(qkv_grad.astype(jnp.bfloat16), "ctx").astype(jnp.float32),
        lax.psum(qkv_bias_grad.astype(jnp.bfloat16), "ctx").astype(jnp.float32),
        lax.psum(out_grad.astype(jnp.bfloat16), "ctx").astype(jnp.float32),
        lax.psum(down_bias_grad.astype(jnp.bfloat16), "ctx").astype(jnp.float32),
        lax.psum(up_grad.astype(jnp.bfloat16), "ctx").astype(jnp.float32),
        lax.psum(up_bias_grad.astype(jnp.bfloat16), "ctx").astype(jnp.float32),
        lax.psum(down_grad.astype(jnp.bfloat16), "ctx").astype(jnp.float32),
        lax.psum(down_bias_grad.astype(jnp.bfloat16), "ctx").astype(jnp.float32),
        lax.psum(attn_gain_grad.astype(jnp.bfloat16), "ctx").astype(jnp.float32),
        lax.psum(attn_shift_grad.astype(jnp.bfloat16), "ctx").astype(jnp.float32),
        lax.psum(mlp_gain_grad.astype(jnp.bfloat16), "ctx").astype(jnp.float32),
        lax.psum(mlp_shift_grad.astype(jnp.bfloat16), "ctx").astype(jnp.float32),
    )
    owned = (
        lax.psum_scatter(
            summed[0].astype(jnp.bfloat16), "fsdp", scatter_dimension=0, tiled=True
        ).astype(jnp.float32),
        lax.psum_scatter(
            summed[1].astype(jnp.bfloat16), "fsdp", scatter_dimension=0, tiled=True
        ).astype(jnp.float32),
        lax.psum_scatter(
            summed[2].astype(jnp.bfloat16), "fsdp", scatter_dimension=0, tiled=True
        ).astype(jnp.float32),
        lax.psum_scatter(
            summed[3].astype(jnp.bfloat16), "fsdp", scatter_dimension=0, tiled=True
        ).astype(jnp.float32),
        lax.psum_scatter(
            summed[4].astype(jnp.bfloat16), "fsdp", scatter_dimension=0, tiled=True
        ).astype(jnp.float32),
        lax.psum_scatter(
            summed[5].astype(jnp.bfloat16), "fsdp", scatter_dimension=0, tiled=True
        ).astype(jnp.float32),
        lax.psum_scatter(
            summed[6].astype(jnp.bfloat16), "fsdp", scatter_dimension=0, tiled=True
        ).astype(jnp.float32),
        lax.psum_scatter(
            summed[7].astype(jnp.bfloat16), "fsdp", scatter_dimension=0, tiled=True
        ).astype(jnp.float32),
        lax.psum_scatter(
            summed[8].astype(jnp.bfloat16), "fsdp", scatter_dimension=0, tiled=True
        ).astype(jnp.float32),
        lax.psum_scatter(
            summed[9].astype(jnp.bfloat16), "fsdp", scatter_dimension=0, tiled=True
        ).astype(jnp.float32),
        lax.psum_scatter(
            summed[10].astype(jnp.bfloat16), "fsdp", scatter_dimension=0, tiled=True
        ).astype(jnp.float32),
        lax.psum_scatter(
            summed[11].astype(jnp.bfloat16), "fsdp", scatter_dimension=0, tiled=True
        ).astype(jnp.float32),
    )
    return (
        layer_out,
        tokens_grad,
        owned[0],
        owned[1],
        owned[2],
        owned[3],
        owned[4],
        owned[5],
        owned[6],
        owned[7],
        owned[8],
        owned[9],
        owned[10],
        owned[11],
    )


def solution(mesh):
    in_specs = (
        P("fsdp", "ctx", None),
        P("fsdp"),
        P("fsdp", "ctx", None),
        P("fsdp", None),
        P("fsdp"),
        P("fsdp", None),
        P("fsdp"),
        P("fsdp", None),
        P("fsdp"),
        P("fsdp", None),
        P("fsdp"),
        P("fsdp"),
        P("fsdp"),
        P("fsdp"),
        P("fsdp"),
    )
    out_specs = (
        P("fsdp", "ctx", None),
        P("fsdp", "ctx", None),
        P("fsdp", None),
        P("fsdp"),
        P("fsdp", None),
        P("fsdp"),
        P("fsdp", None),
        P("fsdp"),
        P("fsdp", None),
        P("fsdp"),
        P("fsdp"),
        P("fsdp"),
        P("fsdp"),
        P("fsdp"),
    )
    return jax.shard_map(local, mesh=mesh, in_specs=in_specs, out_specs=out_specs, check_vma=False)
```

profile of v0, /device:TPU:0, one launch (start us, length us, event | category | flops | bytes accessed | tf_op | source)
XLA Modules:
  0.0 1593.5 jit_solution(15017884526174297412)
XLA Ops:
  12.6 17.8 %all-reduce.17 = (bf16[768]{0:T(1024)(128)(2,1)S(1)}, bf16[768]{0:T(1024)(128)(2,1)S(1)}, bf16[768]{0:T(1024)(128)(2,1)S(1)}, bf16[768]{0:T(1024)(128)(2,1)S(1)}, bf16[2304]{0:T(1024)(128)(2,1)S(1)}) all-reduce(bf16[768]{0:T(1024)(128)(2,1)S(1)} %dynamic-update-slice.5, ...), channel_id=1, replica_groups=mesh['ctx'=8,'fsdp'=4] {'fsdp'}, use_global_device_ids=true, to_apply=%add.5 | all-reduce | flops 5376 | bytes 21504
  33.8 26.2 %all-gather.8.cloned.1.call-done = bf16[768,2304]{1,0:T(8,128)(2,1)} async-done(((bf16[192,2304]{1,0:T(8,128)(2,1)}), bf16[768,2304]{1,0:T(8,128)(2,1)}) %all-gather.8.cloned.1.call-update) | async-done | bytes 3538960 | tf_op jit(solution)/shard_map/all_gather | solution.py:109
  103.6 8.2 all-gather
  111.8 7.2 all-gather.16.cloned.1.call-done
  119.1 26.6 %fusion.43 = (bf16[768,3072]{1,0:T(8,128)(2,1)}, f32[768,3072]{1,0:T(8,128)}) fusion(f32[3072]{0:T(1024)S(1)} %bitcast.151, bf16[768,768]{1,0:T(8,128)(2,1)} %get-tuple-element.719, bf16[768,3072]{1,0:T(8,128)(2,1)} %all-gather.16.cloned.1.call-done), kind=kOutput, calls=%fused_computation.58 | convolution fusion | flops 3779592192 | bytes 20066304 | tf_op jit(solution)/shard_map/dot_general | solution.py:187
  145.7 32.4 %all-gather.18.cloned.1.call-done = bf16[3072,768]{1,0:T(8,128)(2,1)} async-done(((bf16[768,768]{1,0:T(8,128)(2,1)}), bf16[3072,768]{1,0:T(8,128)(2,1)}) %all-gather.18.cloned.1.call-update) | async-done | bytes 4718608 | tf_op jit(solution)/shard_map/all_gather | solution.py:115
  178.0 10.4 fusion.73
  196.4 10.3 reduce-scatter.11.cloned.1.call-start
  219.2 129.3 %all-gather.10.cloned.1.call-done = bf16[4,1536,12,64]{3,0,2,1:T(4,128)(2,1)} async-done(((bf16[4,192,12,64]{3,0,2,1:T(4,128)(2,1)}), bf16[4,1536,12,64]{3,0,2,1:T(4,128)(2,1)}) %all-gather.10.cloned.1.call-update) | async-done | bytes 9437200 | tf_op jit(solution)/shard_map/all_gather | solution.py:149
  348.4 27.7 %copy.67 = bf16[4,1536,12,64]{1,3,2,0:T(8,128)(2,1)} copy(bf16[4,1536,12,64]{3,0,2,1:T(4,128)(2,1)} %all-gather.10.cloned.1.call-done) | data formatting | bytes 18874368
  376.2 140.9 %all-gather.12.cloned.1.call-done = bf16[4,1536,12,64]{3,0,2,1:T(4,128)(2,1)} async-done(((bf16[4,192,12,64]{3,0,2,1:T(4,128)(2,1)}), bf16[4,1536,12,64]{3,0,2,1:T(4,128)(2,1)}) %all-gather.12.cloned.1.call-update) | async-done | bytes 9437200 | tf_op jit(solution)/shard_map/all_gather | solution.py:150
  517.0 27.2 %copy.69 = bf16[4,1536,12,64]{1,3,2,0:T(8,128)(2,1)} copy(bf16[4,1536,12,64]{3,0,2,1:T(4,128)(2,1)} %all-gather.12.cloned.1.call-done) | data formatting | bytes 18874368
  544.2 175.5 %while.42 = (s32[]{:T(128)}, f32[4,12,192]{2,1,0:T(8,128)S(1)}, f32[4,12,192]{2,1,0:T(8,128)S(1)}, f32[4,12,192,64]{2,3,1,0:T(8,128)}, s32[4]{0:T(128)S(1)}, /*i...) while((s32[]{:T(128)}, f32[4,12,192]{2,1,0:T(8,128)S(1)}, ...), condition=%wide.region_5.6_spmd.clone, body=%wide.region_2.5_spmd.clone.sunk | while | flops 477988992 | bytes 60634608 | solution.py:178
  544.6 7.7 fusion.129
  552.3 7.4 fusion.130
  566.7 7.9 fusion.129
  574.6 6.7 fusion.130
  581.4 7.0 fusion.132
  588.8 7.7 fusion.129
  596.5 6.7 fusion.130
  603.3 7.1 fusion.132
  610.8 7.7 fusion.129
  618.4 6.9 fusion.130
  625.4 6.9 fusion.132
  632.8 7.7 fusion.129
  640.5 6.7 fusion.130
  647.3 7.7 fusion.132
  655.4 7.7 fusion.129
  663.1 6.7 fusion.130
  669.9 6.9 fusion.132
  677.2 7.7 fusion.129
  691.5 6.9 fusion.132
  698.9 7.4 fusion.129
  713.0 6.7 fusion.132
  729.0 639.5 %while.43 = (s32[]{:T(128)}, bf16[4,192,12,64]{1,3,2,0:T(8,128)(2,1)}, bf16[4,192,12,64]{1,3,2,0:T(8,128)(2,1)}, f32[4,192,12,64]{1,3,2,0:T(8,128)}, f32[4,192,1...) while((s32[]{:T(128)}, ...), condition=%wide.region_7.8_spmd.clone, body=%wide.region_6.7_spmd.clone.sunk | while | flops 1160959104 | bytes 120956752 | solution.py:256
  769.2 13.3 collective-permute-done.3
  800.6 26.4 %collective-permute-start.2 = (bf16[4,192,12,64]{1,3,2,0:T(8,128)(2,1)}, bf16[4,192,12,64]{1,3,2,0:T(8,128)(2,1)}, u32[]{:S(2)}, u32[]{:S(2)}) collective-permute-start(bf16[4,192,12,64]{1,3,2,0:T(8,128)(2,1)} %fusion.144), channel_id=1, source_target_pairs={{0,4},{4,8},{8,12},{12,16},{16,20},{20,24},{24,28},{28,0},{1,5},{5... | collective-permute-start | bytes 3538952 | tf_op jit(solution)/shard_map/while/body/eval_jaxpr/ppermute | solution.py:30
  870.7 41.6 %collective-permute-start.2 = (bf16[4,192,12,64]{1,3,2,0:T(8,128)(2,1)}, bf16[4,192,12,64]{1,3,2,0:T(8,128)(2,1)}, u32[]{:S(2)}, u32[]{:S(2)}) collective-permute-start(bf16[4,192,12,64]{1,3,2,0:T(8,128)(2,1)} %fusion.144), channel_id=1, source_target_pairs={{0,4},{4,8},{8,12},{12,16},{16,20},{20,24},{24,28},{28,0},{1,5},{5... | collective-permute-start | bytes 3538952 | tf_op jit(solution)/shard_map/while/body/eval_jaxpr/ppermute | solution.py:30
  956.0 41.6 %collective-permute-start.2 = (bf16[4,192,12,64]{1,3,2,0:T(8,128)(2,1)}, bf16[4,192,12,64]{1,3,2,0:T(8,128)(2,1)}, u32[]{:S(2)}, u32[]{:S(2)}) collective-permute-start(bf16[4,192,12,64]{1,3,2,0:T(8,128)(2,1)} %fusion.144), channel_id=1, source_target_pairs={{0,4},{4,8},{8,12},{12,16},{16,20},{20,24},{24,28},{28,0},{1,5},{5... | collective-permute-start | bytes 3538952 | tf_op jit(solution)/shard_map/while/body/eval_jaxpr/ppermute | solution.py:30
  1041.3 41.6 %collective-permute-start.2 = (bf16[4,192,12,64]{1,3,2,0:T(8,128)(2,1)}, bf16[4,192,12,64]{1,3,2,0:T(8,128)(2,1)}, u32[]{:S(2)}, u32[]{:S(2)}) collective-permute-start(bf16[4,192,12,64]{1,3,2,0:T(8,128)(2,1)} %fusion.144), channel_id=1, source_target_pairs={{0,4},{4,8},{8,12},{12,16},{16,20},{20,24},{24,28},{28,0},{1,5},{5... | collective-permute-start | bytes 3538952 | tf_op jit(solution)/shard_map/while/body/eval_jaxpr/ppermute | solution.py:30
  1126.7 41.6 %collective-permute-start.2 = (bf16[4,192,12,64]{1,3,2,0:T(8,128)(2,1)}, bf16[4,192,12,64]{1,3,2,0:T(8,128)(2,1)}, u32[]{:S(2)}, u32[]{:S(2)}) collective-permute-start(bf16[4,192,12,64]{1,3,2,0:T(8,128)(2,1)} %fusion.144), channel_id=1, source_target_pairs={{0,4},{4,8},{8,12},{12,16},{16,20},{20,24},{24,28},{28,0},{1,5},{5... | collective-permute-start | bytes 3538952 | tf_op jit(solution)/shard_map/while/body/eval_jaxpr/ppermute | solution.py:30
  1212.0 41.6 %collective-permute-start.2 = (bf16[4,192,12,64]{1,3,2,0:T(8,128)(2,1)}, bf16[4,192,12,64]{1,3,2,0:T(8,128)(2,1)}, u32[]{:S(2)}, u32[]{:S(2)}) collective-permute-start(bf16[4,192,12,64]{1,3,2,0:T(8,128)(2,1)} %fusion.144), channel_id=1, source_target_pairs={{0,4},{4,8},{8,12},{12,16},{16,20},{20,24},{24,28},{28,0},{1,5},{5... | collective-permute-start | bytes 3538952 | tf_op jit(solution)/shard_map/while/body/eval_jaxpr/ppermute | solution.py:30
  1297.4 41.6 %collective-permute-start.2 = (bf16[4,192,12,64]{1,3,2,0:T(8,128)(2,1)}, bf16[4,192,12,64]{1,3,2,0:T(8,128)(2,1)}, u32[]{:S(2)}, u32[]{:S(2)}) collective-permute-start(bf16[4,192,12,64]{1,3,2,0:T(8,128)(2,1)} %fusion.144), channel_id=1, source_target_pairs={{0,4},{4,8},{8,12},{12,16},{16,20},{20,24},{24,28},{28,0},{1,5},{5... | collective-permute-start | bytes 3538952 | tf_op jit(solution)/shard_map/while/body/eval_jaxpr/ppermute | solution.py:30
  1409.3 9.9 fusion.70
  1419.2 15.8 all-reduce.16
  1435.5 55.0 %all-reduce.14 = (bf16[576]{0:T(1024)(128)(2,1)S(1)}, bf16[192]{0:T(256)(128)(2,1)S(1)}, bf16[768]{0:T(1024)(128)(2,1)S(1)}, bf16[192]{0:T(256)(128)(2,1)S(1)}, ...) all-reduce(bf16[576]{0:T(1024)(128)(2,1)S(1)} %dynamic-slice.8, ...), channel_id=1, replica_groups=mesh['ctx'=8,'fsdp'=4] {'ctx'}, use_global_device_ids=true, to_apply=%region_13.14 | all-reduce | flops 2304 | bytes 9216 | tf_op jit(solution)/shard_map/psum | solution.py:285
  1497.4 7.5 convolution_add_fusion.1
  1507.3 72.0 %all-reduce.20.cloned.1.call-done = (bf16[192,2304]{1,0:T(8,128)(2,1)}, bf16[192,768]{1,0:T(8,128)(2,1)}, bf16[192,3072]{1,0:T(8,128)(2,1)}, bf16[768,768]{1,0:T(8,128)(2,1)}) async-done(((bf16[192,2304]{1,0:T(8,128)(2,1)}, bf16[192,768]{1,0:T(8,128)(2,1)}, bf16[192,3072]{1,0:T(8,128)(2,1)}, bf16[768,768]{1,0:T(8,128)(2,1)}), (bf16[192,2304]{1,0:T(8,128)(2,1)}, bf16[192,768]{1,0:T(8,128)(2,1)}, ...) | async-done | bytes 3538960 | tf_op jit(solution)/shard_map/psum | solution.py:284
  (543 shorter events, 508.0 us)
Async XLA Ops:
  7.3 52.8 %all-gather.8.cloned.1.call-start = ((), (), s32[]{:S(2)}) async-start(), calls=%async_computation.4 | async-start | bytes 4423680 | tf_op jit(solution)/shard_map/all_gather | solution.py:109
  8.0 111.1 %all-gather.16.cloned.1.call-start = ((), (), s32[]{:S(2)}) async-start(), calls=%async_computation.8 | async-start | bytes 5898240 | tf_op jit(solution)/shard_map/all_gather | solution.py:113
  8.7 169.3 %all-gather.18.cloned.1.call-start = ((), (), s32[]{:S(2)}) async-start(), calls=%async_computation.9 | async-start | bytes 5898240 | tf_op jit(solution)/shard_map/all_gather | solution.py:115
  9.5 339.0 %all-gather.10.cloned.1.call-start = ((), (), s32[]{:S(2)}) async-start(), calls=%async_computation.5 | async-start | bytes 21233664 | tf_op jit(solution)/shard_map/all_gather | solution.py:149
  32.1 53.7 %copy-start.24 = (f32[192,8]{0,1:T(8,128)}, f32[192,8]{0,1:T(8,128)S(1)}, u32[]{:S(2)}) copy-start(f32[192,8]{0,1:T(8,128)S(1)} %get-tuple-element.726) | copy-start | bytes 18436
  92.5 424.5 %all-gather.12.cloned.1.call-start = ((), (), s32[]{:S(2)}) async-start(), calls=%async_computation.6 | async-start | bytes 21233664 | tf_op jit(solution)/shard_map/all_gather | solution.py:150
  102.9 620.9 %all-gather.14.cloned.1.call-start = ((), (), s32[]{:S(2)}) async-start(), calls=%async_computation.7 | async-start | bytes 1474560 | tf_op jit(solution)/shard_map/all_gather | solution.py:111
  103.5 1393.8 %reduce-scatter.9.cloned.1.call-start = ((), (), s32[]{:S(2)}) async-start(), calls=%async_computation.12 | async-start | bytes 5898240 | tf_op jit(solution)/shard_map/reduce_scatter | solution.py:310
  196.4 1300.9 %reduce-scatter.11.cloned.1.call-start = ((), (), s32[]{:S(2)}) async-start(), calls=%async_computation.13 | async-start | bytes 5898240 | tf_op jit(solution)/shard_map/reduce_scatter | solution.py:316
  219.1 1278.2 %reduce-scatter.7.cloned.1.call-start = ((), (), s32[]{:S(2)}) async-start(), calls=%async_computation.11 | async-start | bytes 1474560 | tf_op jit(solution)/shard_map/reduce_scatter | solution.py:304
  376.2 168.1 %copy-start.26 = (s32[4]{0:T(128)S(1)}, s32[4]{0:T(128)}, u32[]{:S(2)}) copy-start(s32[4]{0:T(128)} %param.20) | copy-start | bytes 52
  544.2 175.5 %copy-start.10 = (bf16[4,192,768]{2,1,0:T(8,128)(2,1)S(1)}, bf16[4,192,768]{2,1,0:T(8,128)(2,1)}, u32[]{:S(2)}) copy-start(bf16[4,192,768]{2,1,0:T(8,128)(2,1)} %param.21) | copy-start | bytes 3538948
  728.7 768.6 %reduce-scatter.5.cloned.1.call-start = ((), (), s32[]{:S(2)}) async-start(), calls=%async_computation.10 | async-start | bytes 4423680 | tf_op jit(solution)/shard_map/reduce_scatter | solution.py:298
  743.7 22.0 %collective-permute-start.2 = (bf16[4,192,12,64]{1,3,2,0:T(8,128)(2,1)}, bf16[4,192,12,64]{1,3,2,0:T(8,128)(2,1)}, u32[]{:S(2)}, u32[]{:S(2)}) collective-permute-start(bf16[4,192,12,64]{1,3,2,0:T(8,128)(2,1)} %fusion.144), channel_id=1, source_target_pairs={{0,4},{4,8},{8,12},{12,16},{16,20},{20,24},{24,28},{28,0},{1,5},{5... | collective-permute-start | bytes 3538952 | tf_op jit(solution)/shard_map/while/body/eval_jaxpr/ppermute | solution.py:30
  748.4 34.1 %collective-permute-start.3 = (bf16[4,192,12,64]{1,3,2,0:T(8,128)(2,1)}, bf16[4,192,12,64]{1,3,2,0:T(8,128)(2,1)}, u32[]{:S(2)}, u32[]{:S(2)}) collective-permute-start(bf16[4,192,12,64]{1,3,2,0:T(8,128)(2,1)} %fusion.145), channel_id=1, source_target_pairs={{0,4},{4,8},{8,12},{12,16},{16,20},{20,24},{24,28},{28,0},{1,5},{5... | collective-permute-start | bytes 3538952 | tf_op jit(solution)/shard_map/while/body/eval_jaxpr/ppermute | solution.py:30
  748.8 37.2 %collective-permute-start = (bf16[4,192,12,64]{1,3,2,0:T(8,128)(2,1)S(1)}, bf16[4,192,12,64]{1,3,2,0:T(8,128)(2,1)}, u32[]{:S(2)}, u32[]{:S(2)}) collective-permute-start(bf16[4,192,12,64]{1,3,2,0:T(8,128)(2,1)S(1)} %copy.119), channel_id=1, source_target_pairs={{0,4},{4,8},{8,12},{12,16},{16,20},{20,24},{24,28},{1,5},{5,9},{9,... | collective-permute-start | bytes 3538952 | tf_op jit(solution)/shard_map/while/body/eval_jaxpr/ppermute | solution.py:24
  751.8 34.1 %collective-permute-start.1 = (bf16[4,192,12,64]{1,3,2,0:T(8,128)(2,1)}, bf16[4,192,12,64]{1,3,2,0:T(8,128)(2,1)}, u32[]{:S(2)}, u32[]{:S(2)}) collective-permute-start(bf16[4,192,12,64]{1,3,2,0:T(8,128)(2,1)} %copy.120), channel_id=1, source_target_pairs={{0,4},{4,8},{8,12},{12,16},{16,20},{20,24},{24,28},{1,5},{5,9},{9,... | collective-permute-start | bytes 3538952 | tf_op jit(solution)/shard_map/while/body/eval_jaxpr/ppermute | solution.py:24
  800.6 45.7 %collective-permute-start.2 = (bf16[4,192,12,64]{1,3,2,0:T(8,128)(2,1)}, bf16[4,192,12,64]{1,3,2,0:T(8,128)(2,1)}, u32[]{:S(2)}, u32[]{:S(2)}) collective-permute-start(bf16[4,192,12,64]{1,3,2,0:T(8,128)(2,1)} %fusion.144), channel_id=1, source_target_pairs={{0,4},{4,8},{8,12},{12,16},{16,20},{20,24},{24,28},{28,0},{1,5},{5... | collective-permute-start | bytes 3538952 | tf_op jit(solution)/shard_map/while/body/eval_jaxpr/ppermute | solution.py:30
  830.6 22.0 %collective-permute-start.3 = (bf16[4,192,12,64]{1,3,2,0:T(8,128)(2,1)}, bf16[4,192,12,64]{1,3,2,0:T(8,128)(2,1)}, u32[]{:S(2)}, u32[]{:S(2)}) collective-permute-start(bf16[4,192,12,64]{1,3,2,0:T(8,128)(2,1)} %fusion.145), channel_id=1, source_target_pairs={{0,4},{4,8},{8,12},{12,16},{16,20},{20,24},{24,28},{28,0},{1,5},{5... | collective-permute-start | bytes 3538952 | tf_op jit(solution)/shard_map/while/body/eval_jaxpr/ppermute | solution.py:30
  833.1 22.9 %collective-permute-start = (bf16[4,192,12,64]{1,3,2,0:T(8,128)(2,1)S(1)}, bf16[4,192,12,64]{1,3,2,0:T(8,128)(2,1)}, u32[]{:S(2)}, u32[]{:S(2)}) collective-permute-start(bf16[4,192,12,64]{1,3,2,0:T(8,128)(2,1)S(1)} %copy.119), channel_id=1, source_target_pairs={{0,4},{4,8},{8,12},{12,16},{16,20},{20,24},{24,28},{1,5},{5,9},{9,... | collective-permute-start | bytes 3538952 | tf_op jit(solution)/shard_map/while/body/eval_jaxpr/ppermute | solution.py:24
  837.2 18.9 %collective-permute-start.1 = (bf16[4,192,12,64]{1,3,2,0:T(8,128)(2,1)}, bf16[4,192,12,64]{1,3,2,0:T(8,128)(2,1)}, u32[]{:S(2)}, u32[]{:S(2)}) collective-permute-start(bf16[4,192,12,64]{1,3,2,0:T(8,128)(2,1)} %copy.120), channel_id=1, source_target_pairs={{0,4},{4,8},{8,12},{12,16},{16,20},{20,24},{24,28},{1,5},{5,9},{9,... | collective-permute-start | bytes 3538952 | tf_op jit(solution)/shard_map/while/body/eval_jaxpr/ppermute | solution.py:24
  870.7 60.9 %collective-permute-start.2 = (bf16[4,192,12,64]{1,3,2,0:T(8,128)(2,1)}, bf16[4,192,12,64]{1,3,2,0:T(8,128)(2,1)}, u32[]{:S(2)}, u32[]{:S(2)}) collective-permute-start(bf16[4,192,12,64]{1,3,2,0:T(8,128)(2,1)} %fusion.144), channel_id=1, source_target_pairs={{0,4},{4,8},{8,12},{12,16},{16,20},{20,24},{24,28},{28,0},{1,5},{5... | collective-permute-start | bytes 3538952 | tf_op jit(solution)/shard_map/while/body/eval_jaxpr/ppermute | solution.py:30
  916.0 22.0 %collective-permute-start.3 = (bf16[4,192,12,64]{1,3,2,0:T(8,128)(2,1)}, bf16[4,192,12,64]{1,3,2,0:T(8,128)(2,1)}, u32[]{:S(2)}, u32[]{:S(2)}) collective-permute-start(bf16[4,192,12,64]{1,3,2,0:T(8,128)(2,1)} %fusion.145), channel_id=1, source_target_pairs={{0,4},{4,8},{8,12},{12,16},{16,20},{20,24},{24,28},{28,0},{1,5},{5... | collective-permute-start | bytes 3538952 | tf_op jit(solution)/shard_map/while/body/eval_jaxpr/ppermute | solution.py:30
  918.5 22.9 %collective-permute-start = (bf16[4,192,12,64]{1,3,2,0:T(8,128)(2,1)S(1)}, bf16[4,192,12,64]{1,3,2,0:T(8,128)(2,1)}, u32[]{:S(2)}, u32[]{:S(2)}) collective-permute-start(bf16[4,192,12,64]{1,3,2,0:T(8,128)(2,1)S(1)} %copy.119), channel_id=1, source_target_pairs={{0,4},{4,8},{8,12},{12,16},{16,20},{20,24},{24,28},{1,5},{5,9},{9,... | collective-permute-start | bytes 3538952 | tf_op jit(solution)/shard_map/while/body/eval_jaxpr/ppermute | solution.py:24
  922.5 18.9 %collective-permute-start.1 = (bf16[4,192,12,64]{1,3,2,0:T(8,128)(2,1)}, bf16[4,192,12,64]{1,3,2,0:T(8,128)(2,1)}, u32[]{:S(2)}, u32[]{:S(2)}) collective-permute-start(bf16[4,192,12,64]{1,3,2,0:T(8,128)(2,1)} %copy.120), channel_id=1, source_target_pairs={{0,4},{4,8},{8,12},{12,16},{16,20},{20,24},{24,28},{1,5},{5,9},{9,... | collective-permute-start | bytes 3538952 | tf_op jit(solution)/shard_map/while/body/eval_jaxpr/ppermute | solution.py:24
  956.0 60.9 %collective-permute-start.2 = (bf16[4,192,12,64]{1,3,2,0:T(8,128)(2,1)}, bf16[4,192,12,64]{1,3,2,0:T(8,128)(2,1)}, u32[]{:S(2)}, u32[]{:S(2)}) collective-permute-start(bf16[4,192,12,64]{1,3,2,0:T(8,128)(2,1)} %fusion.144), channel_id=1, source_target_pairs={{0,4},{4,8},{8,12},{12,16},{16,20},{20,24},{24,28},{28,0},{1,5},{5... | collective-permute-start | bytes 3538952 | tf_op jit(solution)/shard_map/while/body/eval_jaxpr/ppermute | solution.py:30
  1001.3 22.0 %collective-permute-start.3 = (bf16[4,192,12,64]{1,3,2,0:T(8,128)(2,1)}, bf16[4,192,12,64]{1,3,2,0:T(8,128)(2,1)}, u32[]{:S(2)}, u32[]{:S(2)}) collective-permute-start(bf16[4,192,12,64]{1,3,2,0:T(8,128)(2,1)} %fusion.145), channel_id=1, source_target_pairs={{0,4},{4,8},{8,12},{12,16},{16,20},{20,24},{24,28},{28,0},{1,5},{5... | collective-permute-start | bytes 3538952 | tf_op jit(solution)/shard_map/while/body/eval_jaxpr/ppermute | solution.py:30
  1003.8 22.9 %collective-permute-start = (bf16[4,192,12,64]{1,3,2,0:T(8,128)(2,1)S(1)}, bf16[4,192,12,64]{1,3,2,0:T(8,128)(2,1)}, u32[]{:S(2)}, u32[]{:S(2)}) collective-permute-start(bf16[4,192,12,64]{1,3,2,0:T(8,128)(2,1)S(1)} %copy.119), channel_id=1, source_target_pairs={{0,4},{4,8},{8,12},{12,16},{16,20},{20,24},{24,28},{1,5},{5,9},{9,... | collective-permute-start | bytes 3538952 | tf_op jit(solution)/shard_map/while/body/eval_jaxpr/ppermute | solution.py:24
  1007.9 18.9 %collective-permute-start.1 = (bf16[4,192,12,64]{1,3,2,0:T(8,128)(2,1)}, bf16[4,192,12,64]{1,3,2,0:T(8,128)(2,1)}, u32[]{:S(2)}, u32[]{:S(2)}) collective-permute-start(bf16[4,192,12,64]{1,3,2,0:T(8,128)(2,1)} %copy.120), channel_id=1, source_target_pairs={{0,4},{4,8},{8,12},{12,16},{16,20},{20,24},{24,28},{1,5},{5,9},{9,... | collective-permute-start | bytes 3538952 | tf_op jit(solution)/shard_map/while/body/eval_jaxpr/ppermute | solution.py:24
  1041.3 60.9 %collective-permute-start.2 = (bf16[4,192,12,64]{1,3,2,0:T(8,128)(2,1)}, bf16[4,192,12,64]{1,3,2,0:T(8,128)(2,1)}, u32[]{:S(2)}, u32[]{:S(2)}) collective-permute-start(bf16[4,192,12,64]{1,3,2,0:T(8,128)(2,1)} %fusion.144), channel_id=1, source_target_pairs={{0,4},{4,8},{8,12},{12,16},{16,20},{20,24},{24,28},{28,0},{1,5},{5... | collective-permute-start | bytes 3538952 | tf_op jit(solution)/shard_map/while/body/eval_jaxpr/ppermute | solution.py:30
  1086.6 22.0 %collective-permute-start.3 = (bf16[4,192,12,64]{1,3,2,0:T(8,128)(2,1)}, bf16[4,192,12,64]{1,3,2,0:T(8,128)(2,1)}, u32[]{:S(2)}, u32[]{:S(2)}) collective-permute-start(bf16[4,192,12,64]{1,3,2,0:T(8,128)(2,1)} %fusion.145), channel_id=1, source_target_pairs={{0,4},{4,8},{8,12},{12,16},{16,20},{20,24},{24,28},{28,0},{1,5},{5... | collective-permute-start | bytes 3538952 | tf_op jit(solution)/shard_map/while/body/eval_jaxpr/ppermute | solution.py:30
  1089.1 22.9 %collective-permute-start = (bf16[4,192,12,64]{1,3,2,0:T(8,128)(2,1)S(1)}, bf16[4,192,12,64]{1,3,2,0:T(8,128)(2,1)}, u32[]{:S(2)}, u32[]{:S(2)}) collective-permute-start(bf16[4,192,12,64]{1,3,2,0:T(8,128)(2,1)S(1)} %copy.119), channel_id=1, source_target_pairs={{0,4},{4,8},{8,12},{12,16},{16,20},{20,24},{24,28},{1,5},{5,9},{9,... | collective-permute-start | bytes 3538952 | tf_op jit(solution)/shard_map/while/body/eval_jaxpr/ppermute | solution.py:24
  1093.2 18.9 %collective-permute-start.1 = (bf16[4,192,12,64]{1,3,2,0:T(8,128)(2,1)}, bf16[4,192,12,64]{1,3,2,0:T(8,128)(2,1)}, u32[]{:S(2)}, u32[]{:S(2)}) collective-permute-start(bf16[4,192,12,64]{1,3,2,0:T(8,128)(2,1)} %copy.120), channel_id=1, source_target_pairs={{0,4},{4,8},{8,12},{12,16},{16,20},{20,24},{24,28},{1,5},{5,9},{9,... | collective-permute-start | bytes 3538952 | tf_op jit(solution)/shard_map/while/body/eval_jaxpr/ppermute | solution.py:24
  1126.7 60.9 %collective-permute-start.2 = (bf16[4,192,12,64]{1,3,2,0:T(8,128)(2,1)}, bf16[4,192,12,64]{1,3,2,0:T(8,128)(2,1)}, u32[]{:S(2)}, u32[]{:S(2)}) collective-permute-start(bf16[4,192,12,64]{1,3,2,0:T(8,128)(2,1)} %fusion.144), channel_id=1, source_target_pairs={{0,4},{4,8},{8,12},{12,16},{16,20},{20,24},{24,28},{28,0},{1,5},{5... | collective-permute-start | bytes 3538952 | tf_op jit(solution)/shard_map/while/body/eval_jaxpr/ppermute | solution.py:30
  1172.0 22.0 %collective-permute-start.3 = (bf16[4,192,12,64]{1,3,2,0:T(8,128)(2,1)}, bf16[4,192,12,64]{1,3,2,0:T(8,128)(2,1)}, u32[]{:S(2)}, u32[]{:S(2)}) collective-permute-start(bf16[4,192,12,64]{1,3,2,0:T(8,128)(2,1)} %fusion.145), channel_id=1, source_target_pairs={{0,4},{4,8},{8,12},{12,16},{16,20},{20,24},{24,28},{28,0},{1,5},{5... | collective-permute-start | bytes 3538952 | tf_op jit(solution)/shard_map/while/body/eval_jaxpr/ppermute | solution.py:30
  1174.5 22.9 %collective-permute-start = (bf16[4,192,12,64]{1,3,2,0:T(8,128)(2,1)S(1)}, bf16[4,192,12,64]{1,3,2,0:T(8,128)(2,1)}, u32[]{:S(2)}, u32[]{:S(2)}) collective-permute-start(bf16[4,192,12,64]{1,3,2,0:T(8,128)(2,1)S(1)} %copy.119), channel_id=1, source_target_pairs={{0,4},{4,8},{8,12},{12,16},{16,20},{20,24},{24,28},{1,5},{5,9},{9,... | collective-permute-start | bytes 3538952 | tf_op jit(solution)/shard_map/while/body/eval_jaxpr/ppermute | solution.py:24
  1178.5 18.9 %collective-permute-start.1 = (bf16[4,192,12,64]{1,3,2,0:T(8,128)(2,1)}, bf16[4,192,12,64]{1,3,2,0:T(8,128)(2,1)}, u32[]{:S(2)}, u32[]{:S(2)}) collective-permute-start(bf16[4,192,12,64]{1,3,2,0:T(8,128)(2,1)} %copy.120), channel_id=1, source_target_pairs={{0,4},{4,8},{8,12},{12,16},{16,20},{20,24},{24,28},{1,5},{5,9},{9,... | collective-permute-start | bytes 3538952 | tf_op jit(solution)/shard_map/while/body/eval_jaxpr/ppermute | solution.py:24
  1212.0 60.9 %collective-permute-start.2 = (bf16[4,192,12,64]{1,3,2,0:T(8,128)(2,1)}, bf16[4,192,12,64]{1,3,2,0:T(8,128)(2,1)}, u32[]{:S(2)}, u32[]{:S(2)}) collective-permute-start(bf16[4,192,12,64]{1,3,2,0:T(8,128)(2,1)} %fusion.144), channel_id=1, source_target_pairs={{0,4},{4,8},{8,12},{12,16},{16,20},{20,24},{24,28},{28,0},{1,5},{5... | collective-permute-start | bytes 3538952 | tf_op jit(solution)/shard_map/while/body/eval_jaxpr/ppermute | solution.py:30
  1257.3 22.0 %collective-permute-start.3 = (bf16[4,192,12,64]{1,3,2,0:T(8,128)(2,1)}, bf16[4,192,12,64]{1,3,2,0:T(8,128)(2,1)}, u32[]{:S(2)}, u32[]{:S(2)}) collective-permute-start(bf16[4,192,12,64]{1,3,2,0:T(8,128)(2,1)} %fusion.145), channel_id=1, source_target_pairs={{0,4},{4,8},{8,12},{12,16},{16,20},{20,24},{24,28},{28,0},{1,5},{5... | collective-permute-start | bytes 3538952 | tf_op jit(solution)/shard_map/while/body/eval_jaxpr/ppermute | solution.py:30
  1259.8 22.9 %collective-permute-start = (bf16[4,192,12,64]{1,3,2,0:T(8,128)(2,1)S(1)}, bf16[4,192,12,64]{1,3,2,0:T(8,128)(2,1)}, u32[]{:S(2)}, u32[]{:S(2)}) collective-permute-start(bf16[4,192,12,64]{1,3,2,0:T(8,128)(2,1)S(1)} %copy.119), channel_id=1, source_target_pairs={{0,4},{4,8},{8,12},{12,16},{16,20},{20,24},{24,28},{1,5},{5,9},{9,... | collective-permute-start | bytes 3538952 | tf_op jit(solution)/shard_map/while/body/eval_jaxpr/ppermute | solution.py:24
  1263.9 18.9 %collective-permute-start.1 = (bf16[4,192,12,64]{1,3,2,0:T(8,128)(2,1)}, bf16[4,192,12,64]{1,3,2,0:T(8,128)(2,1)}, u32[]{:S(2)}, u32[]{:S(2)}) collective-permute-start(bf16[4,192,12,64]{1,3,2,0:T(8,128)(2,1)} %copy.120), channel_id=1, source_target_pairs={{0,4},{4,8},{8,12},{12,16},{16,20},{20,24},{24,28},{1,5},{5,9},{9,... | collective-permute-start | bytes 3538952 | tf_op jit(solution)/shard_map/while/body/eval_jaxpr/ppermute | solution.py:24
  1297.4 60.9 %collective-permute-start.2 = (bf16[4,192,12,64]{1,3,2,0:T(8,128)(2,1)}, bf16[4,192,12,64]{1,3,2,0:T(8,128)(2,1)}, u32[]{:S(2)}, u32[]{:S(2)}) collective-permute-start(bf16[4,192,12,64]{1,3,2,0:T(8,128)(2,1)} %fusion.144), channel_id=1, source_target_pairs={{0,4},{4,8},{8,12},{12,16},{16,20},{20,24},{24,28},{28,0},{1,5},{5... | collective-permute-start | bytes 3538952 | tf_op jit(solution)/shard_map/while/body/eval_jaxpr/ppermute | solution.py:30
  1342.7 22.0 %collective-permute-start.3 = (bf16[4,192,12,64]{1,3,2,0:T(8,128)(2,1)}, bf16[4,192,12,64]{1,3,2,0:T(8,128)(2,1)}, u32[]{:S(2)}, u32[]{:S(2)}) collective-permute-start(bf16[4,192,12,64]{1,3,2,0:T(8,128)(2,1)} %fusion.145), channel_id=1, source_target_pairs={{0,4},{4,8},{8,12},{12,16},{16,20},{20,24},{24,28},{28,0},{1,5},{5... | collective-permute-start | bytes 3538952 | tf_op jit(solution)/shard_map/while/body/eval_jaxpr/ppermute | solution.py:30
  1345.1 22.9 %collective-permute-start = (bf16[4,192,12,64]{1,3,2,0:T(8,128)(2,1)S(1)}, bf16[4,192,12,64]{1,3,2,0:T(8,128)(2,1)}, u32[]{:S(2)}, u32[]{:S(2)}) collective-permute-start(bf16[4,192,12,64]{1,3,2,0:T(8,128)(2,1)S(1)} %copy.119), channel_id=1, source_target_pairs={{0,4},{4,8},{8,12},{12,16},{16,20},{20,24},{24,28},{1,5},{5,9},{9,... | collective-permute-start | bytes 3538952 | tf_op jit(solution)/shard_map/while/body/eval_jaxpr/ppermute | solution.py:24
  1349.2 18.9 %collective-permute-start.1 = (bf16[4,192,12,64]{1,3,2,0:T(8,128)(2,1)}, bf16[4,192,12,64]{1,3,2,0:T(8,128)(2,1)}, u32[]{:S(2)}, u32[]{:S(2)}) collective-permute-start(bf16[4,192,12,64]{1,3,2,0:T(8,128)(2,1)} %copy.120), channel_id=1, source_target_pairs={{0,4},{4,8},{8,12},{12,16},{16,20},{20,24},{24,28},{1,5},{5,9},{9,... | collective-permute-start | bytes 3538952 | tf_op jit(solution)/shard_map/while/body/eval_jaxpr/ppermute | solution.py:24
  1397.3 182.0 %all-reduce.20.cloned.1.call-start = ((), (), s32[]{:S(2)}) async-start(), calls=%async_computation.14 | async-start | bytes 7077888 | tf_op jit(solution)/shard_map/psum | solution.py:284
  1409.3 84.8 %copy-start.11 = (bf16[4,192,768]{2,1,0:T(8,128)(2,1)S(1)}, bf16[4,192,768]{2,1,0:T(8,128)(2,1)}, u32[]{:S(2)}) copy-start(bf16[4,192,768]{2,1,0:T(8,128)(2,1)} %param.21) | copy-start | bytes 3538948
  1491.8 94.4 %copy-start.42 = (f32[192]{0:T(256)}, f32[192]{0:T(256)S(1)}, u32[]{:S(2)}) copy-start(f32[192]{0:T(256)S(1)} %convert_element_type.261) | copy-start | bytes 2308
  (84 other events, 811.0 us)
Sparse Core Ops, SparseCore 0:
  9.9 50.0 all-gather.7
  61.8 57.1 all-gather.15
  120.9 57.0 all-gather.17
  180.1 168.2 all-gather.9
  350.5 166.4 all-gather.11
  518.7 25.9 all-gather.13
  547.6 57.0 reduce-scatter.8
  607.8 57.0 reduce-scatter.10
  728.9 26.7 reduce-scatter.6
  1397.5 88.5 reduce-scatter.4
  1497.5 81.7 all-reduce.19
where the time goes:
time: 1610 us; the launch traced here: 1590 us
  waiting for transfers between devices  449 us (28%)
  matrix products  363 us (23%)
  starting transfers between devices  356 us (22%)
  local copies, waits for them, and re-layouts  166 us (10%)
  other arithmetic  142 us (9%)
  blocking collectives  96.9 us (6%)
  between operations  18.2 us (1%)
    ppermute x16, starting transfers between devices, passed_along(): return lax.ppermute(value, axis, pairs)  294 us
    all_gather x1, waiting for transfers between devices, local(): values_piece = lax.all_gather(values_own, 'ctx', axis=1, tiled=True)  141 us
    all_gather x1, waiting for transfers between devices, local(): keys_piece = lax.all_gather(keys_own, 'ctx', axis=1, tiled=True)  129 us
    psum x1, waiting for transfers between devices, local(): lax.psum(qkv_grad.astype(jnp.bfloat16), 'ctx').astype(jnp.float32)  72 us
    unnamed x129, local copies, waits for them, and re-layouts  69.2 us
    dot_general x8, matrix products, inner(): jnp.einsum('sqhd,skhd->shqk', queries, keys_part, preferred_element_type=...  61.4 us
    dot_general x8, matrix products, inner(): jnp.einsum('shqk,skhd->shqd', weights.astype(jnp.bfloat16), values_part,...  55.9 us
    psum x1, blocking collectives, local(): lax.psum(qkv_bias_grad.astype(jnp.bfloat16), 'ctx').astype(jnp.float32)  55 us
  transfers between devices with their start and end apart: 43, of which 15 were waited for; matrix products, arithmetic and copies ran while one was open for 41% of the time, Pallas kernels for 0%

commit v1 on v0

v1 whole, which is shorter than its diff:
```python
import functools

import jax
import jax.numpy as jnp
from jax import lax
from jax.experimental import pallas as pl
from jax.experimental.pallas import tpu as pltpu
from jax.sharding import PartitionSpec as P

D = 768
HEADS = 12
HEAD_DIM = 64
FF = 3072
ROTARY = 16

norm_eps = 1e-05
rope_base = 10000.0
inv_sqrt_two = 0.7071067811865476
inv_sqrt_tau = 0.3989422804014327
log2_e = 1.4426950408889634
masked_bias = -1e30
score_scale = HEAD_DIM ** (-0.5)

f32 = jnp.float32
bf16 = jnp.bfloat16
NT = (((1,), (1,)), ((), ()))
NN = (((1,), (0,)), ((), ()))
TN = (((0,), (0,)), ((), ()))


def dot(a, b, dims=NN):
    return lax.dot_general(a, b, dims, preferred_element_type=f32)


def attention_kernel(
    length_ref,
    attn_in_ref,
    cot_ref,
    w_ref,
    bias_ref,
    out_w_ref,
    cos_ref,
    sin_lo_ref,
    sin_hi_ref,
    mixed_ref,
    dproj_ref,
    q_s,
    k_a,
    k_b,
    v_a,
    v_b,
    kt_a,
    kt_b,
    vt_a,
    vt_b,
    do_s,
    dk_s,
    dv_s,
    *,
    seq_len,
    rows,
    groups,
):
    live = length_ref[0]
    lane = lax.broadcasted_iota(jnp.int32, (rows, 128), 1)
    low = lane < HEAD_DIM

    def rope(x, span, back):
        up = pltpu.roll(x, 120, 1) * sin_lo_ref[span, :]
        down = pltpu.roll(x, 8, 1) * sin_hi_ref[span, :]
        turned = x * cos_ref[span, :]
        return turned - up - down if back else turned + up + down

    def project(j, carry):
        start = pl.multiple_of(j * rows, rows)
        span = pl.ds(start, rows)
        proj = dot(attn_in_ref[span, :], w_ref[...]) + bias_ref[...]
        q_s[span, :] = (rope(proj[:, :128], span, False) * (score_scale * log2_e)).astype(bf16)
        keys = rope(proj[:, 128:256], span, False)
        values = proj[:, 256:]
        key_pos = start + lax.broadcasted_iota(jnp.int32, (rows, 128), 0)
        dead = jnp.where(key_pos < live, 0.0, masked_bias)
        ka = jnp.where(low, keys, jnp.where(lane == HEAD_DIM, dead, 0.0))
        kb = jnp.where(low, jnp.where(lane == 0, dead, 0.0), keys)
        va = jnp.where(low, values, 1.0)
        vb = jnp.where(low, 1.0, values)
        for src, plain, turned in (
            (ka, k_a, kt_a),
            (kb, k_b, kt_b),
            (va, v_a, vt_a),
            (vb, v_b, vt_b),
        ):
            plain[span, :] = src.astype(bf16)
            turned[:, span] = src.T.astype(bf16)
        do_s[span, :] = dot(cot_ref[span, :], out_w_ref[...], NT)
        return carry

    lax.fori_loop(0, seq_len // rows, project, 0)

    def attend(q0, nk, group_keys, first):
        q_span = pl.ds(q0, rows)
        queries = q_s[q_span, :].astype(f32)
        zero = jnp.zeros_like(queries)
        qa = jnp.where(low, queries, zero).astype(bf16)
        qb = jnp.where(low, zero, queries).astype(bf16)
        qa1 = jnp.where(low, queries, jnp.where(lane == HEAD_DIM, 1.0, 0.0)).astype(bf16)
        qb1 = jnp.where(low, jnp.where(lane == 0, 1.0, 0.0), queries).astype(bf16)
        edge = nk - group_keys
        key_pos = edge + lax.broadcasted_iota(jnp.int32, (group_keys, rows), 0)
        query_pos = q0 + lax.broadcasted_iota(jnp.int32, (group_keys, rows), 1)
        causal = key_pos <= query_pos
        probs = []
        mixes = []
        for keys, turned, q1 in ((k_a, vt_a, qa1), (k_b, vt_b, qb1)):
            s_edge = dot(keys[edge:nk, :], q1, NT)
            s_edge = jnp.where(causal, s_edge, masked_bias)
            best = jnp.max(s_edge, 0, keepdims=True)
            if edge:
                s_body = dot(keys[:edge, :], q1, NT)
                best = jnp.maximum(best, jnp.max(s_body, 0, keepdims=True))
                p = jnp.concatenate(
                    [
                        jnp.exp2(s_body - best).astype(bf16),
                        jnp.exp2(s_edge - best).astype(bf16),
                    ],
                    0,
                )
            else:
                p = jnp.exp2(s_edge - best).astype(bf16)
            probs.append(p)
            mixes.append(dot(turned[:, :nk], p).T)
        unscaled = jnp.where(low, mixes[0], mixes[1])
        denom = pltpu.roll(jnp.where(low, mixes[1], mixes[0]), HEAD_DIM, 1)
        inv = 1.0 / denom
        out = unscaled * inv
        mixed_ref[q_span, :] = out.astype(bf16)
        grad = (do_s[q_span, :] * inv).astype(bf16)
        grad_f = grad.astype(f32)
        prod = grad_f * out
        da = jnp.sum(jnp.where(low, prod, 0.0), 1, keepdims=True)
        db = jnp.sum(jnp.where(low, 0.0, prod), 1, keepdims=True)
        da_hi = da.astype(bf16).astype(f32)
        db_hi = db.astype(bf16).astype(f32)
        ga = jnp.where(low, grad_f, 0.0)
        gb = jnp.where(low, 0.0, grad_f)
        ga1 = jnp.where(
            lane == HEAD_DIM, -da_hi, jnp.where(lane == HEAD_DIM + 1, da_hi - da, ga)
        ).astype(bf16)
        gb1 = jnp.where(lane == 0, -db_hi, jnp.where(lane == 1, db_hi - db, gb)).astype(bf16)
        ga = ga.astype(bf16)
        gb = gb.astype(bf16)
        grad_scores = []
        for p, values, g1 in zip(probs, (v_a, v_b), (ga1, gb1)):
            dp = dot(values[:nk, :], g1, NT)
            grad_scores.append((p.astype(f32) * dp).astype(bf16))
        dq = dot(kt_a[:, :nk], grad_scores[0]) + dot(kt_b[:, :nk], grad_scores[1])
        dproj_ref[q_span, :128] = rope(dq.T * score_scale, q_span, True).astype(bf16)
        dk = dot(jnp.concatenate(grad_scores, 1), jnp.concatenate([qa, qb], 0))
        dv = dot(jnp.concatenate(probs, 1), jnp.concatenate([ga, gb], 0))
        if first:
            dk_s[:nk, :] = dk
            dv_s[:nk, :] = dv
        else:
            dk_s[:nk, :] += dk
            dv_s[:nk, :] += dv

    group_keys = seq_len // groups
    per_group = group_keys // rows
    for g in reversed(range(groups)):
        nk = (g + 1) * group_keys
        if g == groups - 1 and per_group > 1:
            dk_s[...] = jnp.zeros_like(dk_s)
            dv_s[...] = jnp.zeros_like(dv_s)
        first = g == groups - 1 and per_group == 1
        if per_group == 1:
            attend(g * group_keys, nk, group_keys, first)
        else:

            def step(j, carry, g=g, nk=nk):
                q0 = pl.multiple_of(g * group_keys + j * rows, rows)
                attend(q0, nk, group_keys, False)
                return carry

            lax.fori_loop(0, per_group, step, 0)

    def finish(j, carry):
        span = pl.ds(pl.multiple_of(j * rows, rows), rows)
        dproj_ref[span, 128:256] = rope(dk_s[span, :] * (1.0 / log2_e), span, True).astype(bf16)
        dproj_ref[span, 256:] = dv_s[span, :].astype(bf16)
        return carry

    lax.fori_loop(0, seq_len // rows, finish, 0)


def attention(length, attn_in, cot, w, bias, out_w, cos, sin_lo, sin_hi):
    seq_len = attn_in.shape[0]
    pairs = w.shape[1] // 384
    rows = 256
    groups = 6
    whole = functools.partial(pl.BlockSpec, pipeline_mode=pl.Buffered(1))
    small = pltpu.VMEM((seq_len, 128), bf16)
    turned = pltpu.VMEM((128, seq_len), bf16)
    wide = pltpu.VMEM((seq_len, 128), f32)
    flops = pairs * seq_len * (2 * D * 512 + 12 * 128 * seq_len)
    return pl.pallas_call(
        functools.partial(attention_kernel, seq_len=seq_len, rows=rows, groups=groups),
        grid=(pairs,),
        in_specs=[
            pl.BlockSpec(memory_space=pltpu.SMEM),
            whole((seq_len, D), lambda p: (0, 0)),
            whole((seq_len, D), lambda p: (0, 0)),
            pl.BlockSpec((D, 384), lambda p: (0, p)),
            pl.BlockSpec((1, 384), lambda p: (0, p)),
            pl.BlockSpec((128, D), lambda p: (p, 0)),
            whole((seq_len, 128), lambda p: (0, 0)),
            whole((seq_len, 128), lambda p: (0, 0)),
            whole((seq_len, 128), lambda p: (0, 0)),
        ],
        out_specs=[
            pl.BlockSpec((seq_len, 128), lambda p: (0, p)),
            pl.BlockSpec((seq_len, 384), lambda p: (0, p)),
        ],
        out_shape=[
            jax.ShapeDtypeStruct((seq_len, pairs * 128), bf16),
            jax.ShapeDtypeStruct((seq_len, pairs * 384), bf16),
        ],
        scratch_shapes=[small] * 5 + [turned] * 4 + [wide] * 3,
        compiler_params=pltpu.CompilerParams(vmem_limit_bytes=58 * 1024 * 1024),
        cost_estimate=pl.CostEstimate(
            flops=flops, bytes_accessed=12_000_000, transcendentals=pairs * seq_len * seq_len
        ),
        name="attention",
    )(length, attn_in, cot, w, bias, out_w, cos, sin_lo, sin_hi)


def swap(x, axis, by):
    n = lax.axis_size(axis)
    return lax.ppermute(x, axis, [(j, j ^ by) for j in range(n)])


def place(out, piece, at, axis=0):
    return lax.dynamic_update_slice_in_dim(out, piece, at * piece.shape[axis], axis)


def take(x, at, size, axis=0):
    return lax.dynamic_slice_in_dim(x, at * size, size, axis)


def gather(x, axis, me, n, step=1, dim=0):
    shape = list(x.shape)
    shape[dim] *= n
    out = place(jnp.zeros(shape, x.dtype), x, me, dim)
    for s in range(1, n):
        out = place(out, swap(x, axis, s * step), me ^ s, dim)
    return out


def scatter_sum(x, axis, me, n, step=1, dim=0):
    size = x.shape[dim] // n
    total = take(x, me, size, dim).astype(f32)
    for s in range(1, n):
        part = take(x, me ^ s, size, dim).astype(bf16)
        total = total + swap(part, axis, s * step).astype(f32)
    return total


def exchange(x, axis, me, n, step=1):
    out = place(jnp.zeros_like(x), take(x, me, 1), me)
    for s in range(1, n):
        out = place(out, swap(take(x, me ^ s, 1), axis, s * step), me ^ s)
    return out


def rope_tables(seq_len):
    half = ROTARY // 2
    frequency = rope_base ** (-2.0 * jnp.arange(half, dtype=f32) / ROTARY)
    angles = jnp.arange(seq_len, dtype=jnp.int32).astype(f32)[:, None] * frequency[None, :]
    cosine, sine = jnp.cos(angles), jnp.sin(angles)
    rest = jnp.zeros((seq_len, HEAD_DIM - ROTARY), f32)
    none = jnp.zeros((seq_len, half), f32)
    cos = jnp.concatenate([cosine, cosine, rest + 1.0] * 2, 1)
    sin_lo = jnp.concatenate([-sine, none, rest] * 2, 1)
    sin_hi = jnp.concatenate([none, sine, rest] * 2, 1)
    return cos, sin_lo, sin_hi


def local(
    tokens,
    lengths,
    cotangent,
    qkv_weight,
    qkv_bias,
    out_weight,
    out_bias,
    up_weight,
    up_bias,
    down_weight,
    down_bias,
    attn_gain,
    attn_shift,
    mlp_gain,
    mlp_shift,
):
    seqs, width = tokens.shape[0], tokens.shape[1]
    ctx_size, fsdp = lax.axis_size("ctx"), lax.axis_size("fsdp")
    team = ctx_size // seqs
    here = lax.axis_index("ctx")
    seat, seq = here % team, here // team
    shard = lax.axis_index("fsdp")
    seq_len = ctx_size * width
    heads = HEADS // team
    pairs = (heads + 1) // 2
    lanes = heads * HEAD_DIM
    spare = pairs * 128 - lanes

    def by_pair(x):
        rows = x.shape[0]
        x = take(x.reshape(rows, 3, D), seat, lanes, 2)
        x = jnp.pad(x, ((0, 0), (0, 0), (0, spare)))
        return jnp.concatenate(
            [x[:, t, p * 128 : (p + 1) * 128] for p in range(pairs) for t in range(3)], 1
        )

    def from_pair(x):
        rows = x.shape[0]
        parts = []
        for t in range(3):
            parts.append(
                jnp.concatenate(
                    [x[:, p * 384 + t * 128 : p * 384 + (t + 1) * 128] for p in range(pairs)], 1
                )[:, None, :lanes]
            )
        return jnp.concatenate(parts, 1).reshape(rows, 3, lanes)

    unit = FF // (fsdp * team)

    def up_columns(x):
        return jnp.concatenate(
            [take(x[:, j * unit * team : (j + 1) * unit * team], seat, unit, 1) for j in range(fsdp)],
            1,
        )

    tok_half = exchange(tokens, "ctx", seq, seqs, team)
    cot_half = exchange(cotangent, "ctx", seq, seqs, team)

    def join(half):
        return gather(half[:, None], "ctx", seat, team, 1, 1).reshape(seq_len, D)

    rows_in = join(tok_half)
    cot = join(cot_half)

    vectors = jnp.concatenate(
        [qkv_bias, out_bias, up_bias, down_bias, attn_gain, attn_shift, mlp_gain, mlp_shift]
    )[None]
    vectors = gather(vectors, "fsdp", shard, fsdp)
    bounds = []
    at = 0
    for v in (qkv_bias, out_bias, up_bias, down_bias, attn_gain, attn_shift, mlp_gain, mlp_shift):
        bounds.append(vectors[:, at : at + v.shape[0]].reshape(-1).astype(f32))
        at += v.shape[0]
    full_qkv_b, full_out_b, full_up_b, full_down_b, gain_a, shift_a, gain_m, shift_m = bounds
    w_up = gather(up_columns(up_weight), "fsdp", shard, fsdp)
    w_down = gather(take(down_weight, seat, unit), "fsdp", shard, fsdp)
    w_qkv = gather(by_pair(qkv_weight), "fsdp", shard, fsdp)
    w_out = gather(out_weight, "fsdp", shard, fsdp)
    w_out_rows = take(w_out, seat, lanes)
    w_out_rows = jnp.pad(w_out_rows, ((0, spare), (0, 0)))
    b_qkv = by_pair(full_qkv_b[None])
    b_up = up_columns(full_up_b[None])

    def normalise(x):
        x = x.astype(f32)
        center = x - jnp.mean(x, -1, keepdims=True)
        inv = lax.rsqrt(jnp.mean(center * center, -1, keepdims=True) + norm_eps)
        return center * inv, inv

    normed, _ = normalise(rows_in)
    attn_in = (normed * gain_a + shift_a).astype(bf16)
    mlp_in = (normed * gain_m + shift_m).astype(bf16)

    pre_act = dot(mlp_in, w_up) + b_up
    cdf = 0.5 * (1.0 + lax.erf(pre_act * inv_sqrt_two))
    hidden = (pre_act * cdf).astype(bf16)
    slope = cdf + pre_act * jnp.exp(-0.5 * pre_act * pre_act) * inv_sqrt_tau
    grad_pre = (dot(cot, w_down, NT) * slope).astype(bf16)
    down_grad = dot(hidden, cot, TN)
    up_grad = dot(mlp_in, grad_pre, TN)
    mlp_out = dot(hidden, w_down)
    grad_mlp_in = dot(grad_pre, w_up, NT)

    length = lax.dynamic_slice_in_dim(lengths, seq, 1, 0)
    mixed, grad_proj = attention(
        length, attn_in, cot, w_qkv, b_qkv, w_out_rows, *rope_tables(seq_len)
    )
    delta_out = mlp_out + dot(mixed, w_out_rows)
    mixed_all = gather(mixed[:, :lanes], "ctx", seat, team, 1, 1)
    out_cols = D // team
    out_grad = dot(mixed_all, take(cot, seat, out_cols, 1), TN)
    qkv_grad = dot(attn_in, grad_proj, TN)
    grad_attn_in = dot(grad_proj, w_qkv, NT)

    def home(x):
        blocks = x.reshape(seqs, team, width, D)
        return scatter_sum(blocks, "ctx", seat, team, 1, 1).reshape(seqs, width, D)

    delta_home = exchange(home(delta_out).astype(bf16), "ctx", seq, seqs, team)
    layer_out = (tokens.astype(f32) + delta_home.astype(f32) + full_out_b + full_down_b).astype(
        bf16
    )

    grad_normed = home(grad_attn_in * gain_a + grad_mlp_in * gain_m)
    normed_half, inv_half = normalise(tok_half)
    delta_in = inv_half * (
        grad_normed
        - jnp.mean(grad_normed, -1, keepdims=True)
        - normed_half * jnp.mean(grad_normed * normed_half, -1, keepdims=True)
    )
    delta_in = exchange(delta_in.astype(bf16), "ctx", seq, seqs, team)
    tokens_grad = cotangent.astype(f32) + delta_in.astype(f32)

    qkv_b_grad = from_pair(jnp.sum(grad_proj.astype(f32), 0)[None])
    qkv_b_grad = place(jnp.zeros((3, D), f32), qkv_b_grad[0], seat, 1)
    up_b_grad = jnp.sum(grad_pre.astype(f32), 0).reshape(fsdp, unit)
    up_b_grad = place(jnp.zeros((fsdp, unit * team), f32), up_b_grad, seat, 1)
    cot_sum = jnp.sum(cot.astype(f32), 0) * (1.0 / team)
    sums = [
        qkv_b_grad.reshape(-1),
        cot_sum,
        up_b_grad.reshape(-1),
        jnp.sum(grad_attn_in * normed, 0),
        jnp.sum(grad_attn_in, 0),
        jnp.sum(grad_mlp_in * normed, 0),
        jnp.sum(grad_mlp_in, 0),
    ]
    total = lax.psum(jnp.concatenate(sums).reshape(-1, 128), ("ctx", "fsdp")).reshape(-1)
    vec = []
    at = 0
    for v in sums:
        size = v.shape[0] // fsdp
        vec.append(lax.dynamic_slice_in_dim(total[at : at + v.shape[0]], shard * size, size, 0))
        at += v.shape[0]

    def reduce(x):
        mine = scatter_sum(x, "fsdp", shard, fsdp)
        part = scatter_sum(mine, "ctx", seq, seqs, team).astype(bf16)
        return gather(part, "ctx", seq, seqs, team)

    up_mine = reduce(up_grad).reshape(D // fsdp, fsdp, 1, unit)
    up_mine = gather(up_mine, "ctx", seat, team, 1, 2).reshape(D // fsdp, FF).astype(f32)
    down_mine = gather(reduce(down_grad), "ctx", seat, team).astype(f32)
    qkv_mine = from_pair(reduce(qkv_grad))
    qkv_mine = gather(qkv_mine, "ctx", seat, team, 1, 2).reshape(D // fsdp, 3 * D).astype(f32)
    out_mine = gather(reduce(out_grad), "ctx", seat, team, 1, 1).astype(f32)

    return (
        layer_out,
        tokens_grad,
        qkv_mine,
        vec[0],
        out_mine,
        vec[1],
        up_mine,
        vec[2],
        down_mine,
        vec[1],
        vec[3],
        vec[4],
        vec[5],
        vec[6],
    )


def solution(mesh):
    rows, whole = P("fsdp", "ctx", None), P("fsdp", None)
    vector = P("fsdp")
    in_specs = (
        rows,
        vector,
        rows,
        whole,
        vector,
        whole,
        vector,
        whole,
        vector,
        whole,
        vector,
        vector,
        vector,
        vector,
        vector,
    )
    out_specs = (
        rows,
        rows,
        whole,
        vector,
        whole,
        vector,
        whole,
        vector,
        whole,
        vector,
        vector,
        vector,
        vector,
        vector,
    )
    return jax.shard_map(local, mesh=mesh, in_specs=in_specs, out_specs=out_specs, check_vma=False)
```

time: 1610 us -> 634 us (0.39)
  matrix products: 363 us -> 62 us
  waiting for transfers between devices: 449 us -> 190 us
  starting transfers between devices: 356 us -> 108 us
  other arithmetic: 142 us -> 29.8 us
  Pallas kernels: 0 us -> 59.8 us
  blocking collectives: 96.9 us -> 37.3 us
  local copies, waits for them, and re-layouts: 166 us -> 135 us
    all_gather x6 -> x0, waiting for transfers between devices: 336 us -> none  [the longest x1 141 us: local(): values_piece = lax.all_gather(values_own, 'ctx', axis=1, tiled=True)]
    dot_general x68 -> x10, matrix products: 363 us -> 62 us  [dot(): return lax.dot_general(a, b, dims, preferred_element_type=f32)]
    ppermute x32 -> x72, starting transfers between devices: 345 us -> 108 us  [swap(): return lax.ppermute(x, axis, [(j, j ^ by) for j in range(n)])]
    ppermute x32 -> x72, waiting for transfers between devices: 38.4 us -> 190 us  [swap(): return lax.ppermute(x, axis, [(j, j ^ by) for j in range(n)])]
    psum x1 -> x0, waiting for transfers between devices: 72 us -> none  [local(): lax.psum(qkv_grad.astype(jnp.bfloat16), 'ctx').astype(jnp.float32)]
    dynamic_update_slice x0 -> x60, local copies, waits for them, and re-layouts: none -> 67.8 us  [place(): lax.dynamic_update_slice_in_dim(out, piece, at * piece.shape[axis], axis)]
    unnamed x129 -> x150, local copies, waits for them, and re-layouts: 69.2 us -> 4.26 us
    pallas_call x0 -> x1, Pallas kernels: none -> 59.8 us  [attention(): pl.pallas_call(functools.partial(attention_kernel, seq_len=seq_len, rows=...]
  transfers between devices with their start and end apart: 43 -> 72, of which waited for: 15 -> 32; matrix products, arithmetic and copies ran while one was open for 41% -> 24% of each run, Pallas kernels for 0% -> 0%
where the time goes in v1:
time: 634 us; the launch traced here: 625 us
  waiting for transfers between devices  190 us (30%)
  local copies, waits for them, and re-layouts  135 us (21%)
  starting transfers between devices  108 us (17%)
  matrix products  62 us (10%)
  Pallas kernels  59.8 us (9%)
  blocking collectives  37.3 us (6%)
  other arithmetic  29.8 us (5%)
    ppermute x72, waiting for transfers between devices, swap(): return lax.ppermute(x, axis, [(j, j ^ by) for j in range(n)])  190 us
    ppermute x72, starting transfers between devices, swap(): return lax.ppermute(x, axis, [(j, j ^ by) for j in range(n)])  108 us
    dynamic_update_slice x60, local copies, waits for them, and re-layouts, place(): lax.dynamic_update_slice_in_dim(out, piece, at * piece.shape[axis], axis)  67.8 us
    dot_general x10, matrix products, dot(): return lax.dot_general(a, b, dims, preferred_element_type=f32)  62 us
    pallas_call x1, Pallas kernels, attention(): pl.pallas_call(functools.partial(attention_kernel, seq_len=seq_len, rows=...  59.8 us
    psum x1, blocking collectives, local(): lax.psum(jnp.concatenate(sums).reshape(-1, 128), ('ctx', 'fsdp'))  37.3 us
  transfers between devices with their start and end apart: 72, of which 32 were waited for; matrix products, arithmetic and copies ran while one was open for 24% of the time, Pallas kernels for 0%

profile of v1, /device:TPU:0, one launch (start us, length us, event | category | flops | bytes accessed | tf_op | source)
XLA Modules:
  0.0 624.9 jit_solution(2140169782038606699)
XLA Ops:
  0.7 5.6 concatenate.51
  6.3 3.0 collective-permute-start.4
  28.6 4.3 multiply_sine_fusion
  36.2 3.7 concatenate.57.sin_lo_ref
  39.9 3.8 concatenate.58.sin_hi_ref
  63.8 7.4 %collective-permute-done.14 = bf16[1,192,768]{2,1,0:T(8,128)(2,1)S(1)} collective-permute-done((bf16[1,192,768]{2,1,0:T(8,128)(2,1)S(1)}, bf16[1,192,768]{2,1,0:T(8,128)(2,1)S(1)}, u32[]{:S(2)}, u32[]{:S(2)}) %collective-permute-start.14) | collective-permute-done | bytes 294944 | tf_op jit(solution)/shard_map/ppermute | solution.py:238
  72.4 6.1 collective-permute-start.1
  80.1 3.1 collective-permute-start.2
  84.9 14.1 %collective-permute-done.1 = bf16[1,192,768]{2,1,0:T(8,128)(2,1)S(1)} collective-permute-done((bf16[1,192,768]{2,1,0:T(8,128)(2,1)}, bf16[1,192,768]{2,1,0:T(8,128)(2,1)S(1)}, u32[]{:S(2)}, u32[]{:S(2)}) %collective-permute-start.1) | collective-permute-done | bytes 294944 | tf_op jit(solution)/shard_map/ppermute | solution.py:238
  101.3 7.1 %collective-permute-done.20 = bf16[192,768]{1,0:T(8,128)(2,1)S(1)} collective-permute-done((bf16[192,768]{1,0:T(8,128)(2,1)S(1)}, bf16[192,768]{1,0:T(8,128)(2,1)S(1)}, u32[]{:S(2)}, u32[]{:S(2)}) %collective-permute-start.20) | collective-permute-done | bytes 294944 | tf_op jit(solution)/shard_map/ppermute | solution.py:238
  110.7 6.5 %collective-permute-done.21 = bf16[192,768]{1,0:T(8,128)(2,1)S(1)} collective-permute-done((bf16[192,768]{1,0:T(8,128)(2,1)S(1)}, bf16[192,768]{1,0:T(8,128)(2,1)S(1)}, u32[]{:S(2)}, u32[]{:S(2)}) %collective-permute-start.21) | collective-permute-done | bytes 294944 | tf_op jit(solution)/shard_map/ppermute | solution.py:238
  120.7 5.2 collective-permute-done.22
  132.6 3.7 collective-permute-done.18
  138.0 7.6 %collective-permute-done.19 = bf16[192,1152]{1,0:T(8,128)(2,1)S(1)} collective-permute-done((bf16[192,1152]{1,0:T(8,128)(2,1)S(1)}, bf16[192,1152]{1,0:T(8,128)(2,1)S(1)}, u32[]{:S(2)}, u32[]{:S(2)}) %collective-permute-start.19) | collective-permute-done | bytes 442400 | tf_op jit(solution)/shard_map/ppermute | solution.py:238
  155.4 18.8 %collective-permute-done.8 = bf16[192,1536]{1,0:T(8,128)(2,1)S(1)} collective-permute-done((bf16[192,1536]{1,0:T(8,128)(2,1)S(1)}, bf16[192,1536]{1,0:T(8,128)(2,1)S(1)}, u32[]{:S(2)}, u32[]{:S(2)}) %collective-permute-start.8) | collective-permute-done | bytes 589856 | tf_op jit(solution)/shard_map/ppermute | solution.py:238
  186.3 59.8 %attention.1 = (bf16[1536,384]{1,0:T(8,128)(2,1)}, bf16[1536,1152]{1,0:T(8,128)(2,1)}) custom-call(s32[1]{0:T(128)} %dynamic_slice.240.length_ref, bf16[1536,768]{1,0:T(8,128)(2,1)} %get-tuple-element.45.attn_in_ref, bf16[1536,768]{1,0:T(8,128)(2,1)} %bitcast.188, bf16[768,1152]{1,0:T(8,128)(2,1)} %copy-done.19, f32[1,1152]{1,0:T(1,128)} %copy-done.52, ...), custom_call_target="tpu_custom_call" | custom-call | flops 14495514624 | bytes 12000000 | tf_op jit(solution)/shard_map/attention/pallas_call | solution.py:205
  249.2 6.4 %fusion.45 = f32[1536,768]{1,0:T(8,128)} fusion(bf16[1536,1152]{1,0:T(8,128)(2,1)S(1)} %copy-done.12, bf16[768,1152]{1,0:T(8,128)(2,1)} %copy-done.19), kind=kOutput, calls=%fused_computation.265 | convolution fusion | flops 2717908992 | bytes 10027008 | tf_op jit(solution)/shard_map/dot_general | solution.py:32
  255.6 8.0 %multiply_convert_fusion = (bf16[1536,1536]{1,0:T(8,128)(2,1)}, f32[1536,1536]{1,0:T(8,128)S(1)}) fusion(f32[1536]{0:T(1024)S(1)} %copy-done.50, bf16[1536,768]{1,0:T(8,128)(2,1)S(1)} %get-tuple-element.44, bf16[768,1536]{1,0:T(8,128)(2,1)} %constant_dynamic-update-slice_fusion.54), kind=kOutput, calls=%fused_computation.7 | convolution fusion | flops 3638034432 | bytes 18880512 | tf_op jit(solution)/shard_map/dot_general | solution.py:32
  263.6 9.9 %convert_reduce_fusion = (f32[1536]{0:T(1024)}, bf16[1536,1536]{1,0:T(8,128)(2,1)S(1)}) fusion(f32[1536,1536]{1,0:T(8,128)S(1)} %get-tuple-element.127, bf16[1536,768]{1,0:T(8,128)(2,1)S(1)} %bitcast.189, bf16[1536,768]{1,0:T(8,128)(2,1)} %constant_dynamic-update-slice_fusion.50), kind=kOutput, calls=%fused_computation.6 | convolution fusion | flops 3652188672 | bytes 18880512 | tf_op jit(solution)/shard_map/dot_general | solution.py:32
  273.6 5.6 fusion.47
  286.2 9.8 %fusion.38 = (f32[768]{0:T(1024)S(1)}, f32[768]{0:T(1024)S(1)}, f32[1536,768]{1,0:T(8,128)}, f32[768]{0:T(1024)S(1)}, f32[768]{0:T(1024)S(1)}) fusion(f32[1536]{0:T(1024)} %rsqrt.20, f32[1536]{0:T(1024)S(1)} %copy-done.40, bf16[4,2,192,768]{3,2,1,0:T(8,128)(2,1)S(1)} %bitcast_dynamic-update-slice_fusion.1, f32[768]{0:T(1024)} %reshape.235, ...), kind=kOutput, calls=%fused_computation.258 | convolution fusion | flops 3638031360 | bytes 18905088 | tf_op jit(solution)/shard_map/dot_general | solution.py:32
  296.7 37.3 %psum.7 = f32[72,128]{1,0:T(8,128)S(1)} all-reduce(f32[72,128]{1,0:T(8,128)} %bitcast.201), channel_id=1, replica_groups=mesh['ctx'=8,'fsdp'=4] {'ctx','fsdp'}, use_global_device_ids=true, to_apply=%region_13.14 | all-reduce | flops 9216 | bytes 73728 | tf_op jit(solution)/shard_map/psum | solution.py:435
  334.0 6.1 fusion.46
  340.2 6.3 %fusion.48 = f32[1536,768]{1,0:T(8,128)S(1)} fusion(bf16[1536,1536]{1,0:T(8,128)(2,1)} %get-tuple-element.126, bf16[1536,768]{1,0:T(8,128)(2,1)S(1)} %bitcast.190), kind=kOutput, calls=%fused_computation.268 | convolution fusion | flops 3623878656 | bytes 11796480 | tf_op jit(solution)/shard_map/dot_general | solution.py:32
  354.1 5.5 convolution_add_fusion.1
  366.3 6.4 %collective-permute-done.31 = bf16[192,1152]{1,0:T(8,128)(2,1)S(1)} collective-permute-done((bf16[192,1152]{1,0:T(8,128)(2,1)S(1)}, bf16[192,1152]{1,0:T(8,128)(2,1)S(1)}, u32[]{:S(2)}, u32[]{:S(2)}) %collective-permute-start.31) | collective-permute-done | bytes 442400 | tf_op jit(solution)/shard_map/ppermute | solution.py:238
  375.7 8.2 %collective-permute-done.33 = bf16[192,1152]{1,0:T(8,128)(2,1)S(1)} collective-permute-done((bf16[192,1152]{1,0:T(8,128)(2,1)S(1)}, bf16[192,1152]{1,0:T(8,128)(2,1)S(1)}, u32[]{:S(2)}, u32[]{:S(2)}) %collective-permute-start.33) | collective-permute-done | bytes 442400 | tf_op jit(solution)/shard_map/ppermute | solution.py:238
  393.4 4.0 collective-permute-done.35
  402.0 12.1 %collective-permute-done.62 = bf16[384,768]{1,0:T(8,128)(2,1)S(1)} collective-permute-done((bf16[384,768]{1,0:T(8,128)(2,1)S(1)}, bf16[384,768]{1,0:T(8,128)(2,1)S(1)}, u32[]{:S(2)}, u32[]{:S(2)}) %collective-permute-start.62) | collective-permute-done | bytes 589856 | tf_op jit(solution)/shard_map/ppermute | solution.py:238
  415.3 10.6 %collective-permute-done.63 = bf16[384,768]{1,0:T(8,128)(2,1)S(1)} collective-permute-done((bf16[384,768]{1,0:T(8,128)(2,1)S(1)}, bf16[384,768]{1,0:T(8,128)(2,1)S(1)}, u32[]{:S(2)}, u32[]{:S(2)}) %collective-permute-start.63) | collective-permute-done | bytes 589856 | tf_op jit(solution)/shard_map/ppermute | solution.py:238
  429.8 5.4 collective-permute-done.38
  440.3 6.8 %collective-permute-start.65 = (bf16[96,768]{1,0:T(8,128)(2,1)S(1)}, bf16[96,768]{1,0:T(8,128)(2,1)S(1)}, u32[]{:S(2)}, u32[]{:S(2)}) collective-permute-start(bf16[96,768]{1,0:T(8,128)(2,1)S(1)} %get-tuple-element.46), channel_id=1, source_target_pairs={{0,8},{4,12},{8,0},{12,4},{16,24},{20,28},{24,16},{28,20},{1,9},{5... | collective-permute-start | bytes 442376 | tf_op jit(solution)/shard_map/ppermute | solution.py:238
  447.1 3.0 collective-permute-done.56
  453.7 5.2 collective-permute-done.66
  458.9 3.0 collective-permute-start.59
  463.5 4.4 collective-permute-done.58
  483.3 3.6 collective-permute-done.60
  490.1 3.3 copy.52
  495.0 19.5 %dynamic_update_slice.268 = bf16[192,4,2,384]{3,2,1,0:T(2,128)(2,1)} dynamic-update-slice(bf16[192,4,2,384]{3,2,1,0:T(2,128)(2,1)} %broadcast_in_dim.122, bf16[192,4,1,384]{3,2,1,0:T(2,128)(2,1)} %copy.52, s32[]{:T(128)} %constant.38.clone.1, s32[]{:T(128)} %constant.38.clone.1, s32[]{:T(128)S(6)} %select_n.77, s32[]{:T(128)} %constant.38.clone.1) | dynamic-update-slice | bytes 1179652 | tf_op jit(solution)/shard_map/dynamic_update_slice | solution.py:242
  521.7 3.1 fusion.15
  527.6 4.4 collective-permute-start.43
  536.3 4.6 collective-permute-done.44
  550.1 10.5 %collective-permute-done.48 = bf16[48,384]{1,0:T(8,128)(2,1)S(1)} collective-permute-done((bf16[48,384]{1,0:T(8,128)(2,1)S(1)}, bf16[48,384]{1,0:T(8,128)(2,1)S(1)}, u32[]{:S(2)}, u32[]{:S(2)}) %collective-permute-start.48) | collective-permute-done | bytes 36896 | tf_op jit(solution)/shard_map/ppermute | solution.py:238
  561.7 4.5 collective-permute-done.49
  568.1 3.9 collective-permute-done.50
  576.7 7.2 %collective-permute-done.30 = bf16[1,192,768]{2,1,0:T(8,128)(2,1)S(1)} collective-permute-done((bf16[1,192,768]{2,1,0:T(8,128)(2,1)S(1)}, bf16[1,192,768]{2,1,0:T(8,128)(2,1)S(1)}, u32[]{:S(2)}, u32[]{:S(2)}) %collective-permute-start.30) | collective-permute-done | bytes 294944 | tf_op jit(solution)/shard_map/ppermute | solution.py:238
  589.5 14.6 %collective-permute-done.25 = bf16[1,192,768]{2,1,0:T(8,128)(2,1)S(1)} collective-permute-done((bf16[1,192,768]{2,1,0:T(8,128)(2,1)S(1)}, bf16[1,192,768]{2,1,0:T(8,128)(2,1)S(1)}, u32[]{:S(2)}, u32[]{:S(2)}) %collective-permute-start.25) | collective-permute-done | bytes 294944 | tf_op jit(solution)/shard_map/ppermute | solution.py:238
  609.6 11.8 %dynamic_update_slice.269 = bf16[192,4,2,384]{3,2,1,0:T(2,128)(2,1)S(1)} dynamic-update-slice(bf16[192,4,2,384]{3,2,1,0:T(2,128)(2,1)S(1)} %copy-done.7, bf16[192,4,1,384]{3,2,1,0:T(2,128)(2,1)S(1)} %copy.53, s32[]{:T(128)} %constant.38.clone.1, s32[]{:T(128)} %constant.38.clone.1, s32[]{:T(128)S(6)} %select_n.78, s32[]{:T(128)} %constant.38.clone.1) | dynamic-update-slice | bytes 1179652 | tf_op jit(solution)/shard_map/dynamic_update_slice | solution.py:242
  (453 shorter events, 207.8 us)
Async XLA Ops:
  6.3 40.1 %collective-permute-start.4 = (bf16[1,2496]{1,0:T(2,128)(2,1)S(1)}, bf16[1,2496]{1,0:T(2,128)(2,1)}, u32[]{:S(2)}, u32[]{:S(2)}) collective-permute-start(bf16[1,2496]{1,0:T(2,128)(2,1)S(1)} %broadcast_in_dim.99), channel_id=1, source_target_pairs={{0,1},{1,0},{2,3},{3,2},{4,5},{5,4},{6,7},{7,6},{8,9},{9,8},{10,11... | collective-permute-start | bytes 14984 | tf_op jit(solution)/shard_map/ppermute | solution.py:238
  9.3 37.9 %collective-permute-start.5 = (bf16[1,2496]{1,0:T(2,128)(2,1)S(1)}, bf16[1,2496]{1,0:T(2,128)(2,1)}, u32[]{:S(2)}, u32[]{:S(2)}) collective-permute-start(bf16[1,2496]{1,0:T(2,128)(2,1)S(1)} %broadcast_in_dim.99), channel_id=1, source_target_pairs={{0,2},{1,3},{2,0},{3,1},{4,6},{5,7},{6,4},{7,5},{8,10},{9,11},{10,... | collective-permute-start | bytes 14984 | tf_op jit(solution)/shard_map/ppermute | solution.py:238
  10.8 39.3 %collective-permute-start.6 = (bf16[1,2496]{1,0:T(2,128)(2,1)S(1)}, bf16[1,2496]{1,0:T(2,128)(2,1)}, u32[]{:S(2)}, u32[]{:S(2)}) collective-permute-start(bf16[1,2496]{1,0:T(2,128)(2,1)S(1)} %broadcast_in_dim.99), channel_id=1, source_target_pairs={{0,3},{1,2},{2,1},{3,0},{4,7},{5,6},{6,5},{7,4},{8,11},{9,10},{10,... | collective-permute-start | bytes 14984 | tf_op jit(solution)/shard_map/ppermute | solution.py:238
  13.6 132.1 %collective-permute-start.10 = (bf16[384,768]{1,0:T(8,128)(2,1)}, bf16[384,768]{1,0:T(8,128)(2,1)}, u32[]{:S(2)}, u32[]{:S(2)}) collective-permute-start(bf16[384,768]{1,0:T(8,128)(2,1)} %get-tuple-element.31), channel_id=1, source_target_pairs={{0,1},{1,0},{2,3},{3,2},{4,5},{5,4},{6,7},{7,6},{8,9},{9,8},{10,11... | collective-permute-start | bytes 1769480 | tf_op jit(solution)/shard_map/ppermute | solution.py:238
  15.5 132.7 %collective-permute-start.11 = (bf16[384,768]{1,0:T(8,128)(2,1)}, bf16[384,768]{1,0:T(8,128)(2,1)}, u32[]{:S(2)}, u32[]{:S(2)}) collective-permute-start(bf16[384,768]{1,0:T(8,128)(2,1)} %get-tuple-element.31), channel_id=1, source_target_pairs={{0,2},{1,3},{2,0},{3,1},{4,6},{5,7},{6,4},{7,5},{8,10},{9,11},{10,... | collective-permute-start | bytes 1769480 | tf_op jit(solution)/shard_map/ppermute | solution.py:238
  46.4 106.2 %collective-permute-start.12 = (bf16[384,768]{1,0:T(8,128)(2,1)}, bf16[384,768]{1,0:T(8,128)(2,1)}, u32[]{:S(2)}, u32[]{:S(2)}) collective-permute-start(bf16[384,768]{1,0:T(8,128)(2,1)} %get-tuple-element.31), channel_id=1, source_target_pairs={{0,3},{1,2},{2,1},{3,0},{4,7},{5,6},{6,5},{7,4},{8,11},{9,10},{10,... | collective-permute-start | bytes 1769480 | tf_op jit(solution)/shard_map/ppermute | solution.py:238
  47.2 13.1 %collective-permute-start.13 = (bf16[1,192,768]{2,1,0:T(8,128)(2,1)}, bf16[1,192,768]{2,1,0:T(8,128)(2,1)S(1)}, u32[]{:S(2)}, u32[]{:S(2)}) collective-permute-start(bf16[1,192,768]{2,1,0:T(8,128)(2,1)} %get-tuple-element.77), channel_id=1, source_target_pairs={{0,8},{4,12},{8,0},{12,4},{16,24},{20,28},{24,16},{28,20},{1,9},{5... | collective-permute-start | bytes 884744 | tf_op jit(solution)/shard_map/ppermute | solution.py:238
  50.1 21.0 %collective-permute-start.14 = (bf16[1,192,768]{2,1,0:T(8,128)(2,1)S(1)}, bf16[1,192,768]{2,1,0:T(8,128)(2,1)S(1)}, u32[]{:S(2)}, u32[]{:S(2)}) collective-permute-start(bf16[1,192,768]{2,1,0:T(8,128)(2,1)S(1)} %copy-done.33), channel_id=1, source_target_pairs={{0,16},{4,20},{8,24},{12,28},{16,0},{20,4},{24,8},{28,12},{1,17},{... | collective-permute-start | bytes 884744 | tf_op jit(solution)/shard_map/ppermute | solution.py:238
  60.3 12.1 %collective-permute-start.15 = (bf16[1,192,768]{2,1,0:T(8,128)(2,1)S(1)}, bf16[1,192,768]{2,1,0:T(8,128)(2,1)S(1)}, u32[]{:S(2)}, u32[]{:S(2)}) collective-permute-start(bf16[1,192,768]{2,1,0:T(8,128)(2,1)S(1)} %copy-done.32), channel_id=1, source_target_pairs={{0,24},{4,28},{8,16},{12,20},{16,8},{20,12},{24,0},{28,4},{1,25},{... | collective-permute-start | bytes 884744 | tf_op jit(solution)/shard_map/ppermute | solution.py:238
  72.4 26.5 %collective-permute-start.1 = (bf16[1,192,768]{2,1,0:T(8,128)(2,1)}, bf16[1,192,768]{2,1,0:T(8,128)(2,1)S(1)}, u32[]{:S(2)}, u32[]{:S(2)}) collective-permute-start(bf16[1,192,768]{2,1,0:T(8,128)(2,1)} %get-tuple-element.81), channel_id=1, source_target_pairs={{0,16},{4,20},{8,24},{12,28},{16,0},{20,4},{24,8},{28,12},{1,17},{... | collective-permute-start | bytes 884744 | tf_op jit(solution)/shard_map/ppermute | solution.py:238
  80.1 20.3 %collective-permute-start.2 = (bf16[1,192,768]{2,1,0:T(8,128)(2,1)}, bf16[1,192,768]{2,1,0:T(8,128)(2,1)S(1)}, u32[]{:S(2)}, u32[]{:S(2)}) collective-permute-start(bf16[1,192,768]{2,1,0:T(8,128)(2,1)} %get-tuple-element.78), channel_id=1, source_target_pairs={{0,24},{4,28},{8,16},{12,20},{16,8},{20,12},{24,0},{28,4},{1,25},{... | collective-permute-start | bytes 884744 | tf_op jit(solution)/shard_map/ppermute | solution.py:238
  100.5 31.2 %collective-permute-start.17 = (bf16[192,1152]{1,0:T(8,128)(2,1)S(1)}, bf16[192,1152]{1,0:T(8,128)(2,1)S(1)}, u32[]{:S(2)}, u32[]{:S(2)}) collective-permute-start(bf16[192,1152]{1,0:T(8,128)(2,1)S(1)} %copy-done.25), channel_id=1, source_target_pairs={{0,1},{1,0},{2,3},{3,2},{4,5},{5,4},{6,7},{7,6},{8,9},{9,8},{10,11... | collective-permute-start | bytes 1327112 | tf_op jit(solution)/shard_map/ppermute | solution.py:238
  131.7 14.0 %collective-permute-start.19 = (bf16[192,1152]{1,0:T(8,128)(2,1)S(1)}, bf16[192,1152]{1,0:T(8,128)(2,1)S(1)}, u32[]{:S(2)}, u32[]{:S(2)}) collective-permute-start(bf16[192,1152]{1,0:T(8,128)(2,1)S(1)} %copy-done.25), channel_id=1, source_target_pairs={{0,3},{1,2},{2,1},{3,0},{4,7},{5,6},{6,5},{7,4},{8,11},{9,10},{10,... | collective-permute-start | bytes 1327112 | tf_op jit(solution)/shard_map/ppermute | solution.py:238
  136.3 18.2 %collective-permute-start.7 = (bf16[192,1536]{1,0:T(8,128)(2,1)S(1)}, bf16[192,1536]{1,0:T(8,128)(2,1)S(1)}, u32[]{:S(2)}, u32[]{:S(2)}) collective-permute-start(bf16[192,1536]{1,0:T(8,128)(2,1)S(1)} %copy-done.23), channel_id=1, source_target_pairs={{0,1},{1,0},{2,3},{3,2},{4,5},{5,4},{6,7},{7,6},{8,9},{9,8},{10,11... | collective-permute-start | bytes 1769480 | tf_op jit(solution)/shard_map/ppermute | solution.py:238
  145.6 30.2 %collective-permute-start.3 = (bf16[4,1,192,768]{3,2,0,1:T(8,128)(2,1)S(1)}, bf16[4,1,192,768]{3,2,0,1:T(8,128)(2,1)S(1)}, u32[]{:S(2)}, u32[]{:S(2)}) collective-permute-start(bf16[4,1,192,768]{3,2,0,1:T(8,128)(2,1)S(1)} %bitcast.181), channel_id=1, source_target_pairs={{0,4},{4,0},{8,12},{12,8},{16,20},{20,16},{24,28},{28,24},{1,5},{5... | collective-permute-start | bytes 3538952 | tf_op jit(solution)/shard_map/ppermute | solution.py:238
  145.7 28.4 %collective-permute-start.8 = (bf16[192,1536]{1,0:T(8,128)(2,1)S(1)}, bf16[192,1536]{1,0:T(8,128)(2,1)S(1)}, u32[]{:S(2)}, u32[]{:S(2)}) collective-permute-start(bf16[192,1536]{1,0:T(8,128)(2,1)S(1)} %copy-done.23), channel_id=1, source_target_pairs={{0,2},{1,3},{2,0},{3,1},{4,6},{5,7},{6,4},{7,5},{8,10},{9,11},{10,... | collective-permute-start | bytes 1769480 | tf_op jit(solution)/shard_map/ppermute | solution.py:238
  148.2 26.8 %collective-permute-start.9 = (bf16[192,1536]{1,0:T(8,128)(2,1)S(1)}, bf16[192,1536]{1,0:T(8,128)(2,1)S(1)}, u32[]{:S(2)}, u32[]{:S(2)}) collective-permute-start(bf16[192,1536]{1,0:T(8,128)(2,1)S(1)} %copy-done.23), channel_id=1, source_target_pairs={{0,3},{1,2},{2,1},{3,0},{4,7},{5,6},{6,5},{7,4},{8,11},{9,10},{10,... | collective-permute-start | bytes 1769480 | tf_op jit(solution)/shard_map/ppermute | solution.py:238
  152.6 26.1 %collective-permute-start.16 = (bf16[4,1,192,768]{3,2,1,0:T(8,128)(2,1)}, bf16[4,1,192,768]{3,2,1,0:T(8,128)(2,1)}, u32[]{:S(2)}, u32[]{:S(2)}) collective-permute-start(bf16[4,1,192,768]{3,2,1,0:T(8,128)(2,1)} %bitcast_dynamic-update-slice_fusion.3), channel_id=1, source_target_pairs={{0,4},{4,0},{8,12},{12,8},{16,20},{20,16},{24,28},{28,24},{1,5},{5... | collective-permute-start | bytes 3538952 | tf_op jit(solution)/shard_map/ppermute | solution.py:238
  346.8 53.3 %collective-permute-start.52 = (bf16[192,1536]{1,0:T(8,128)(2,1)S(1)}, bf16[192,1536]{1,0:T(8,128)(2,1)S(1)}, u32[]{:S(2)}, u32[]{:S(2)}) collective-permute-start(bf16[192,1536]{1,0:T(8,128)(2,1)S(1)} %get-tuple-element.35), channel_id=1, source_target_pairs={{0,1},{1,0},{2,3},{3,2},{4,5},{5,4},{6,7},{7,6},{8,9},{9,8},{10,11... | collective-permute-start | bytes 1769480 | tf_op jit(solution)/shard_map/ppermute | solution.py:238
  349.2 23.6 %collective-permute-start.31 = (bf16[192,1152]{1,0:T(8,128)(2,1)S(1)}, bf16[192,1152]{1,0:T(8,128)(2,1)S(1)}, u32[]{:S(2)}, u32[]{:S(2)}) collective-permute-start(bf16[192,1152]{1,0:T(8,128)(2,1)S(1)} %get-tuple-element.41), channel_id=1, source_target_pairs={{0,1},{1,0},{2,3},{3,2},{4,5},{5,4},{6,7},{7,6},{8,9},{9,8},{10,11... | collective-permute-start | bytes 1327112 | tf_op jit(solution)/shard_map/ppermute | solution.py:238
  349.3 26.4 %collective-permute-start.32 = (bf16[192,1152]{1,0:T(8,128)(2,1)S(1)}, bf16[192,1152]{1,0:T(8,128)(2,1)S(1)}, u32[]{:S(2)}, u32[]{:S(2)}) collective-permute-start(bf16[192,1152]{1,0:T(8,128)(2,1)S(1)} %get-tuple-element.43), channel_id=1, source_target_pairs={{0,2},{1,3},{2,0},{3,1},{4,6},{5,7},{6,4},{7,5},{8,10},{9,11},{10,... | collective-permute-start | bytes 1327112 | tf_op jit(solution)/shard_map/ppermute | solution.py:238
  351.3 32.5 %collective-permute-start.33 = (bf16[192,1152]{1,0:T(8,128)(2,1)S(1)}, bf16[192,1152]{1,0:T(8,128)(2,1)S(1)}, u32[]{:S(2)}, u32[]{:S(2)}) collective-permute-start(bf16[192,1152]{1,0:T(8,128)(2,1)S(1)} %get-tuple-element.42), channel_id=1, source_target_pairs={{0,3},{1,2},{2,1},{3,0},{4,7},{5,6},{6,5},{7,4},{8,11},{9,10},{10,... | collective-permute-start | bytes 1327112 | tf_op jit(solution)/shard_map/ppermute | solution.py:238
  359.7 40.4 %collective-permute-start.53 = (bf16[192,1536]{1,0:T(8,128)(2,1)S(1)}, bf16[192,1536]{1,0:T(8,128)(2,1)S(1)}, u32[]{:S(2)}, u32[]{:S(2)}) collective-permute-start(bf16[192,1536]{1,0:T(8,128)(2,1)S(1)} %get-tuple-element.37), channel_id=1, source_target_pairs={{0,2},{1,3},{2,0},{3,1},{4,6},{5,7},{6,4},{7,5},{8,10},{9,11},{10,... | collective-permute-start | bytes 1769480 | tf_op jit(solution)/shard_map/ppermute | solution.py:238
  372.7 28.8 %collective-permute-start.54 = (bf16[192,1536]{1,0:T(8,128)(2,1)S(1)}, bf16[192,1536]{1,0:T(8,128)(2,1)S(1)}, u32[]{:S(2)}, u32[]{:S(2)}) collective-permute-start(bf16[192,1536]{1,0:T(8,128)(2,1)S(1)} %get-tuple-element.36), channel_id=1, source_target_pairs={{0,3},{1,2},{2,1},{3,0},{4,7},{5,6},{6,5},{7,4},{8,11},{9,10},{10,... | collective-permute-start | bytes 1769480 | tf_op jit(solution)/shard_map/ppermute | solution.py:238
  397.3 122.0 %collective-permute-start.41 = (bf16[1536,384]{1,0:T(8,128)(2,1)S(1)}, bf16[1536,384]{1,0:T(8,128)(2,1)}, u32[]{:S(2)}, u32[]{:S(2)}) collective-permute-start(bf16[1536,384]{1,0:T(8,128)(2,1)S(1)} %copy-done.4), channel_id=1, source_target_pairs={{0,4},{4,0},{8,12},{12,8},{16,20},{20,16},{24,28},{28,24},{1,5},{5... | collective-permute-start | bytes 3538952 | tf_op jit(solution)/shard_map/ppermute | solution.py:238
  397.3 16.8 %collective-permute-start.62 = (bf16[384,768]{1,0:T(8,128)(2,1)S(1)}, bf16[384,768]{1,0:T(8,128)(2,1)S(1)}, u32[]{:S(2)}, u32[]{:S(2)}) collective-permute-start(bf16[384,768]{1,0:T(8,128)(2,1)S(1)} %get-tuple-element.32), channel_id=1, source_target_pairs={{0,1},{1,0},{2,3},{3,2},{4,5},{5,4},{6,7},{7,6},{8,9},{9,8},{10,11... | collective-permute-start | bytes 1769480 | tf_op jit(solution)/shard_map/ppermute | solution.py:238
  400.0 25.9 %collective-permute-start.63 = (bf16[384,768]{1,0:T(8,128)(2,1)S(1)}, bf16[384,768]{1,0:T(8,128)(2,1)S(1)}, u32[]{:S(2)}, u32[]{:S(2)}) collective-permute-start(bf16[384,768]{1,0:T(8,128)(2,1)S(1)} %get-tuple-element.34), channel_id=1, source_target_pairs={{0,2},{1,3},{2,0},{3,1},{4,6},{5,7},{6,4},{7,5},{8,10},{9,11},{10,... | collective-permute-start | bytes 1769480 | tf_op jit(solution)/shard_map/ppermute | solution.py:238
  400.1 25.8 %collective-permute-start.64 = (bf16[384,768]{1,0:T(8,128)(2,1)S(1)}, bf16[384,768]{1,0:T(8,128)(2,1)S(1)}, u32[]{:S(2)}, u32[]{:S(2)}) collective-permute-start(bf16[384,768]{1,0:T(8,128)(2,1)S(1)} %get-tuple-element.33), channel_id=1, source_target_pairs={{0,3},{1,2},{2,1},{3,0},{4,7},{5,6},{6,5},{7,4},{8,11},{9,10},{10,... | collective-permute-start | bytes 1769480 | tf_op jit(solution)/shard_map/ppermute | solution.py:238
  401.6 126.1 %collective-permute-start.27 = (bf16[4,1,192,768]{3,2,0,1:T(8,128)(2,1)}, bf16[4,1,192,768]{3,2,0,1:T(8,128)(2,1)S(1)}, u32[]{:S(2)}, u32[]{:S(2)}) collective-permute-start(bf16[4,1,192,768]{3,2,0,1:T(8,128)(2,1)} %bitcast_convert_fusion), channel_id=1, source_target_pairs={{0,4},{4,0},{8,12},{12,8},{16,20},{20,16},{24,28},{28,24},{1,5},{5... | collective-permute-start | bytes 3538952 | tf_op jit(solution)/shard_map/ppermute | solution.py:238
  414.1 13.9 %collective-permute-start.37 = (bf16[48,1152]{1,0:T(8,128)(2,1)S(1)}, bf16[48,1152]{1,0:T(8,128)(2,1)S(1)}, u32[]{:S(2)}, u32[]{:S(2)}) collective-permute-start(bf16[48,1152]{1,0:T(8,128)(2,1)S(1)} %get-tuple-element.29), channel_id=1, source_target_pairs={{0,8},{4,12},{8,0},{12,4},{16,24},{20,28},{24,16},{28,20},{1,9},{5... | collective-permute-start | bytes 331784 | tf_op jit(solution)/shard_map/ppermute | solution.py:238
  428.0 12.3 %collective-permute-start.55 = (bf16[48,1536]{1,0:T(8,128)(2,1)S(1)}, bf16[48,1536]{1,0:T(8,128)(2,1)S(1)}, u32[]{:S(2)}, u32[]{:S(2)}) collective-permute-start(bf16[48,1536]{1,0:T(8,128)(2,1)S(1)} %get-tuple-element.49), channel_id=1, source_target_pairs={{0,8},{4,12},{8,0},{12,4},{16,24},{20,28},{24,16},{28,20},{1,9},{5... | collective-permute-start | bytes 442376 | tf_op jit(solution)/shard_map/ppermute | solution.py:238
  435.2 14.9 %collective-permute-start.56 = (bf16[48,1536]{1,0:T(8,128)(2,1)S(1)}, bf16[48,1536]{1,0:T(8,128)(2,1)S(1)}, u32[]{:S(2)}, u32[]{:S(2)}) collective-permute-start(bf16[48,1536]{1,0:T(8,128)(2,1)S(1)} %get-tuple-element.51), channel_id=1, source_target_pairs={{0,16},{4,20},{8,24},{12,28},{16,0},{20,4},{24,8},{28,12},{1,17},{... | collective-permute-start | bytes 442376 | tf_op jit(solution)/shard_map/ppermute | solution.py:238
  435.3 14.9 %collective-permute-start.57 = (bf16[48,1536]{1,0:T(8,128)(2,1)S(1)}, bf16[48,1536]{1,0:T(8,128)(2,1)S(1)}, u32[]{:S(2)}, u32[]{:S(2)}) collective-permute-start(bf16[48,1536]{1,0:T(8,128)(2,1)S(1)} %get-tuple-element.50), channel_id=1, source_target_pairs={{0,24},{4,28},{8,16},{12,20},{16,8},{20,12},{24,0},{28,4},{1,25},{... | collective-permute-start | bytes 442376 | tf_op jit(solution)/shard_map/ppermute | solution.py:238
  440.3 13.4 %collective-permute-start.65 = (bf16[96,768]{1,0:T(8,128)(2,1)S(1)}, bf16[96,768]{1,0:T(8,128)(2,1)S(1)}, u32[]{:S(2)}, u32[]{:S(2)}) collective-permute-start(bf16[96,768]{1,0:T(8,128)(2,1)S(1)} %get-tuple-element.46), channel_id=1, source_target_pairs={{0,8},{4,12},{8,0},{12,4},{16,24},{20,28},{24,16},{28,20},{1,9},{5... | collective-permute-start | bytes 442376 | tf_op jit(solution)/shard_map/ppermute | solution.py:238
  453.7 80.5 %collective-permute-start.23 = (bf16[4,1,192,768]{3,2,1,0:T(8,128)(2,1)}, bf16[4,1,192,768]{3,2,1,0:T(8,128)(2,1)}, u32[]{:S(2)}, u32[]{:S(2)}) collective-permute-start(bf16[4,1,192,768]{3,2,1,0:T(8,128)(2,1)} %dynamic-slice_convert_fusion), channel_id=1, source_target_pairs={{0,4},{4,0},{8,12},{12,8},{16,20},{20,16},{24,28},{28,24},{1,5},{5... | collective-permute-start | bytes 3538952 | tf_op jit(solution)/shard_map/ppermute | solution.py:238
  468.5 11.5 %collective-permute-start.69 = (bf16[96,768]{1,0:T(8,128)(2,1)S(1)}, bf16[96,768]{1,0:T(8,128)(2,1)S(1)}, u32[]{:S(2)}, u32[]{:S(2)}) collective-permute-start(bf16[96,768]{1,0:T(8,128)(2,1)S(1)} %get-tuple-element.23), channel_id=1, source_target_pairs={{0,16},{4,20},{8,24},{12,28},{16,0},{20,4},{24,8},{28,12},{1,17},{... | collective-permute-start | bytes 442376 | tf_op jit(solution)/shard_map/ppermute | solution.py:238
  482.7 33.2 %collective-permute-start.40 = (bf16[192,3,384]{2,0,1:T(8,128)(2,1)}, bf16[192,3,384]{2,0,1:T(8,128)(2,1)}, u32[]{:S(2)}, u32[]{:S(2)}) collective-permute-start(bf16[192,3,384]{2,0,1:T(8,128)(2,1)} %pad_maximum_fusion.1), channel_id=1, source_target_pairs={{0,4},{4,0},{8,12},{12,8},{16,20},{20,16},{24,28},{28,24},{1,5},{5... | collective-permute-start | bytes 1327112 | tf_op jit(solution)/shard_map/ppermute | solution.py:238
  486.9 118.8 %collective-permute-start.71 = (bf16[384,768]{1,0:T(8,128)(2,1)}, bf16[384,768]{1,0:T(8,128)(2,1)}, u32[]{:S(2)}, u32[]{:S(2)}) collective-permute-start(bf16[384,768]{1,0:T(8,128)(2,1)} %constant_dynamic-update-slice_fusion.12), channel_id=1, source_target_pairs={{0,4},{4,0},{8,12},{12,8},{16,20},{20,16},{24,28},{28,24},{1,5},{5... | collective-permute-start | bytes 1769480 | tf_op jit(solution)/shard_map/ppermute | solution.py:238
  515.9 92.5 %collective-permute-start.61 = (bf16[192,4,1,384]{3,1,0,2:T(4,128)(2,1)S(1)}, bf16[192,4,1,384]{3,1,0,2:T(4,128)(2,1)S(1)}, u32[]{:S(2)}, u32[]{:S(2)}) collective-permute-start(bf16[192,4,1,384]{3,1,0,2:T(4,128)(2,1)S(1)} %copy-done.15), channel_id=1, source_target_pairs={{0,4},{4,0},{8,12},{12,8},{16,20},{20,16},{24,28},{28,24},{1,5},{5... | collective-permute-start | bytes 1769480 | tf_op jit(solution)/shard_map/ppermute | solution.py:238
  524.9 11.3 %collective-permute-start.42 = (bf16[192,384]{1,0:T(8,128)(2,1)S(1)}, bf16[192,384]{1,0:T(8,128)(2,1)S(1)}, u32[]{:S(2)}, u32[]{:S(2)}) collective-permute-start(bf16[192,384]{1,0:T(8,128)(2,1)S(1)} %get-tuple-element.52), channel_id=1, source_target_pairs={{0,1},{1,0},{2,3},{3,2},{4,5},{5,4},{6,7},{7,6},{8,9},{9,8},{10,11... | collective-permute-start | bytes 442376 | tf_op jit(solution)/shard_map/ppermute | solution.py:238
  545.5 28.5 %collective-permute-start.28 = (bf16[1,192,768]{2,1,0:T(8,128)(2,1)S(1)}, bf16[1,192,768]{2,1,0:T(8,128)(2,1)S(1)}, u32[]{:S(2)}, u32[]{:S(2)}) collective-permute-start(bf16[1,192,768]{2,1,0:T(8,128)(2,1)S(1)} %get-tuple-element.57), channel_id=1, source_target_pairs={{0,8},{4,12},{8,0},{12,4},{16,24},{20,28},{24,16},{28,20},{1,9},{5... | collective-permute-start | bytes 884744 | tf_op jit(solution)/shard_map/ppermute | solution.py:238
  546.0 28.1 %collective-permute-start.29 = (bf16[1,192,768]{2,1,0:T(8,128)(2,1)S(1)}, bf16[1,192,768]{2,1,0:T(8,128)(2,1)S(1)}, u32[]{:S(2)}, u32[]{:S(2)}) collective-permute-start(bf16[1,192,768]{2,1,0:T(8,128)(2,1)S(1)} %get-tuple-element.56), channel_id=1, source_target_pairs={{0,16},{4,20},{8,24},{12,28},{16,0},{20,4},{24,8},{28,12},{1,17},{... | collective-permute-start | bytes 884744 | tf_op jit(solution)/shard_map/ppermute | solution.py:238
  549.9 10.7 %collective-permute-start.48 = (bf16[48,384]{1,0:T(8,128)(2,1)S(1)}, bf16[48,384]{1,0:T(8,128)(2,1)S(1)}, u32[]{:S(2)}, u32[]{:S(2)}) collective-permute-start(bf16[48,384]{1,0:T(8,128)(2,1)S(1)} %get-tuple-element.27), channel_id=1, source_target_pairs={{0,8},{4,12},{8,0},{12,4},{16,24},{20,28},{24,16},{28,20},{1,9},{5... | collective-permute-start | bytes 110600 | tf_op jit(solution)/shard_map/ppermute | solution.py:238
  572.0 11.8 %collective-permute-start.30 = (bf16[1,192,768]{2,1,0:T(8,128)(2,1)S(1)}, bf16[1,192,768]{2,1,0:T(8,128)(2,1)S(1)}, u32[]{:S(2)}, u32[]{:S(2)}) collective-permute-start(bf16[1,192,768]{2,1,0:T(8,128)(2,1)S(1)} %get-tuple-element.55), channel_id=1, source_target_pairs={{0,24},{4,28},{8,16},{12,20},{16,8},{20,12},{24,0},{28,4},{1,25},{... | collective-permute-start | bytes 884744 | tf_op jit(solution)/shard_map/ppermute | solution.py:238
  574.0 15.5 %collective-permute-start.24 = (bf16[1,192,768]{2,1,0:T(8,128)(2,1)S(1)}, bf16[1,192,768]{2,1,0:T(8,128)(2,1)S(1)}, u32[]{:S(2)}, u32[]{:S(2)}) collective-permute-start(bf16[1,192,768]{2,1,0:T(8,128)(2,1)S(1)} %get-tuple-element.61), channel_id=1, source_target_pairs={{0,8},{4,12},{8,0},{12,4},{16,24},{20,28},{24,16},{28,20},{1,9},{5... | collective-permute-start | bytes 884744 | tf_op jit(solution)/shard_map/ppermute | solution.py:238
  574.1 30.0 %collective-permute-start.25 = (bf16[1,192,768]{2,1,0:T(8,128)(2,1)S(1)}, bf16[1,192,768]{2,1,0:T(8,128)(2,1)S(1)}, u32[]{:S(2)}, u32[]{:S(2)}) collective-permute-start(bf16[1,192,768]{2,1,0:T(8,128)(2,1)S(1)} %get-tuple-element.60), channel_id=1, source_target_pairs={{0,16},{4,20},{8,24},{12,28},{16,0},{20,4},{24,8},{28,12},{1,17},{... | collective-permute-start | bytes 884744 | tf_op jit(solution)/shard_map/ppermute | solution.py:238
  583.8 20.3 %collective-permute-start.26 = (bf16[1,192,768]{2,1,0:T(8,128)(2,1)S(1)}, bf16[1,192,768]{2,1,0:T(8,128)(2,1)S(1)}, u32[]{:S(2)}, u32[]{:S(2)}) collective-permute-start(bf16[1,192,768]{2,1,0:T(8,128)(2,1)S(1)} %get-tuple-element.59), channel_id=1, source_target_pairs={{0,24},{4,28},{8,16},{12,20},{16,8},{20,12},{24,0},{28,4},{1,25},{... | collective-permute-start | bytes 884744 | tf_op jit(solution)/shard_map/ppermute | solution.py:238
  589.5 33.7 %collective-permute-start.51 = (bf16[192,384]{1,0:T(8,128)(2,1)S(1)}, bf16[192,384]{1,0:T(8,128)(2,1)S(1)}, u32[]{:S(2)}, u32[]{:S(2)}) collective-permute-start(bf16[192,384]{1,0:T(8,128)(2,1)S(1)} %constant_dynamic-update-slice_fusion.22), channel_id=1, source_target_pairs={{0,4},{4,0},{8,12},{12,8},{16,20},{20,16},{24,28},{28,24},{1,5},{5... | collective-permute-start | bytes 442376 | tf_op jit(solution)/shard_map/ppermute | solution.py:238
  (87 other events, 792.8 us)

commit v2 on v1

--- a/solution.py
+++ b/solution.py
@@ -1,7 +1,9 @@
 import functools
+import math
 
 import jax
 import jax.numpy as jnp
+import numpy as np
 from jax import lax
 from jax.experimental import pallas as pl
 from jax.experimental.pallas import tpu as pltpu
@@ -40,8 +42,7 @@
     bias_ref,
     out_w_ref,
     cos_ref,
-    sin_lo_ref,
-    sin_hi_ref,
+    sin_ref,
     mixed_ref,
     dproj_ref,
     q_s,
@@ -64,12 +65,13 @@
     live = length_ref[0]
     lane = lax.broadcasted_iota(jnp.int32, (rows, 128), 1)
     low = lane < HEAD_DIM
+    first_half = lane % HEAD_DIM < ROTARY // 2
 
     def rope(x, span, back):
-        up = pltpu.roll(x, 120, 1) * sin_lo_ref[span, :]
-        down = pltpu.roll(x, 8, 1) * sin_hi_ref[span, :]
+        partner = jnp.where(first_half, pltpu.roll(x, 120, 1), pltpu.roll(x, 8, 1))
+        partner = partner * sin_ref[span, :]
         turned = x * cos_ref[span, :]
-        return turned - up - down if back else turned + up + down
+        return turned - partner if back else turned + partner
 
     def project(j, carry):
         start = pl.multiple_of(j * rows, rows)
@@ -192,7 +194,7 @@
     lax.fori_loop(0, seq_len // rows, finish, 0)
 
 
-def attention(length, attn_in, cot, w, bias, out_w, cos, sin_lo, sin_hi):
+def attention(length, attn_in, cot, w, bias, out_w, cos, sin):
     seq_len = attn_in.shape[0]
     pairs = w.shape[1] // 384
     rows = 256
@@ -214,7 +216,6 @@
             pl.BlockSpec((128, D), lambda p: (p, 0)),
             whole((seq_len, 128), lambda p: (0, 0)),
             whole((seq_len, 128), lambda p: (0, 0)),
-            whole((seq_len, 128), lambda p: (0, 0)),
         ],
         out_specs=[
             pl.BlockSpec((seq_len, 128), lambda p: (0, p)),
@@ -230,7 +231,161 @@
             flops=flops, bytes_accessed=12_000_000, transcendentals=pairs * seq_len * seq_len
         ),
         name="attention",
-    )(length, attn_in, cot, w, bias, out_w, cos, sin_lo, sin_hi)
+    )(length, attn_in, cot, w, bias, out_w, cos, sin)
+
+
+def mlp_kernel(
+    shard_ref,
+    rows_ref,
+    cot_ref,
+    affine_ref,
+    bias_ref,
+    *refs,
+    layout,
+    fsdp,
+    own_rows,
+    unit,
+    chunk,
+):
+    pieces = refs[: len(layout)]
+    attn_in_ref, out_ref, grad_in_ref, grads_ref, vec_ref = refs[len(layout) : len(layout) + 5]
+    mlp_in, mlp_in_t, w_up, w_down, sems = refs[len(layout) + 5 :]
+    seq_len = rows_ref.shape[0]
+    up_width = fsdp * unit
+    folds = unit // own_rows
+    rows = 256
+
+    copies = []
+    for n, (k, first, count) in enumerate(layout):
+        j = shard_ref[0] ^ k
+        count = min(count, own_rows - first)
+        source = pl.ds(0, count)
+        at = pl.ds(pl.multiple_of(j * own_rows + first, 16), count)
+        copies.append(
+            pltpu.make_async_copy(
+                pieces[n].at[source, pl.ds(0, up_width)], w_up.at[at, :], sems.at[n, 0]
+            )
+        )
+        for i in range(folds):
+            at = pl.ds(pl.multiple_of(j * unit + i * own_rows + first, 16), count)
+            copies.append(
+                pltpu.make_async_copy(
+                    pieces[n].at[source, pl.ds(up_width + i * D, D)],
+                    w_down.at[at, :],
+                    sems.at[n, 1 + i],
+                )
+            )
+    for copy in copies:
+        copy.start()
+
+    def normed_rows(span):
+        x = rows_ref[span, :].astype(f32)
+        center = x - jnp.mean(x, -1, keepdims=True)
+        return center * lax.rsqrt(jnp.mean(center * center, -1, keepdims=True) + norm_eps)
+
+    def prepare(j, cot_sum):
+        span = pl.ds(pl.multiple_of(j * rows, rows), rows)
+        normed = normed_rows(span)
+        attn_in_ref[span, :] = (normed * affine_ref[0:1, :] + affine_ref[1:2, :]).astype(bf16)
+        scaled = normed * affine_ref[2:3, :] + affine_ref[3:4, :]
+        mlp_in[span, :] = scaled.astype(bf16)
+        mlp_in_t[:, span] = scaled.T.astype(bf16)
+        return cot_sum + jnp.sum(cot_ref[span, :].astype(f32), 0, keepdims=True)
+
+    cot_sum = lax.fori_loop(0, seq_len // rows, prepare, jnp.zeros((1, D), f32))
+    for copy in copies:
+        copy.wait()
+
+    for c in range(up_width // chunk):
+        part = slice(c * chunk, (c + 1) * chunk)
+        pre_act = dot(mlp_in[...], w_up[:, part]) + bias_ref[:, part]
+        cdf = 0.5 + 0.5 * lax.erf(pre_act * inv_sqrt_two)
+        hidden = (pre_act * cdf).astype(bf16)
+        slope = cdf + pre_act * jnp.exp(-0.5 * pre_act * pre_act) * inv_sqrt_tau
+        grad_pre = (dot(cot_ref[...], w_down[part, :], NT) * slope).astype(bf16)
+        vec_ref[0:1, part] = jnp.sum(grad_pre.astype(f32), 0, keepdims=True)
+        forward = dot(hidden, w_down[part, :])
+        backward = dot(grad_pre, w_up[:, part], NT)
+        if c == 0:
+            out_ref[...] = forward
+            grad_in_ref[...] = backward
+        else:
+            out_ref[...] += forward
+            grad_in_ref[...] += backward
+        up_grad = dot(mlp_in_t[...], grad_pre).astype(bf16)
+        for j in range(fsdp):
+            grads_ref[j, :own_rows, part] = up_grad[j * own_rows : (j + 1) * own_rows]
+        down_grad = dot(hidden, cot_ref[...], TN).astype(bf16)
+        step = math.gcd(own_rows, chunk)
+        for r in range(0, chunk, step):
+            u = c * chunk + r
+            j, i, at = u // unit, u % unit // own_rows, u % own_rows
+            grads_ref[j, at : at + step, up_width + i * D : up_width + (i + 1) * D] = down_grad[
+                r : r + step
+            ]
+
+    def sums(j, carry):
+        span = pl.ds(pl.multiple_of(j * rows, rows), rows)
+        grad = grad_in_ref[span, :]
+        return (
+            carry[0] + jnp.sum(grad * normed_rows(span), 0, keepdims=True),
+            carry[1] + jnp.sum(grad, 0, keepdims=True),
+        )
+
+    none = jnp.zeros((1, D), f32)
+    gain_sum, shift_sum = lax.fori_loop(0, seq_len // rows, sums, (none, none))
+    vec_ref[1:2, :D] = gain_sum
+    vec_ref[2:3, :D] = shift_sum
+    vec_ref[3:4, :D] = cot_sum
+
+
+def mlp(shard, rows_in, cot, affine, bias, got, fsdp, unit):
+    seq_len = rows_in.shape[0]
+    layout = [(k, first, piece.shape[0]) for k, first, piece in got]
+    pieces = [piece for _, _, piece in got]
+    own_rows = D // fsdp
+    packed_width = pieces[0].shape[1]
+    up_width = fsdp * unit
+    chunk = 256
+    vmem = pl.BlockSpec(memory_space=pltpu.VMEM)
+    return pl.pallas_call(
+        functools.partial(
+            mlp_kernel, layout=layout, fsdp=fsdp, own_rows=own_rows, unit=unit, chunk=chunk
+        ),
+        in_specs=[pl.BlockSpec(memory_space=pltpu.SMEM)]
+        + [vmem] * 4
+        + [pl.BlockSpec(memory_space=pl.ANY)] * len(pieces),
+        out_specs=[vmem] * 5,
+        out_shape=[
+            jax.ShapeDtypeStruct((seq_len, D), bf16),
+            jax.ShapeDtypeStruct((seq_len, D), f32),
+            jax.ShapeDtypeStruct((seq_len, D), f32),
+            jax.ShapeDtypeStruct((fsdp, own_rows + 16, packed_width), bf16),
+            jax.ShapeDtypeStruct((8, up_width), f32),
+        ],
+        scratch_shapes=[
+            pltpu.VMEM((seq_len, D), bf16),
+            pltpu.VMEM((D, seq_len), bf16),
+            pltpu.VMEM((D, up_width), bf16),
+            pltpu.VMEM((up_width, D), bf16),
+            pltpu.SemaphoreType.DMA((len(pieces), 1 + unit // own_rows)),
+        ],
+        compiler_params=pltpu.CompilerParams(vmem_limit_bytes=58 * 1024 * 1024),
+        cost_estimate=pl.CostEstimate(
+            flops=12 * seq_len * D * up_width,
+            bytes_accessed=30_000_000,
+            transcendentals=2 * seq_len * up_width,
+        ),
+        name="mlp",
+    )(shard, rows_in, cot, affine, bias, *pieces)
+
+
+def take(x, at, size, axis=0):
+    return lax.dynamic_slice_in_dim(x, at * size, size, axis)
+
+
+def place(out, piece, at, axis=0):
+    return lax.dynamic_update_slice_in_dim(out, piece, at * piece.shape[axis], axis)
 
 
 def swap(x, axis, by):
@@ -238,50 +393,64 @@
     return lax.ppermute(x, axis, [(j, j ^ by) for j in range(n)])
 
 
-def place(out, piece, at, axis=0):
-    return lax.dynamic_update_slice_in_dim(out, piece, at * piece.shape[axis], axis)
-
-
-def take(x, at, size, axis=0):
-    return lax.dynamic_slice_in_dim(x, at * size, size, axis)
-
-
-def gather(x, axis, me, n, step=1, dim=0):
-    shape = list(x.shape)
-    shape[dim] *= n
-    out = place(jnp.zeros(shape, x.dtype), x, me, dim)
-    for s in range(1, n):
-        out = place(out, swap(x, axis, s * step), me ^ s, dim)
+def exchange(x, group):
+    axis, n, step, me = group
+    return [(me ^ s, swap(take(x, me ^ s, 1), axis, s * step) if s else take(x, me, 1)) for s in range(n)]
+
+
+def gather(x, group):
+    axis, n, step, me = group
+    return [(me ^ s, swap(x, axis, s * step) if s else x) for s in range(n)]
+
+
+def gather_rows(x, group):
+    axis, n, step, _ = group
+    if n != 4:
+        return [(k, 0, swap(x, axis, k * step) if k else x) for k in range(n)]
+    one, two = swap(x, axis, step), swap(x, axis, 2 * step)
+    half = x.shape[0] // 2
+    return [
+        (0, 0, x),
+        (1, 0, one),
+        (2, 0, two),
+        (3, 0, swap(one[:half], axis, 2 * step)),
+        (3, half, swap(two[half:], axis, step)),
+    ]
+
+
+def stacked(pieces):
+    if len(pieces) == 2:
+        (me, own), (_, other) = pieces
+        first = me == 0
+        return jnp.stack([jnp.where(first, own, other), jnp.where(first, other, own)])
+    out = jnp.zeros((len(pieces),) + pieces[0][1].shape, pieces[0][1].dtype)
+    for j, piece in pieces:
+        out = place(out, piece[None], j)
     return out
 
 
-def scatter_sum(x, axis, me, n, step=1, dim=0):
-    size = x.shape[dim] // n
-    total = take(x, me, size, dim).astype(f32)
-    for s in range(1, n):
-        part = take(x, me ^ s, size, dim).astype(bf16)
-        total = total + swap(part, axis, s * step).astype(f32)
-    return total
-
-
-def exchange(x, axis, me, n, step=1):
-    out = place(jnp.zeros_like(x), take(x, me, 1), me)
-    for s in range(1, n):
-        out = place(out, swap(take(x, me ^ s, 1), axis, s * step), me ^ s)
-    return out
+def after(x, pieces):
+    held, arrived = lax.optimization_barrier((x, [piece[-1] for piece in pieces]))
+    return held, [piece[:-1] + (got,) for piece, got in zip(pieces, arrived)]
+
+
+def total(pieces):
+    return sum(piece[0].astype(f32) for _, piece in pieces)
+
+
+def scatter_sum(x, group):
+    return total(exchange(x, group))
 
 
 def rope_tables(seq_len):
     half = ROTARY // 2
-    frequency = rope_base ** (-2.0 * jnp.arange(half, dtype=f32) / ROTARY)
-    angles = jnp.arange(seq_len, dtype=jnp.int32).astype(f32)[:, None] * frequency[None, :]
-    cosine, sine = jnp.cos(angles), jnp.sin(angles)
-    rest = jnp.zeros((seq_len, HEAD_DIM - ROTARY), f32)
-    none = jnp.zeros((seq_len, half), f32)
-    cos = jnp.concatenate([cosine, cosine, rest + 1.0] * 2, 1)
-    sin_lo = jnp.concatenate([-sine, none, rest] * 2, 1)
-    sin_hi = jnp.concatenate([none, sine, rest] * 2, 1)
-    return cos, sin_lo, sin_hi
+    frequency = rope_base ** (-2.0 * np.arange(half) / ROTARY)
+    angles = np.arange(seq_len)[:, None] * frequency[None, :]
+    cosine, sine = np.cos(angles), np.sin(angles)
+    rest = np.zeros((seq_len, HEAD_DIM - ROTARY))
+    cos = np.concatenate([cosine, cosine, rest + 1.0] * 2, 1)
+    sin = np.concatenate([-sine, sine, rest] * 2, 1)
+    return jnp.asarray(cos, f32), jnp.asarray(sin, f32)
 
 
 def local(
@@ -321,17 +490,6 @@
             [x[:, t, p * 128 : (p + 1) * 128] for p in range(pairs) for t in range(3)], 1
         )
 
-    def from_pair(x):
-        rows = x.shape[0]
-        parts = []
-        for t in range(3):
-            parts.append(
-                jnp.concatenate(
-                    [x[:, p * 384 + t * 128 : p * 384 + (t + 1) * 128] for p in range(pairs)], 1
-                )[:, None, :lanes]
-            )
-        return jnp.concatenate(parts, 1).reshape(rows, 3, lanes)
-
     unit = FF // (fsdp * team)
 
     def up_columns(x):
@@ -340,31 +498,59 @@
             1,
         )
 
-    tok_half = exchange(tokens, "ctx", seq, seqs, team)
-    cot_half = exchange(cotangent, "ctx", seq, seqs, team)
-
-    def join(half):
-        return gather(half[:, None], "ctx", seat, team, 1, 1).reshape(seq_len, D)
-
-    rows_in = join(tok_half)
-    cot = join(cot_half)
-
-    vectors = jnp.concatenate(
-        [qkv_bias, out_bias, up_bias, down_bias, attn_gain, attn_shift, mlp_gain, mlp_shift]
-    )[None]
-    vectors = gather(vectors, "fsdp", shard, fsdp)
+    seqs_group = ("ctx", seqs, team, seq)
+    team_group = ("ctx", team, 1, seat)
+    fsdp_group = ("fsdp", fsdp, 1, shard)
+    own_rows = D // fsdp
+    folds = unit // own_rows
+
+    both = []
+    for s in range(seqs):
+        block = jnp.concatenate([take(tokens, seq ^ s, 1), take(cotangent, seq ^ s, 1)])
+        both.append((seq ^ s, swap(block, "ctx", s * team) if s else block))
+    half = stacked(both)
+    joined = gather(half, team_group)
+    tok_half = half[:, 0]
+    rows_in = stacked([(j, h[:, 0]) for j, h in joined]).swapaxes(0, 1).reshape(seq_len, D)
+    cot = stacked([(j, h[:, 1]) for j, h in joined]).swapaxes(0, 1).reshape(seq_len, D)
+
+    down_own = take(down_weight, seat, unit)
+    mlp_pack = jnp.concatenate(
+        [up_columns(up_weight)] + [down_own[i * own_rows : (i + 1) * own_rows] for i in range(folds)],
+        1,
+    )
+    up_width = fsdp * unit
+    mlp_width = up_width + folds * D
+    vectors = (qkv_bias, out_bias, up_bias, down_bias, attn_gain, attn_shift, mlp_gain, mlp_shift)
+    vector_size = sum(v.shape[0] for v in vectors)
+    vector_pack = jnp.pad(jnp.concatenate(vectors), (0, mlp_width - vector_size))
+    vector_pack = jnp.pad(vector_pack[None], ((0, 31), (0, 0)))
+    mlp_pack = jnp.concatenate([mlp_pack, vector_pack], 0)
+    mlp_got = gather_rows(mlp_pack, fsdp_group)
+    attn_pack = jnp.concatenate([by_pair(qkv_weight), out_weight], 1)
+    attn_pack, mlp_got = after(attn_pack, mlp_got)
+    attn_got = gather_rows(attn_pack, fsdp_group)
+    qkv_width = pairs * 384
+    packed = stacked(
+        [
+            (shard ^ k, piece[own_rows - first, :vector_size])
+            for k, first, piece in mlp_got
+            if first <= own_rows < first + piece.shape[0]
+        ]
+    )
     bounds = []
     at = 0
-    for v in (qkv_bias, out_bias, up_bias, down_bias, attn_gain, attn_shift, mlp_gain, mlp_shift):
-        bounds.append(vectors[:, at : at + v.shape[0]].reshape(-1).astype(f32))
+    for v in vectors:
+        bounds.append(packed[:, at : at + v.shape[0]].reshape(-1).astype(f32))
         at += v.shape[0]
     full_qkv_b, full_out_b, full_up_b, full_down_b, gain_a, shift_a, gain_m, shift_m = bounds
-    w_up = gather(up_columns(up_weight), "fsdp", shard, fsdp)
-    w_down = gather(take(down_weight, seat, unit), "fsdp", shard, fsdp)
-    w_qkv = gather(by_pair(qkv_weight), "fsdp", shard, fsdp)
-    w_out = gather(out_weight, "fsdp", shard, fsdp)
-    w_out_rows = take(w_out, seat, lanes)
-    w_out_rows = jnp.pad(w_out_rows, ((0, spare), (0, 0)))
+    w_qkv = jnp.zeros((D, qkv_width), bf16)
+    w_out = jnp.zeros((D, D), bf16)
+    for k, first, piece in attn_got:
+        at = (shard ^ k) * own_rows + first
+        w_qkv = lax.dynamic_update_slice(w_qkv, piece[:, :qkv_width], (at, 0))
+        w_out = lax.dynamic_update_slice(w_out, piece[:, qkv_width:], (at, 0))
+    w_out_rows = jnp.pad(take(w_out, seat, lanes), ((0, spare), (0, 0)))
     b_qkv = by_pair(full_qkv_b[None])
     b_up = up_columns(full_up_b[None])
 
@@ -374,39 +560,155 @@
         inv = lax.rsqrt(jnp.mean(center * center, -1, keepdims=True) + norm_eps)
         return center * inv, inv
 
+    def columns(x):
+        return jnp.sum(x, 0)
+
+    def vector_row(parts, size):
+        row = jnp.concatenate([v.reshape(fsdp, -1) for v in parts], 1)
+        row = jnp.pad(row, ((0, 0), (0, size - row.shape[1])))[:, None]
+        return jnp.pad(row, ((0, 0), (0, 15), (0, 0))).astype(bf16)
+
     normed, _ = normalise(rows_in)
-    attn_in = (normed * gain_a + shift_a).astype(bf16)
-    mlp_in = (normed * gain_m + shift_m).astype(bf16)
-
-    pre_act = dot(mlp_in, w_up) + b_up
-    cdf = 0.5 * (1.0 + lax.erf(pre_act * inv_sqrt_two))
-    hidden = (pre_act * cdf).astype(bf16)
-    slope = cdf + pre_act * jnp.exp(-0.5 * pre_act * pre_act) * inv_sqrt_tau
-    grad_pre = (dot(cot, w_down, NT) * slope).astype(bf16)
-    down_grad = dot(hidden, cot, TN)
-    up_grad = dot(mlp_in, grad_pre, TN)
-    mlp_out = dot(hidden, w_down)
-    grad_mlp_in = dot(grad_pre, w_up, NT)
-
+    if seq_len <= 2048:
+        affine = jnp.concatenate(
+            [gain_a[None], shift_a[None], gain_m[None], shift_m[None], jnp.zeros((4, D), f32)]
+        )
+        attn_in, mlp_out, grad_mlp_in, mlp_grads, sums = mlp(
+            shard.reshape(1).astype(jnp.int32),
+            rows_in,
+            cot,
+            affine,
+            b_up,
+            mlp_got,
+            fsdp,
+            unit,
+        )
+        row = vector_row(
+            [sums[0], sums[1, :D], sums[2, :D], sums[3, :D] * (1.0 / team)], mlp_width
+        )
+        mlp_grads = lax.dynamic_update_slice(mlp_grads, row, (0, own_rows, 0))
+    else:
+        w_up = jnp.zeros((D, up_width), bf16)
+        w_down = jnp.zeros((fsdp, folds, own_rows, D), bf16)
+        for k, _, piece in mlp_got:
+            w_up = place(w_up, piece[:own_rows, :up_width], shard ^ k)
+            for i in range(folds):
+                part = piece[:own_rows, up_width + i * D : up_width + (i + 1) * D]
+                w_down = lax.dynamic_update_slice(w_down, part[None, None], (shard ^ k, i, 0, 0))
+        w_down = w_down.reshape(up_width, D)
+        attn_in = (normed * gain_a + shift_a).astype(bf16)
+        mlp_in = (normed * gain_m + shift_m).astype(bf16)
+
+        pre_act = dot(mlp_in, w_up) + b_up
+        cdf = 0.5 * (1.0 + lax.erf(pre_act * inv_sqrt_two))
+        hidden = (pre_act * cdf).astype(bf16)
+        slope = cdf + pre_act * jnp.exp(-0.5 * pre_act * pre_act) * inv_sqrt_tau
+        grad_pre = (dot(cot, w_down, NT) * slope).astype(bf16)
+        down_grad = dot(hidden, cot, TN)
+        up_grad = dot(mlp_in, grad_pre, TN)
+        mlp_out = dot(hidden, w_down)
+        grad_mlp_in = dot(grad_pre, w_up, NT)
+
+        cot_sum = columns(cot.astype(f32)) * (1.0 / team)
+        mlp_grads = jnp.concatenate(
+            [up_grad.astype(bf16).reshape(fsdp, own_rows, up_width)]
+            + [
+                down_grad.astype(bf16).reshape(fsdp, folds, own_rows, D)[:, i] for i in range(folds)
+            ],
+            2,
+        )
+        mlp_grads = jnp.concatenate(
+            [
+                mlp_grads,
+                vector_row(
+                    [
+                        columns(grad_pre.astype(f32)),
+                        columns(grad_mlp_in * normed),
+                        columns(grad_mlp_in),
+                        cot_sum,
+                    ],
+                    mlp_width,
+                ),
+            ],
+            1,
+        )
+
+    def spread(mine):
+        cols = mine.shape[1] // seqs
+        return [
+            (s, swap(take(mine, seq ^ s, cols, 1), "ctx", s * team) if s else take(mine, seq, cols, 1))
+            for s in range(seqs)
+        ]
+
+    def joined_columns(pieces):
+        rows, cols = pieces[0][1].shape
+        whole = jnp.zeros((rows, seqs * cols), bf16)
+        for j, piece in pieces:
+            whole = place(whole, piece, j, 1)
+        return stacked(gather(whole, team_group))
+
+    def summed(parts):
+        return sum(part.astype(f32) for _, part in parts).astype(bf16)
+
+    attn_in, cot_held, mlp_grads = lax.optimization_barrier((attn_in, cot, mlp_grads))
+    mlp_pieces = exchange(mlp_grads, fsdp_group)
     length = lax.dynamic_slice_in_dim(lengths, seq, 1, 0)
     mixed, grad_proj = attention(
-        length, attn_in, cot, w_qkv, b_qkv, w_out_rows, *rope_tables(seq_len)
-    )
+        length, attn_in, cot_held, w_qkv, b_qkv, w_out_rows, *rope_tables(seq_len)
+    )
+    (mixed, grad_proj), mlp_pieces = after((mixed, grad_proj), mlp_pieces)
+    mlp_mine = total(mlp_pieces).astype(bf16)
+    mixed, grad_proj, mlp_mine = lax.optimization_barrier((mixed, grad_proj, mlp_mine))
+    mlp_parts = spread(mlp_mine)
+    mixed_all = stacked(gather(mixed[:, :lanes], team_group)).swapaxes(0, 1).reshape(seq_len, D)
+    qkv_grad = dot(attn_in, grad_proj, TN)
+    grad_attn_in = dot(grad_proj, w_qkv, NT)
     delta_out = mlp_out + dot(mixed, w_out_rows)
-    mixed_all = gather(mixed[:, :lanes], "ctx", seat, team, 1, 1)
     out_cols = D // team
     out_grad = dot(mixed_all, take(cot, seat, out_cols, 1), TN)
-    qkv_grad = dot(attn_in, grad_proj, TN)
-    grad_attn_in = dot(grad_proj, w_qkv, NT)
+
+    qkv_b_grad = columns(grad_proj.astype(f32))
+    qkv_b_grad = jnp.concatenate(
+        [
+            jnp.concatenate(
+                [
+                    qkv_b_grad[p * 384 + i * 128 : p * 384 + i * 128 + min(128, lanes - p * 128)]
+                    for p in range(pairs)
+                ]
+            )[None]
+            for i in range(3)
+        ],
+        0,
+    )
+    qkv_b_grad = place(jnp.zeros((3, D), f32), qkv_b_grad, seat, 1)
+    attn_width = qkv_width + out_cols
+    attn_grads = jnp.concatenate(
+        [
+            qkv_grad.astype(bf16).reshape(fsdp, own_rows, qkv_width),
+            out_grad.astype(bf16).reshape(fsdp, own_rows, out_cols),
+        ],
+        2,
+    )
+    attn_grads = jnp.concatenate(
+        [
+            attn_grads,
+            vector_row(
+                [qkv_b_grad, columns(grad_attn_in * normed), columns(grad_attn_in)], attn_width
+            ),
+        ],
+        1,
+    )
+    attn_pieces = exchange(attn_grads, fsdp_group)
 
     def home(x):
-        blocks = x.reshape(seqs, team, width, D)
-        return scatter_sum(blocks, "ctx", seat, team, 1, 1).reshape(seqs, width, D)
-
-    delta_home = exchange(home(delta_out).astype(bf16), "ctx", seq, seqs, team)
-    layer_out = (tokens.astype(f32) + delta_home.astype(f32) + full_out_b + full_down_b).astype(
-        bf16
-    )
+        return scatter_sum(x.astype(bf16).reshape(seqs, team, width, D).swapaxes(0, 1), team_group)
+
+    def returned(pieces):
+        return stacked([(j, piece[0]) for j, piece in pieces])
+
+    delta_out, mlp_parts = after(home(delta_out).astype(bf16), mlp_parts)
+    mlp_part = summed(mlp_parts)
+    out_pieces = exchange(delta_out, seqs_group)
 
     grad_normed = home(grad_attn_in * gain_a + grad_mlp_in * gain_m)
     normed_half, inv_half = normalise(tok_half)
@@ -415,58 +717,71 @@
         - jnp.mean(grad_normed, -1, keepdims=True)
         - normed_half * jnp.mean(grad_normed * normed_half, -1, keepdims=True)
     )
-    delta_in = exchange(delta_in.astype(bf16), "ctx", seq, seqs, team)
-    tokens_grad = cotangent.astype(f32) + delta_in.astype(f32)
-
-    qkv_b_grad = from_pair(jnp.sum(grad_proj.astype(f32), 0)[None])
-    qkv_b_grad = place(jnp.zeros((3, D), f32), qkv_b_grad[0], seat, 1)
-    up_b_grad = jnp.sum(grad_pre.astype(f32), 0).reshape(fsdp, unit)
-    up_b_grad = place(jnp.zeros((fsdp, unit * team), f32), up_b_grad, seat, 1)
-    cot_sum = jnp.sum(cot.astype(f32), 0) * (1.0 / team)
-    sums = [
-        qkv_b_grad.reshape(-1),
-        cot_sum,
-        up_b_grad.reshape(-1),
-        jnp.sum(grad_attn_in * normed, 0),
-        jnp.sum(grad_attn_in, 0),
-        jnp.sum(grad_mlp_in * normed, 0),
-        jnp.sum(grad_mlp_in, 0),
-    ]
-    total = lax.psum(jnp.concatenate(sums).reshape(-1, 128), ("ctx", "fsdp")).reshape(-1)
-    vec = []
-    at = 0
-    for v in sums:
-        size = v.shape[0] // fsdp
-        vec.append(lax.dynamic_slice_in_dim(total[at : at + v.shape[0]], shard * size, size, 0))
-        at += v.shape[0]
-
-    def reduce(x):
-        mine = scatter_sum(x, "fsdp", shard, fsdp)
-        part = scatter_sum(mine, "ctx", seq, seqs, team).astype(bf16)
-        return gather(part, "ctx", seq, seqs, team)
-
-    up_mine = reduce(up_grad).reshape(D // fsdp, fsdp, 1, unit)
-    up_mine = gather(up_mine, "ctx", seat, team, 1, 2).reshape(D // fsdp, FF).astype(f32)
-    down_mine = gather(reduce(down_grad), "ctx", seat, team).astype(f32)
-    qkv_mine = from_pair(reduce(qkv_grad))
-    qkv_mine = gather(qkv_mine, "ctx", seat, team, 1, 2).reshape(D // fsdp, 3 * D).astype(f32)
-    out_mine = gather(reduce(out_grad), "ctx", seat, team, 1, 1).astype(f32)
+    delta_in, out_pieces = after(delta_in.astype(bf16), out_pieces)
+    in_pieces = exchange(delta_in, seqs_group)
+    layer_out = (
+        tokens.astype(f32) + returned(out_pieces).astype(f32) + full_out_b + full_down_b
+    ).astype(bf16)
+
+    mlp_part, in_pieces = after(mlp_part, in_pieces)
+    tokens_grad = cotangent.astype(f32) + returned(in_pieces).astype(f32)
+    mlp_whole = gather(mlp_part, seqs_group)
+    attn_mine, mlp_whole = after(total(attn_pieces).astype(bf16), mlp_whole)
+    attn_parts = spread(attn_mine)
+    mlp_all = joined_columns(mlp_whole)
+    attn_all = joined_columns(gather(summed(attn_parts), seqs_group))
+
+    up_mine = jnp.concatenate(
+        [
+            mlp_all[t, :own_rows, j * unit : (j + 1) * unit]
+            for j in range(fsdp)
+            for t in range(team)
+        ],
+        1,
+    ).astype(f32)
+    down_mine = jnp.concatenate(
+        [
+            mlp_all[t, :own_rows, up_width + i * D : up_width + (i + 1) * D]
+            for t in range(team)
+            for i in range(folds)
+        ],
+        0,
+    ).astype(f32)
+    qkv_mine = jnp.concatenate(
+        [
+            attn_all[
+                t, :own_rows, p * 384 + i * 128 : p * 384 + i * 128 + min(128, lanes - p * 128)
+            ]
+            for i in range(3)
+            for t in range(team)
+            for p in range(pairs)
+        ],
+        1,
+    ).astype(f32)
+    out_mine = jnp.concatenate([attn_all[t, :own_rows, qkv_width:] for t in range(team)], 1).astype(f32)
+    mlp_vec = mlp_all[:, own_rows].astype(f32)
+    attn_vec = columns(attn_all[:, own_rows].astype(f32))
+    up_b_mine = mlp_vec[:, :unit].reshape(-1)
+    mlp_vec = columns(mlp_vec)[unit:]
+    bias_mine = mlp_vec[2 * own_rows : 3 * own_rows]
+    qkv_b_mine = attn_vec[: 3 * own_rows]
+    attn_vec = attn_vec[3 * own_rows :]
 
     return (
         layer_out,
         tokens_grad,
         qkv_mine,
-        vec[0],
+        qkv_b_mine,
         out_mine,
-        vec[1],
+        bias_mine,
         up_mine,
-        vec[2],
+        up_b_mine,
         down_mine,
-        vec[1],
-        vec[3],
-        vec[4],
-        vec[5],
-        vec[6],
+        bias_mine,
+        attn_vec[:own_rows],
+        attn_vec[own_rows : 2 * own_rows],
+        mlp_vec[:own_rows],
+        mlp_vec[own_rows : 2 * own_rows],
     )
 
 

time: 634 us -> 443 us (0.70)
  waiting for transfers between devices: 190 us -> 124 us
  local copies, waits for them, and re-layouts: 135 us -> 86.2 us
  matrix products: 62 us -> 18.6 us
  Pallas kernels: 59.8 us -> 98.8 us
  blocking collectives: 37.3 us -> 0 us
  starting transfers between devices: 108 us -> 70.9 us
    ppermute x72 -> x41, waiting for transfers between devices: 190 us -> 124 us  [swap(): return lax.ppermute(x, axis, [(j, j ^ by) for j in range(n)])]
    dynamic_update_slice x60 -> x22, local copies, waits for them, and re-layouts: 67.8 us -> 7.13 us  [place(): lax.dynamic_update_slice_in_dim(out, piece, at * piece.shape[axis], axis)]
    dot_general x10 -> x4, matrix products: 62 us -> 18.6 us  [dot(): return lax.dot_general(a, b, dims, preferred_element_type=f32)]
    pallas_call x0 -> x1, Pallas kernels: none -> 39.6 us  [mlp(): pl.pallas_call(functools.partial(mlp_kernel, layout=layout, fsdp=fsdp, ow...]
    psum x1 -> x0, blocking collectives: 37.3 us -> none  [local(): lax.psum(jnp.concatenate(sums).reshape(-1, 128), ('ctx', 'fsdp'))]
    ppermute x72 -> x41, starting transfers between devices: 108 us -> 70.9 us  [swap(): return lax.ppermute(x, axis, [(j, j ^ by) for j in range(n)])]
    slice x5 -> x15, local copies, waits for them, and re-layouts: 0.11 us -> 10.8 us  [the longest x2 2.89 us: gather_rows(): two[half:]]
    dynamic_update_slice x0 -> x11, local copies, waits for them, and re-layouts: none -> 9.78 us  [the longest x5 4.76 us: local(): w_qkv = lax.dynamic_update_slice(w_qkv, piece[:, :qkv_width], (at, 0))]
  transfers between devices with their start and end apart: 72 -> 41, of which waited for: 32 -> 15; matrix products, arithmetic and copies ran while one was open for 24% -> 25% of each run, Pallas kernels for 0% -> 23%
where the time goes in v2:
time: 443 us; the launch traced here: 435 us
  waiting for transfers between devices  124 us (28%)
  Pallas kernels  98.8 us (22%)
  local copies, waits for them, and re-layouts  86.2 us (19%)
  starting transfers between devices  70.9 us (16%)
  other arithmetic  34.3 us (8%)
  matrix products  18.6 us (4%)
    ppermute x41, waiting for transfers between devices, swap(): return lax.ppermute(x, axis, [(j, j ^ by) for j in range(n)])  124 us
    ppermute x41, starting transfers between devices, swap(): return lax.ppermute(x, axis, [(j, j ^ by) for j in range(n)])  70.9 us
    pallas_call x1, Pallas kernels, attention(): pl.pallas_call(functools.partial(attention_kernel, seq_len=seq_len, rows=...  59.3 us
    pallas_call x1, Pallas kernels, mlp(): pl.pallas_call(functools.partial(mlp_kernel, layout=layout, fsdp=fsdp, ow...  39.6 us
    dot_general x4, matrix products, dot(): return lax.dot_general(a, b, dims, preferred_element_type=f32)  18.6 us
    unnamed x132, local copies, waits for them, and re-layouts  12.4 us
    dynamic_slice x12, local copies, waits for them, and re-layouts, take(): return lax.dynamic_slice_in_dim(x, at * size, size, axis)  11.7 us
  transfers between devices with their start and end apart: 41, of which 15 were waited for; matrix products, arithmetic and copies ran while one was open for 25% of the time, Pallas kernels for 23%

profile of v2, /device:TPU:0, one launch (start us, length us, event | category | flops | bytes accessed | tf_op | source)
XLA Modules:
  0.0 435.2 jit_solution(8792761344467323482)
XLA Ops:
  0.7 5.4 %concatenate.77 = bf16[2496]{0:T(1024)(128)(2,1)S(1)} concatenate(bf16[576]{0:T(1024)(128)(2,1)} %param.21, bf16[192]{0:T(256)(128)(2,1)} %param.23, bf16[768]{0:T(1024)(128)(2,1)} %param.25, bf16[192]{0:T(256)(128)(2,1)} %param.27, bf16[192]{0:T(256)(128)(2,1)} %param.28, bf16[192]{0:T(256)(128)(2,1)} %param.29, bf16[192]{0:T(256)(128)(2,1)} %param.30, bf16[192]{0:T(256)(128)(2,1)} %param.31), dimensions={0} | concatenate | bytes 9984 | tf_op jit(solution)/shard_map/concatenate | solution.py:526
  9.1 2.9 collective-permute-start.4
  13.8 1.6 collective-permute-start
  16.3 2.6 collective-permute-start.1
  20.4 1.7 constant_dynamic-slice_fusion.44
  27.5 1.7 constant_dynamic-update-slice_fusion
  29.2 10.4 %collective-permute-done = bf16[2,192,768]{2,1,0:T(8,128)(2,1)} collective-permute-done((bf16[2,192,768]{2,1,0:T(8,128)(2,1)S(1)}, bf16[2,192,768]{2,1,0:T(8,128)(2,1)}, u32[]{:S(2)}, u32[]{:S(2)}) %collective-permute-start) | collective-permute-done | bytes 589856 | tf_op jit(solution)/shard_map/ppermute | solution.py:393
  40.7 18.4 %collective-permute-done.1 = bf16[2,192,768]{2,1,0:T(8,128)(2,1)} collective-permute-done((bf16[2,192,768]{2,1,0:T(8,128)(2,1)}, bf16[2,192,768]{2,1,0:T(8,128)(2,1)}, u32[]{:S(2)}, u32[]{:S(2)}) %collective-permute-start.1) | collective-permute-done | bytes 589856 | tf_op jit(solution)/shard_map/ppermute | solution.py:393
  65.7 14.8 %collective-permute-done.6.refs_3_ = bf16[112,3072]{1,0:T(8,128)(2,1)S(1)} collective-permute-done((bf16[112,3072]{1,0:T(8,128)(2,1)S(1)}, bf16[112,3072]{1,0:T(8,128)(2,1)S(1)}, u32[]{:S(2)}, u32[]{:S(2)}) %collective-permute-start.6) | collective-permute-done | bytes 688160 | tf_op jit(solution)/shard_map/ppermute | solution.py:393
  93.2 9.7 %collective-permute-done.8 = bf16[192,1920]{1,0:T(8,128)(2,1)S(1)} collective-permute-done((bf16[192,1920]{1,0:T(8,128)(2,1)}, bf16[192,1920]{1,0:T(8,128)(2,1)S(1)}, u32[]{:S(2)}, u32[]{:S(2)}) %collective-permute-start.8) | collective-permute-done | bytes 737312 | tf_op jit(solution)/shard_map/ppermute | solution.py:393
  105.2 1.7 slice.481
  111.1 1.9 select_bitcast_fusion.5
  117.5 39.6 %mlp.1 = (bf16[1536,768]{1,0:T(8,128)(2,1)}, f32[1536,768]{1,0:T(8,128)}, f32[1536,768]{1,0:T(8,128)}, bf16[4,208,3072]{2,1,0:T(8,128)(2,1)}, f32[8,1536]{1,0:T(8,128)}) custom-call(s32[1]{0:T(128)} %bitcast.5.shard_ref, bf16[1536,768]{1,0:T(8,128)(2,1)} %bitcast.315, bf16[1536,768]{1,0:T(8,128)(2,1)} %bitcast.312, f32[8,768]{1,0:T(8,128)} %concatenate.79.affine_ref, ...), custom_call_target="tpu_custom_call" | custom-call | flops 21743271936 | bytes 30000000 | tf_op jit(solution)/shard_map/mlp/pallas_call | solution.py:351
  168.0 4.9 %constant_dynamic-slice_fusion.34 = (bf16[1,208,3072]{2,1,0:T(8,128)(2,1)}, bf16[1,208,3072]{2,1,0:T(8,128)(2,1)}, bf16[1,208,3072]{2,1,0:T(8,128)(2,1)}, bf16[1,208,3072]{2,1,0:T(8,128)(2,1)}) fusion(bf16[4,208,3072]{2,1,0:T(8,128)(2,1)} %pad_dynamic-update-slice_fusion, s32[]{:T(128)S(6)} %select_n.259, s32[]{:T(128)S(6)} %select_n.258, ...), kind=kLoop, calls=%fused_computation.226 | loop fusion | bytes 10223632 | tf_op jit(solution)/shard_map/dynamic_slice | solution.py:384
  178.1 1.6 slice_dynamic-update-slice_fusion.9
  179.7 1.6 slice_dynamic-update-slice_fusion.8
  181.3 1.9 constant_dynamic-slice_fusion.38.out_w_ref
  183.2 1.6 slice_dynamic-update-slice_fusion.7
  184.8 1.6 slice_dynamic-update-slice_fusion.6.w_ref
  186.5 59.3 %attention.1 = (bf16[1536,384]{1,0:T(8,128)(2,1)}, bf16[1536,1152]{1,0:T(8,128)(2,1)}) custom-call(s32[1]{0:T(128)} %dynamic_slice.154.length_ref, bf16[1536,768]{1,0:T(8,128)(2,1)} %get-tuple-element.67.attn_in_ref, bf16[1536,768]{1,0:T(8,128)(2,1)} %bitcast.313, bf16[768,1152]{1,0:T(8,128)(2,1)} %slice_dynamic-update-slice_fusion.6.w_ref, ...), custom_call_target="tpu_custom_call" | custom-call | flops 14495514624 | bytes 12000000 | tf_op jit(solution)/shard_map/attention/pallas_call | solution.py:207
  245.8 2.3 fusion.18
  250.0 6.4 %multiply_reduce_fusion = (bf16[768]{0:T(1024)(128)(2,1)}, bf16[768]{0:T(1024)(128)(2,1)}, bf16[1536,768]{1,0:T(8,128)(2,1)S(1)}) fusion(f32[1536]{0:T(1024)S(1)} %rsqrt.21, f32[1536]{0:T(1024)S(1)} %div.36, bf16[4,2,192,768]{3,2,1,0:T(8,128)(2,1)S(1)} %copy-done.16, f32[1536,768]{1,0:T(8,128)} %get-tuple-element.80, f32[768]{0:T(1024)S(1)} %copy-done.32, ...), kind=kOutput, calls=%fused_computation.7 | convolution fusion | flops 2729703936 | bytes 14767104 | tf_op jit(solution)/shard_map/dot_general | solution.py:34
  263.7 10.1 %collective-permute-start.17 = (bf16[208,768]{1,0:T(8,128)(2,1)}, bf16[208,768]{1,0:T(8,128)(2,1)}, u32[]{:S(2)}, u32[]{:S(2)}) collective-permute-start(bf16[208,768]{1,0:T(8,128)(2,1)} %get-tuple-element.138), channel_id=1, source_target_pairs={{0,8},{4,12},{8,0},{12,4},{16,24},{20,28},{24,16},{28,20},{1,9},{5... | collective-permute-start | bytes 958472 | tf_op jit(solution)/shard_map/ppermute | solution.py:393
  280.9 7.3 %convolution_convert_fusion = bf16[768,1152]{1,0:T(8,128)(2,1)} fusion(bf16[1536,768]{1,0:T(8,128)(2,1)} %get-tuple-element.67.attn_in_ref, bf16[1536,1152]{1,0:T(8,128)(2,1)} %get-tuple-element.79), kind=kOutput, calls=%fused_computation.10 | convolution fusion | flops 2718793728 | bytes 7667712 | tf_op jit(solution)/shard_map/dot_general | solution.py:34
  289.0 1.6 fusion.15
  290.6 8.5 %collective-permute-done.18 = bf16[208,768]{1,0:T(8,128)(2,1)} collective-permute-done((bf16[208,768]{1,0:T(8,128)(2,1)}, bf16[208,768]{1,0:T(8,128)(2,1)}, u32[]{:S(2)}, u32[]{:S(2)}) %collective-permute-start.18) | collective-permute-done | bytes 319520 | tf_op jit(solution)/shard_map/ppermute | solution.py:393
  300.2 6.7 %collective-permute-start.20 = (bf16[1,192,768]{2,1,0:T(8,128)(2,1)}, bf16[1,192,768]{2,1,0:T(8,128)(2,1)}, u32[]{:S(2)}, u32[]{:S(2)}) collective-permute-start(bf16[1,192,768]{2,1,0:T(8,128)(2,1)} %get-tuple-element.146), channel_id=1, source_target_pairs={{0,8},{4,12},{8,0},{12,4},{16,24},{20,28},{24,16},{28,20},{1,9},{5... | collective-permute-start | bytes 884744 | tf_op jit(solution)/shard_map/ppermute | solution.py:393
  309.3 2.2 fusion.16
  311.8 1.7 maximum_bitcast_fusion.2
  313.5 4.5 %copy.50 = bf16[1536,2,384]{0,2,1:T(8,128)(2,1)} copy(bf16[1536,2,384]{2,0,1:T(8,128)(2,1)} %maximum_bitcast_fusion.2) | data formatting | bytes 4718592 | tf_op jit(solution)/shard_map/transpose | solution.py:663
  318.0 3.5 convolution_convert_fusion.1
  324.9 2.0 fusion.13
  328.9 1.7 collective-permute-done.21
  330.7 5.0 %collective-permute-start.23 = (bf16[1,192,768]{2,1,0:T(8,128)(2,1)S(1)}, bf16[1,192,768]{2,1,0:T(8,128)(2,1)S(1)}, u32[]{:S(2)}, u32[]{:S(2)}) collective-permute-start(bf16[1,192,768]{2,1,0:T(8,128)(2,1)S(1)} %get-tuple-element.142), channel_id=1, source_target_pairs={{0,8},{4,12},{8,0},{12,4},{16,24},{20,28},{24,16},{28,20},{1,9},{5... | collective-permute-start | bytes 884744 | tf_op jit(solution)/shard_map/ppermute | solution.py:393
  340.1 6.8 %collective-permute-done.23 = bf16[1,192,768]{2,1,0:T(8,128)(2,1)S(1)} collective-permute-done((bf16[1,192,768]{2,1,0:T(8,128)(2,1)S(1)}, bf16[1,192,768]{2,1,0:T(8,128)(2,1)S(1)}, u32[]{:S(2)}, u32[]{:S(2)}) %collective-permute-start.23) | collective-permute-done | bytes 294944 | tf_op jit(solution)/shard_map/ppermute | solution.py:393
  349.7 7.5 %collective-permute-done.24 = bf16[1,192,768]{2,1,0:T(8,128)(2,1)S(1)} collective-permute-done((bf16[1,192,768]{2,1,0:T(8,128)(2,1)S(1)}, bf16[1,192,768]{2,1,0:T(8,128)(2,1)S(1)}, u32[]{:S(2)}, u32[]{:S(2)}) %collective-permute-start.24) | collective-permute-done | bytes 294944 | tf_op jit(solution)/shard_map/ppermute | solution.py:393
  357.2 5.9 %collective-permute-start.30 = (bf16[208,768]{1,0:T(8,128)(2,1)S(1)}, bf16[208,768]{1,0:T(8,128)(2,1)S(1)}, u32[]{:S(2)}, u32[]{:S(2)}) collective-permute-start(bf16[208,768]{1,0:T(8,128)(2,1)S(1)} %add_convert_fusion.5), channel_id=1, source_target_pairs={{0,8},{4,12},{8,0},{12,4},{16,24},{20,28},{24,16},{28,20},{1,9},{5... | collective-permute-start | bytes 958472 | tf_op jit(solution)/shard_map/ppermute | solution.py:393
  365.9 9.3 %collective-permute-done.30 = bf16[208,768]{1,0:T(8,128)(2,1)S(1)} collective-permute-done((bf16[208,768]{1,0:T(8,128)(2,1)S(1)}, bf16[208,768]{1,0:T(8,128)(2,1)S(1)}, u32[]{:S(2)}, u32[]{:S(2)}) %collective-permute-start.30) | collective-permute-done | bytes 319520 | tf_op jit(solution)/shard_map/ppermute | solution.py:393
  375.2 14.6 %collective-permute-done.31 = bf16[208,768]{1,0:T(8,128)(2,1)S(1)} collective-permute-done((bf16[208,768]{1,0:T(8,128)(2,1)S(1)}, bf16[208,768]{1,0:T(8,128)(2,1)S(1)}, u32[]{:S(2)}, u32[]{:S(2)}) %collective-permute-start.31) | collective-permute-done | bytes 319520 | tf_op jit(solution)/shard_map/ppermute | solution.py:393
  389.9 2.5 collective-permute-start.35
  392.4 4.2 collective-permute-start.34
  398.0 9.2 %collective-permute-done.34 = bf16[208,384]{1,0:T(8,128)(2,1)S(1)} collective-permute-done((bf16[208,384]{1,0:T(8,128)(2,1)S(1)}, bf16[208,384]{1,0:T(8,128)(2,1)S(1)}, u32[]{:S(2)}, u32[]{:S(2)}) %collective-permute-start.34) | collective-permute-done | bytes 159776 | tf_op jit(solution)/shard_map/ppermute | solution.py:393
  407.5 1.8 collective-permute-start.37
  409.3 2.7 collective-permute-start.38
  412.0 2.9 collective-permute-done.36
  415.0 7.3 %collective-permute-done.37 = bf16[208,384]{1,0:T(8,128)(2,1)S(1)} collective-permute-done((bf16[208,384]{1,0:T(8,128)(2,1)S(1)}, bf16[208,384]{1,0:T(8,128)(2,1)S(1)}, u32[]{:S(2)}, u32[]{:S(2)}) %collective-permute-start.37) | collective-permute-done | bytes 159776 | tf_op jit(solution)/shard_map/ppermute | solution.py:393
  422.5 1.7 convert_add_fusion.2
  430.4 1.7 convert_element_type.349
  (341 shorter events, 106.0 us)
Async XLA Ops:
  9.1 52.3 %collective-permute-start.4 = (bf16[224,3072]{1,0:T(8,128)(2,1)}, bf16[224,3072]{1,0:T(8,128)(2,1)}, u32[]{:S(2)}, u32[]{:S(2)}) collective-permute-start(bf16[224,3072]{1,0:T(8,128)(2,1)} %fusion.17.refs_0_), channel_id=1, source_target_pairs={{0,1},{1,0},{2,3},{3,2},{4,5},{5,4},{6,7},{7,6},{8,9},{9,8},{10,11... | collective-permute-start | bytes 4128776 | tf_op jit(solution)/shard_map/ppermute | solution.py:393
  12.1 51.1 %collective-permute-start.5 = (bf16[224,3072]{1,0:T(8,128)(2,1)}, bf16[224,3072]{1,0:T(8,128)(2,1)}, u32[]{:S(2)}, u32[]{:S(2)}) collective-permute-start(bf16[224,3072]{1,0:T(8,128)(2,1)} %fusion.17.refs_0_), channel_id=1, source_target_pairs={{0,2},{1,3},{2,0},{3,1},{4,6},{5,7},{6,4},{7,5},{8,10},{9,11},{10,... | collective-permute-start | bytes 4128776 | tf_op jit(solution)/shard_map/ppermute | solution.py:393
  13.8 25.7 %collective-permute-start = (bf16[2,192,768]{2,1,0:T(8,128)(2,1)S(1)}, bf16[2,192,768]{2,1,0:T(8,128)(2,1)}, u32[]{:S(2)}, u32[]{:S(2)}) collective-permute-start(bf16[2,192,768]{2,1,0:T(8,128)(2,1)S(1)} %pad_maximum_fusion), channel_id=1, source_target_pairs={{0,8},{4,12},{8,0},{12,4},{16,24},{20,28},{24,16},{28,20},{1,9},{5... | collective-permute-start | bytes 1769480 | tf_op jit(solution)/shard_map/ppermute | solution.py:393
  16.3 42.8 %collective-permute-start.1 = (bf16[2,192,768]{2,1,0:T(8,128)(2,1)}, bf16[2,192,768]{2,1,0:T(8,128)(2,1)}, u32[]{:S(2)}, u32[]{:S(2)}) collective-permute-start(bf16[2,192,768]{2,1,0:T(8,128)(2,1)} %pad_maximum_fusion.1), channel_id=1, source_target_pairs={{0,16},{4,20},{8,24},{12,28},{16,0},{20,4},{24,8},{28,12},{1,17},{... | collective-permute-start | bytes 1769480 | tf_op jit(solution)/shard_map/ppermute | solution.py:393
  19.8 40.4 %collective-permute-start.2 = (bf16[2,192,768]{2,1,0:T(8,128)(2,1)}, bf16[2,192,768]{2,1,0:T(8,128)(2,1)}, u32[]{:S(2)}, u32[]{:S(2)}) collective-permute-start(bf16[2,192,768]{2,1,0:T(8,128)(2,1)} %pad_maximum_fusion.2), channel_id=1, source_target_pairs={{0,24},{4,28},{8,16},{12,20},{16,8},{20,12},{24,0},{28,4},{1,25},{... | collective-permute-start | bytes 1769480 | tf_op jit(solution)/shard_map/ppermute | solution.py:393
  61.3 49.8 %collective-permute-start.3 = (bf16[4,2,192,768]{3,2,0,1:T(8,128)(2,1)S(1)}, bf16[4,2,192,768]{3,2,0,1:T(8,128)(2,1)}, u32[]{:S(2)}, u32[]{:S(2)}) collective-permute-start(bf16[4,2,192,768]{3,2,0,1:T(8,128)(2,1)S(1)} %bitcast_dynamic-update-slice_fusion), channel_id=1, source_target_pairs={{0,4},{4,0},{8,12},{12,8},{16,20},{20,16},{24,28},{28,24},{1,5},{5... | collective-permute-start | bytes 7077896 | tf_op jit(solution)/shard_map/ppermute | solution.py:393
  62.6 17.9 %collective-permute-start.6 = (bf16[112,3072]{1,0:T(8,128)(2,1)S(1)}, bf16[112,3072]{1,0:T(8,128)(2,1)S(1)}, u32[]{:S(2)}, u32[]{:S(2)}) collective-permute-start(bf16[112,3072]{1,0:T(8,128)(2,1)S(1)} %slice.463), channel_id=1, source_target_pairs={{0,2},{1,3},{2,0},{3,1},{4,6},{5,7},{6,4},{7,5},{8,10},{9,11},{10,... | collective-permute-start | bytes 2064392 | tf_op jit(solution)/shard_map/ppermute | solution.py:393
  64.3 17.6 %collective-permute-start.7 = (bf16[112,3072]{1,0:T(8,128)(2,1)S(1)}, bf16[112,3072]{1,0:T(8,128)(2,1)S(1)}, u32[]{:S(2)}, u32[]{:S(2)}) collective-permute-start(bf16[112,3072]{1,0:T(8,128)(2,1)S(1)} %slice.464), channel_id=1, source_target_pairs={{0,1},{1,0},{2,3},{3,2},{4,5},{5,4},{6,7},{7,6},{8,9},{9,8},{10,11... | collective-permute-start | bytes 2064392 | tf_op jit(solution)/shard_map/ppermute | solution.py:393
  84.9 18.0 %collective-permute-start.8 = (bf16[192,1920]{1,0:T(8,128)(2,1)}, bf16[192,1920]{1,0:T(8,128)(2,1)S(1)}, u32[]{:S(2)}, u32[]{:S(2)}) collective-permute-start(bf16[192,1920]{1,0:T(8,128)(2,1)} %constant_dynamic-update-slice_fusion), channel_id=1, source_target_pairs={{0,1},{1,0},{2,3},{3,2},{4,5},{5,4},{6,7},{7,6},{8,9},{9,8},{10,11... | collective-permute-start | bytes 2211848 | tf_op jit(solution)/shard_map/ppermute | solution.py:393
  85.4 19.7 %collective-permute-start.9 = (bf16[192,1920]{1,0:T(8,128)(2,1)}, bf16[192,1920]{1,0:T(8,128)(2,1)}, u32[]{:S(2)}, u32[]{:S(2)}) collective-permute-start(bf16[192,1920]{1,0:T(8,128)(2,1)} %constant_dynamic-update-slice_fusion), channel_id=1, source_target_pairs={{0,2},{1,3},{2,0},{3,1},{4,6},{5,7},{6,4},{7,5},{8,10},{9,11},{10,... | collective-permute-start | bytes 2211848 | tf_op jit(solution)/shard_map/ppermute | solution.py:393
  103.6 74.5 %collective-permute-start.10 = (bf16[96,1920]{1,0:T(8,128)(2,1)}, bf16[96,1920]{1,0:T(8,128)(2,1)}, u32[]{:S(2)}, u32[]{:S(2)}) collective-permute-start(bf16[96,1920]{1,0:T(8,128)(2,1)} %slice.479), channel_id=1, source_target_pairs={{0,2},{1,3},{2,0},{3,1},{4,6},{5,7},{6,4},{7,5},{8,10},{9,11},{10,... | collective-permute-start | bytes 1105928 | tf_op jit(solution)/shard_map/ppermute | solution.py:393
  106.9 72.8 %collective-permute-start.11 = (bf16[96,1920]{1,0:T(8,128)(2,1)}, bf16[96,1920]{1,0:T(8,128)(2,1)}, u32[]{:S(2)}, u32[]{:S(2)}) collective-permute-start(bf16[96,1920]{1,0:T(8,128)(2,1)} %slice.481), channel_id=1, source_target_pairs={{0,1},{1,0},{2,3},{3,2},{4,5},{5,4},{6,7},{7,6},{8,9},{9,8},{10,11... | collective-permute-start | bytes 1105928 | tf_op jit(solution)/shard_map/ppermute | solution.py:393
  174.6 71.1 %collective-permute-start.12 = (bf16[1,208,3072]{2,1,0:T(8,128)(2,1)}, bf16[1,208,3072]{2,1,0:T(8,128)(2,1)S(1)}, u32[]{:S(2)}, u32[]{:S(2)}) collective-permute-start(bf16[1,208,3072]{2,1,0:T(8,128)(2,1)} %get-tuple-element.116), channel_id=1, source_target_pairs={{0,1},{1,0},{2,3},{3,2},{4,5},{5,4},{6,7},{7,6},{8,9},{9,8},{10,11... | collective-permute-start | bytes 3833864 | tf_op jit(solution)/shard_map/ppermute | solution.py:393
  176.1 69.7 %collective-permute-start.13 = (bf16[1,208,3072]{2,1,0:T(8,128)(2,1)}, bf16[1,208,3072]{2,1,0:T(8,128)(2,1)S(1)}, u32[]{:S(2)}, u32[]{:S(2)}) collective-permute-start(bf16[1,208,3072]{2,1,0:T(8,128)(2,1)} %get-tuple-element.115), channel_id=1, source_target_pairs={{0,2},{1,3},{2,0},{3,1},{4,6},{5,7},{6,4},{7,5},{8,10},{9,11},{10,... | collective-permute-start | bytes 3833864 | tf_op jit(solution)/shard_map/ppermute | solution.py:393
  176.6 69.2 %collective-permute-start.14 = (bf16[1,208,3072]{2,1,0:T(8,128)(2,1)}, bf16[1,208,3072]{2,1,0:T(8,128)(2,1)}, u32[]{:S(2)}, u32[]{:S(2)}) collective-permute-start(bf16[1,208,3072]{2,1,0:T(8,128)(2,1)} %get-tuple-element.114), channel_id=1, source_target_pairs={{0,3},{1,2},{2,1},{3,0},{4,7},{5,6},{6,5},{7,4},{8,11},{9,10},{10,... | collective-permute-start | bytes 3833864 | tf_op jit(solution)/shard_map/ppermute | solution.py:393
  186.5 59.3 %copy-start.8 = (bf16[1,208,3072]{2,1,0:T(8,128)(2,1)S(1)}, bf16[1,208,3072]{2,1,0:T(8,128)(2,1)}, u32[]{:S(2)}) copy-start(bf16[1,208,3072]{2,1,0:T(8,128)(2,1)} %get-tuple-element.75) | copy-start | bytes 3833860
  258.2 51.1 %collective-permute-start.15 = (bf16[1,4,192,768]{3,2,1,0:T(8,128)(2,1)}, bf16[1,4,192,768]{3,2,1,0:T(8,128)(2,1)}, u32[]{:S(2)}, u32[]{:S(2)}) collective-permute-start(bf16[1,4,192,768]{3,2,1,0:T(8,128)(2,1)} %dynamic-slice_bitcast_fusion.1), channel_id=1, source_target_pairs={{0,4},{4,0},{8,12},{12,8},{16,20},{20,16},{24,28},{28,24},{1,5},{5... | collective-permute-start | bytes 3538952 | tf_op jit(solution)/shard_map/ppermute | solution.py:393
  262.6 26.4 %collective-permute-start.16 = (bf16[1,4,192,768]{3,2,1,0:T(8,128)(2,1)}, bf16[1,4,192,768]{3,2,1,0:T(8,128)(2,1)}, u32[]{:S(2)}, u32[]{:S(2)}) collective-permute-start(bf16[1,4,192,768]{3,2,1,0:T(8,128)(2,1)} %dynamic-slice_bitcast_fusion), channel_id=1, source_target_pairs={{0,4},{4,0},{8,12},{12,8},{16,20},{20,16},{24,28},{28,24},{1,5},{5... | collective-permute-start | bytes 3538952 | tf_op jit(solution)/shard_map/ppermute | solution.py:393
  263.7 26.9 %collective-permute-start.17 = (bf16[208,768]{1,0:T(8,128)(2,1)}, bf16[208,768]{1,0:T(8,128)(2,1)}, u32[]{:S(2)}, u32[]{:S(2)}) collective-permute-start(bf16[208,768]{1,0:T(8,128)(2,1)} %get-tuple-element.138), channel_id=1, source_target_pairs={{0,8},{4,12},{8,0},{12,4},{16,24},{20,28},{24,16},{28,20},{1,9},{5... | collective-permute-start | bytes 958472 | tf_op jit(solution)/shard_map/ppermute | solution.py:393
  273.8 25.3 %collective-permute-start.18 = (bf16[208,768]{1,0:T(8,128)(2,1)}, bf16[208,768]{1,0:T(8,128)(2,1)}, u32[]{:S(2)}, u32[]{:S(2)}) collective-permute-start(bf16[208,768]{1,0:T(8,128)(2,1)} %get-tuple-element.137), channel_id=1, source_target_pairs={{0,16},{4,20},{8,24},{12,28},{16,0},{20,4},{24,8},{28,12},{1,17},{... | collective-permute-start | bytes 958472 | tf_op jit(solution)/shard_map/ppermute | solution.py:393
  274.8 24.3 %collective-permute-start.19 = (bf16[208,768]{1,0:T(8,128)(2,1)}, bf16[208,768]{1,0:T(8,128)(2,1)}, u32[]{:S(2)}, u32[]{:S(2)}) collective-permute-start(bf16[208,768]{1,0:T(8,128)(2,1)} %get-tuple-element.136), channel_id=1, source_target_pairs={{0,24},{4,28},{8,16},{12,20},{16,8},{20,12},{24,0},{28,4},{1,25},{... | collective-permute-start | bytes 958472 | tf_op jit(solution)/shard_map/ppermute | solution.py:393
  280.9 8.1 %copy-start.3 = (bf16[1536,768]{1,0:T(8,128)(2,1)S(1)}, bf16[1536,768]{1,0:T(8,128)(2,1)}, u32[]{:S(2)}) copy-start(bf16[1536,768]{1,0:T(8,128)(2,1)} %copy-done.2) | copy-start | bytes 7077892
  289.0 22.5 %collective-permute-start.26 = (bf16[1536,384]{1,0:T(8,128)(2,1)S(1)}, bf16[1536,384]{1,0:T(8,128)(2,1)S(1)}, u32[]{:S(2)}, u32[]{:S(2)}) collective-permute-start(bf16[1536,384]{1,0:T(8,128)(2,1)S(1)} %copy-done.4), channel_id=1, source_target_pairs={{0,4},{4,0},{8,12},{12,8},{16,20},{20,16},{24,28},{28,24},{1,5},{5... | collective-permute-start | bytes 3538952 | tf_op jit(solution)/shard_map/ppermute | solution.py:393
  290.6 18.7 %copy-start.6 = (bf16[1536,768]{1,0:T(8,128)(2,1)S(1)}, bf16[1536,768]{1,0:T(8,128)(2,1)}, u32[]{:S(2)}) copy-start(bf16[1536,768]{1,0:T(8,128)(2,1)} %copy-done.5) | copy-start | bytes 7077892
  300.2 28.1 %collective-permute-start.20 = (bf16[1,192,768]{2,1,0:T(8,128)(2,1)}, bf16[1,192,768]{2,1,0:T(8,128)(2,1)}, u32[]{:S(2)}, u32[]{:S(2)}) collective-permute-start(bf16[1,192,768]{2,1,0:T(8,128)(2,1)} %get-tuple-element.146), channel_id=1, source_target_pairs={{0,8},{4,12},{8,0},{12,4},{16,24},{20,28},{24,16},{28,20},{1,9},{5... | collective-permute-start | bytes 884744 | tf_op jit(solution)/shard_map/ppermute | solution.py:393
  306.8 23.8 %collective-permute-start.21 = (bf16[1,192,768]{2,1,0:T(8,128)(2,1)}, bf16[1,192,768]{2,1,0:T(8,128)(2,1)}, u32[]{:S(2)}, u32[]{:S(2)}) collective-permute-start(bf16[1,192,768]{2,1,0:T(8,128)(2,1)} %get-tuple-element.145), channel_id=1, source_target_pairs={{0,16},{4,20},{8,24},{12,28},{16,0},{20,4},{24,8},{28,12},{1,17},{... | collective-permute-start | bytes 884744 | tf_op jit(solution)/shard_map/ppermute | solution.py:393
  307.9 22.8 %collective-permute-start.22 = (bf16[1,192,768]{2,1,0:T(8,128)(2,1)}, bf16[1,192,768]{2,1,0:T(8,128)(2,1)}, u32[]{:S(2)}, u32[]{:S(2)}) collective-permute-start(bf16[1,192,768]{2,1,0:T(8,128)(2,1)} %get-tuple-element.144), channel_id=1, source_target_pairs={{0,24},{4,28},{8,16},{12,20},{16,8},{20,12},{24,0},{28,4},{1,25},{... | collective-permute-start | bytes 884744 | tf_op jit(solution)/shard_map/ppermute | solution.py:393
  321.9 42.2 %collective-permute-start.29 = (bf16[1,208,1536]{2,1,0:T(8,128)(2,1)S(1)}, bf16[1,208,1536]{2,1,0:T(8,128)(2,1)S(1)}, u32[]{:S(2)}, u32[]{:S(2)}) collective-permute-start(bf16[1,208,1536]{2,1,0:T(8,128)(2,1)S(1)} %get-tuple-element.126), channel_id=1, source_target_pairs={{0,3},{1,2},{2,1},{3,0},{4,7},{5,6},{6,5},{7,4},{8,11},{9,10},{10,... | collective-permute-start | bytes 1916936 | tf_op jit(solution)/shard_map/ppermute | solution.py:393
  323.4 42.2 %collective-permute-start.28 = (bf16[1,208,1536]{2,1,0:T(8,128)(2,1)S(1)}, bf16[1,208,1536]{2,1,0:T(8,128)(2,1)S(1)}, u32[]{:S(2)}, u32[]{:S(2)}) collective-permute-start(bf16[1,208,1536]{2,1,0:T(8,128)(2,1)S(1)} %get-tuple-element.127), channel_id=1, source_target_pairs={{0,2},{1,3},{2,0},{3,1},{4,6},{5,7},{6,4},{7,5},{8,10},{9,11},{10,... | collective-permute-start | bytes 1916936 | tf_op jit(solution)/shard_map/ppermute | solution.py:393
  328.3 37.2 %collective-permute-start.27 = (bf16[1,208,1536]{2,1,0:T(8,128)(2,1)S(1)}, bf16[1,208,1536]{2,1,0:T(8,128)(2,1)S(1)}, u32[]{:S(2)}, u32[]{:S(2)}) collective-permute-start(bf16[1,208,1536]{2,1,0:T(8,128)(2,1)S(1)} %get-tuple-element.125), channel_id=1, source_target_pairs={{0,1},{1,0},{2,3},{3,2},{4,5},{5,4},{6,7},{7,6},{8,9},{9,8},{10,11... | collective-permute-start | bytes 1916936 | tf_op jit(solution)/shard_map/ppermute | solution.py:393
  330.7 16.2 %collective-permute-start.23 = (bf16[1,192,768]{2,1,0:T(8,128)(2,1)S(1)}, bf16[1,192,768]{2,1,0:T(8,128)(2,1)S(1)}, u32[]{:S(2)}, u32[]{:S(2)}) collective-permute-start(bf16[1,192,768]{2,1,0:T(8,128)(2,1)S(1)} %get-tuple-element.142), channel_id=1, source_target_pairs={{0,8},{4,12},{8,0},{12,4},{16,24},{20,28},{24,16},{28,20},{1,9},{5... | collective-permute-start | bytes 884744 | tf_op jit(solution)/shard_map/ppermute | solution.py:393
  335.8 21.4 %collective-permute-start.24 = (bf16[1,192,768]{2,1,0:T(8,128)(2,1)S(1)}, bf16[1,192,768]{2,1,0:T(8,128)(2,1)S(1)}, u32[]{:S(2)}, u32[]{:S(2)}) collective-permute-start(bf16[1,192,768]{2,1,0:T(8,128)(2,1)S(1)} %get-tuple-element.141), channel_id=1, source_target_pairs={{0,16},{4,20},{8,24},{12,28},{16,0},{20,4},{24,8},{28,12},{1,17},{... | collective-permute-start | bytes 884744 | tf_op jit(solution)/shard_map/ppermute | solution.py:393
  336.9 11.3 %copy-start.10 = (bf16[4,192,768]{2,1,0:T(8,128)(2,1)S(1)}, bf16[4,192,768]{2,1,0:T(8,128)(2,1)}, u32[]{:S(2)}) copy-start(bf16[4,192,768]{2,1,0:T(8,128)(2,1)} %param.17) | copy-start | bytes 3538948
  337.0 11.3 %copy-start.28 = (f32[768]{0:T(1024)S(1)}, f32[768]{0:T(1024)}, u32[]{:S(2)}) copy-start(f32[768]{0:T(1024)} %reshape.362) | copy-start | bytes 9220
  337.0 11.3 %copy-start.29 = (f32[768]{0:T(1024)S(1)}, f32[768]{0:T(1024)}, u32[]{:S(2)}) copy-start(f32[768]{0:T(1024)} %reshape.361) | copy-start | bytes 9220
  346.9 10.3 %collective-permute-start.25 = (bf16[1,192,768]{2,1,0:T(8,128)(2,1)S(1)}, bf16[1,192,768]{2,1,0:T(8,128)(2,1)S(1)}, u32[]{:S(2)}, u32[]{:S(2)}) collective-permute-start(bf16[1,192,768]{2,1,0:T(8,128)(2,1)S(1)} %get-tuple-element.140), channel_id=1, source_target_pairs={{0,24},{4,28},{8,16},{12,20},{16,8},{20,12},{24,0},{28,4},{1,25},{... | collective-permute-start | bytes 884744 | tf_op jit(solution)/shard_map/ppermute | solution.py:393
  357.2 18.0 %collective-permute-start.30 = (bf16[208,768]{1,0:T(8,128)(2,1)S(1)}, bf16[208,768]{1,0:T(8,128)(2,1)S(1)}, u32[]{:S(2)}, u32[]{:S(2)}) collective-permute-start(bf16[208,768]{1,0:T(8,128)(2,1)S(1)} %add_convert_fusion.5), channel_id=1, source_target_pairs={{0,8},{4,12},{8,0},{12,4},{16,24},{20,28},{24,16},{28,20},{1,9},{5... | collective-permute-start | bytes 958472 | tf_op jit(solution)/shard_map/ppermute | solution.py:393
  363.1 26.8 %collective-permute-start.31 = (bf16[208,768]{1,0:T(8,128)(2,1)S(1)}, bf16[208,768]{1,0:T(8,128)(2,1)S(1)}, u32[]{:S(2)}, u32[]{:S(2)}) collective-permute-start(bf16[208,768]{1,0:T(8,128)(2,1)S(1)} %add_convert_fusion.5), channel_id=1, source_target_pairs={{0,16},{4,20},{8,24},{12,28},{16,0},{20,4},{24,8},{28,12},{1,17},{... | collective-permute-start | bytes 958472 | tf_op jit(solution)/shard_map/ppermute | solution.py:393
  364.1 25.8 %collective-permute-start.32 = (bf16[208,768]{1,0:T(8,128)(2,1)S(1)}, bf16[208,768]{1,0:T(8,128)(2,1)S(1)}, u32[]{:S(2)}, u32[]{:S(2)}) collective-permute-start(bf16[208,768]{1,0:T(8,128)(2,1)S(1)} %add_convert_fusion.5), channel_id=1, source_target_pairs={{0,24},{4,28},{8,16},{12,20},{16,8},{20,12},{24,0},{28,4},{1,25},{... | collective-permute-start | bytes 958472 | tf_op jit(solution)/shard_map/ppermute | solution.py:393
  389.9 8.1 %collective-permute-start.35 = (bf16[208,384]{1,0:T(8,128)(2,1)S(1)}, bf16[208,384]{1,0:T(8,128)(2,1)S(1)}, u32[]{:S(2)}, u32[]{:S(2)}) collective-permute-start(bf16[208,384]{1,0:T(8,128)(2,1)S(1)} %get-tuple-element.170), channel_id=1, source_target_pairs={{0,24},{4,28},{8,16},{12,20},{16,8},{20,12},{24,0},{28,4},{1,25},{... | collective-permute-start | bytes 479240 | tf_op jit(solution)/shard_map/ppermute | solution.py:393
  392.4 14.8 %collective-permute-start.34 = (bf16[208,384]{1,0:T(8,128)(2,1)S(1)}, bf16[208,384]{1,0:T(8,128)(2,1)S(1)}, u32[]{:S(2)}, u32[]{:S(2)}) collective-permute-start(bf16[208,384]{1,0:T(8,128)(2,1)S(1)} %get-tuple-element.171), channel_id=1, source_target_pairs={{0,16},{4,20},{8,24},{12,28},{16,0},{20,4},{24,8},{28,12},{1,17},{... | collective-permute-start | bytes 479240 | tf_op jit(solution)/shard_map/ppermute | solution.py:393
  396.7 10.5 %collective-permute-start.33 = (bf16[208,384]{1,0:T(8,128)(2,1)S(1)}, bf16[208,384]{1,0:T(8,128)(2,1)S(1)}, u32[]{:S(2)}, u32[]{:S(2)}) collective-permute-start(bf16[208,384]{1,0:T(8,128)(2,1)S(1)} %get-tuple-element.169), channel_id=1, source_target_pairs={{0,8},{4,12},{8,0},{12,4},{16,24},{20,28},{24,16},{28,20},{1,9},{5... | collective-permute-start | bytes 479240 | tf_op jit(solution)/shard_map/ppermute | solution.py:393
  407.4 15.1 %copy-start.12 = (bf16[4,192,768]{2,1,0:T(8,128)(2,1)S(1)}, bf16[4,192,768]{2,1,0:T(8,128)(2,1)}, u32[]{:S(2)}) copy-start(bf16[4,192,768]{2,1,0:T(8,128)(2,1)} %param.19) | copy-start | bytes 3538948
  407.4 7.5 %collective-permute-start.36 = (bf16[208,384]{1,0:T(8,128)(2,1)S(1)}, bf16[208,384]{1,0:T(8,128)(2,1)S(1)}, u32[]{:S(2)}, u32[]{:S(2)}) collective-permute-start(bf16[208,384]{1,0:T(8,128)(2,1)S(1)} %get-tuple-element.113), channel_id=1, source_target_pairs={{0,8},{4,12},{8,0},{12,4},{16,24},{20,28},{24,16},{28,20},{1,9},{5... | collective-permute-start | bytes 479240 | tf_op jit(solution)/shard_map/ppermute | solution.py:393
  407.5 14.8 %collective-permute-start.37 = (bf16[208,384]{1,0:T(8,128)(2,1)S(1)}, bf16[208,384]{1,0:T(8,128)(2,1)S(1)}, u32[]{:S(2)}, u32[]{:S(2)}) collective-permute-start(bf16[208,384]{1,0:T(8,128)(2,1)S(1)} %get-tuple-element.113), channel_id=1, source_target_pairs={{0,16},{4,20},{8,24},{12,28},{16,0},{20,4},{24,8},{28,12},{1,17},{... | collective-permute-start | bytes 479240 | tf_op jit(solution)/shard_map/ppermute | solution.py:393
  409.3 13.0 %collective-permute-start.38 = (bf16[208,384]{1,0:T(8,128)(2,1)S(1)}, bf16[208,384]{1,0:T(8,128)(2,1)S(1)}, u32[]{:S(2)}, u32[]{:S(2)}) collective-permute-start(bf16[208,384]{1,0:T(8,128)(2,1)S(1)} %get-tuple-element.113), channel_id=1, source_target_pairs={{0,24},{4,28},{8,16},{12,20},{16,8},{20,12},{24,0},{28,4},{1,25},{... | collective-permute-start | bytes 479240 | tf_op jit(solution)/shard_map/ppermute | solution.py:393
  422.4 2.6 collective-permute-start.39
  424.4 4.6 %collective-permute-start.40 = (bf16[208,3072]{1,0:T(8,128)(2,1)S(1)}, bf16[208,3072]{1,0:T(8,128)(2,1)S(1)}, u32[]{:S(2)}, u32[]{:S(2)}) collective-permute-start(bf16[208,3072]{1,0:T(8,128)(2,1)S(1)} %constant_dynamic-update-slice_fusion.37), channel_id=1, source_target_pairs={{0,4},{4,0},{8,12},{12,8},{16,20},{20,16},{24,28},{28,24},{1,5},{5... | collective-permute-start | bytes 3833864 | tf_op jit(solution)/shard_map/ppermute | solution.py:393
  (34 other events, 114.1 us)

commit v3 on v2

--- a/solution.py
+++ b/solution.py
@@ -35,34 +35,51 @@
 
 
 def attention_kernel(
-    length_ref,
+    scalar_ref,
     attn_in_ref,
     cot_ref,
-    w_ref,
     bias_ref,
-    out_w_ref,
     cos_ref,
     sin_ref,
-    mixed_ref,
-    dproj_ref,
-    q_s,
-    k_a,
-    k_b,
-    v_a,
-    v_b,
-    kt_a,
-    kt_b,
-    vt_a,
-    vt_b,
-    do_s,
-    dk_s,
-    dv_s,
-    *,
+    *refs,
     seq_len,
     rows,
     groups,
+    fsdp,
+    lanes,
 ):
-    live = length_ref[0]
+    pieces, refs = refs[:fsdp], refs[fsdp:]
+    mixed_ref, dproj_ref, w_s, out_w_s, sems = refs[:5]
+    scratch = refs[5:]
+    q_s, k_a, k_b, v_a, v_b, kt_a, kt_b, vt_a, vt_b, do_s, dk_s, dv_s = scratch
+    pair = pl.program_id(0)
+    own_rows = D // fsdp
+    width = w_s.shape[1]
+
+    @pl.when(pair == 0)
+    def _():
+        out_w_s[D:, :] = jnp.zeros((128, D), bf16)
+        copies = []
+        for k in range(fsdp):
+            at = pl.ds(pl.multiple_of((scalar_ref[1] ^ k) * own_rows, own_rows), own_rows)
+            copies.append(
+                pltpu.make_async_copy(
+                    pieces[k].at[:, pl.ds(0, width)], w_s.at[at, :], sems.at[k, 0]
+                )
+            )
+            copies.append(
+                pltpu.make_async_copy(
+                    pieces[k].at[:, pl.ds(width, D)], out_w_s.at[at, :], sems.at[k, 1]
+                )
+            )
+        for copy in copies:
+            copy.start()
+        for copy in copies:
+            copy.wait()
+
+    w_cols = pl.ds(pl.multiple_of(pair * 384, 128), 384)
+    out_rows = pl.ds(pl.multiple_of(scalar_ref[2] * lanes + pair * 128, HEAD_DIM), 128)
+    live = scalar_ref[0]
     lane = lax.broadcasted_iota(jnp.int32, (rows, 128), 1)
     low = lane < HEAD_DIM
     first_half = lane % HEAD_DIM < ROTARY // 2
@@ -76,7 +93,7 @@
     def project(j, carry):
         start = pl.multiple_of(j * rows, rows)
         span = pl.ds(start, rows)
-        proj = dot(attn_in_ref[span, :], w_ref[...]) + bias_ref[...]
+        proj = dot(attn_in_ref[span, :], w_s[:, w_cols]) + bias_ref[...]
         q_s[span, :] = (rope(proj[:, :128], span, False) * (score_scale * log2_e)).astype(bf16)
         keys = rope(proj[:, 128:256], span, False)
         values = proj[:, 256:]
@@ -94,7 +111,7 @@
         ):
             plain[span, :] = src.astype(bf16)
             turned[:, span] = src.T.astype(bf16)
-        do_s[span, :] = dot(cot_ref[span, :], out_w_ref[...], NT)
+        do_s[span, :] = dot(cot_ref[span, :], out_w_s[out_rows, :], NT)
         return carry
 
     lax.fori_loop(0, seq_len // rows, project, 0)
@@ -194,9 +211,11 @@
     lax.fori_loop(0, seq_len // rows, finish, 0)
 
 
-def attention(length, attn_in, cot, w, bias, out_w, cos, sin):
+def attention(scalars, attn_in, cot, pieces, bias, cos, sin, lanes):
     seq_len = attn_in.shape[0]
-    pairs = w.shape[1] // 384
+    fsdp = len(pieces)
+    width = bias.shape[1]
+    pairs = width // 384
     rows = 256
     groups = 6
     whole = functools.partial(pl.BlockSpec, pipeline_mode=pl.Buffered(1))
@@ -205,18 +224,19 @@
     wide = pltpu.VMEM((seq_len, 128), f32)
     flops = pairs * seq_len * (2 * D * 512 + 12 * 128 * seq_len)
     return pl.pallas_call(
-        functools.partial(attention_kernel, seq_len=seq_len, rows=rows, groups=groups),
+        functools.partial(
+            attention_kernel, seq_len=seq_len, rows=rows, groups=groups, fsdp=fsdp, lanes=lanes
+        ),
         grid=(pairs,),
         in_specs=[
             pl.BlockSpec(memory_space=pltpu.SMEM),
             whole((seq_len, D), lambda p: (0, 0)),
             whole((seq_len, D), lambda p: (0, 0)),
-            pl.BlockSpec((D, 384), lambda p: (0, p)),
             pl.BlockSpec((1, 384), lambda p: (0, p)),
-            pl.BlockSpec((128, D), lambda p: (p, 0)),
             whole((seq_len, 128), lambda p: (0, 0)),
             whole((seq_len, 128), lambda p: (0, 0)),
-        ],
+        ]
+        + [pl.BlockSpec(memory_space=pl.ANY)] * fsdp,
         out_specs=[
             pl.BlockSpec((seq_len, 128), lambda p: (0, p)),
             pl.BlockSpec((seq_len, 384), lambda p: (0, p)),
@@ -225,13 +245,18 @@
             jax.ShapeDtypeStruct((seq_len, pairs * 128), bf16),
             jax.ShapeDtypeStruct((seq_len, pairs * 384), bf16),
         ],
-        scratch_shapes=[small] * 5 + [turned] * 4 + [wide] * 3,
+        scratch_shapes=[
+            pltpu.VMEM((D, width), bf16),
+            pltpu.VMEM((D + 128, D), bf16),
+            pltpu.SemaphoreType.DMA((fsdp, 2)),
+        ]
+        + [small] * 5 + [turned] * 4 + [wide] * 3,
         compiler_params=pltpu.CompilerParams(vmem_limit_bytes=58 * 1024 * 1024),
         cost_estimate=pl.CostEstimate(
             flops=flops, bytes_accessed=12_000_000, transcendentals=pairs * seq_len * seq_len
         ),
         name="attention",
-    )(length, attn_in, cot, w, bias, out_w, cos, sin)
+    )(scalars, attn_in, cot, bias, cos, sin, *pieces)
 
 
 def mlp_kernel(
@@ -248,8 +273,10 @@
     chunk,
 ):
     pieces = refs[: len(layout)]
-    attn_in_ref, out_ref, grad_in_ref, grads_ref, vec_ref = refs[len(layout) : len(layout) + 5]
-    mlp_in, mlp_in_t, w_up, w_down, sems = refs[len(layout) + 5 :]
+    refs = refs[len(layout) :]
+    attn_in_ref, out_ref, grad_in_ref = refs[:3]
+    packed_refs = refs[3 : 3 + fsdp]
+    mlp_in, mlp_in_t, w_up, w_down, grads_ref, vec_ref, sems, out_sems = refs[3 + fsdp :]
     seq_len = rows_ref.shape[0]
     up_width = fsdp * unit
     folds = unit // own_rows
@@ -334,9 +361,26 @@
 
     none = jnp.zeros((1, D), f32)
     gain_sum, shift_sum = lax.fori_loop(0, seq_len // rows, sums, (none, none))
-    vec_ref[1:2, :D] = gain_sum
-    vec_ref[2:3, :D] = shift_sum
-    vec_ref[3:4, :D] = cot_sum
+    row = lax.broadcasted_iota(jnp.int32, (16, D), 0)
+    vectors = jnp.where(row == 1, gain_sum, 0.0)
+    vectors = jnp.where(row == 2, shift_sum, vectors)
+    vectors = jnp.where(row == 3, cot_sum, vectors).astype(bf16)
+    row = lax.broadcasted_iota(jnp.int32, (16, unit), 0)
+    for j in range(fsdp):
+        grads_ref[j, own_rows:, :] = jnp.zeros((16, grads_ref.shape[2]), bf16)
+        grads_ref[j, own_rows:, :D] = vectors
+        bias = jnp.where(row == 0, vec_ref[0:1, j * unit : (j + 1) * unit], 0.0)
+        grads_ref[j, own_rows:, D : D + unit] = bias.astype(bf16)
+    copies = [
+        pltpu.make_async_copy(
+            grads_ref.at[pl.ds(shard_ref[0] ^ k, 1)], packed_refs[k], out_sems.at[k]
+        )
+        for k in range(fsdp)
+    ]
+    for copy in copies:
+        copy.start()
+    for copy in copies:
+        copy.wait()
 
 
 def mlp(shard, rows_in, cot, affine, bias, got, fsdp, unit):
@@ -355,20 +399,22 @@
         in_specs=[pl.BlockSpec(memory_space=pltpu.SMEM)]
         + [vmem] * 4
         + [pl.BlockSpec(memory_space=pl.ANY)] * len(pieces),
-        out_specs=[vmem] * 5,
+        out_specs=[vmem] * 3 + [pl.BlockSpec(memory_space=pl.ANY)] * fsdp,
         out_shape=[
             jax.ShapeDtypeStruct((seq_len, D), bf16),
             jax.ShapeDtypeStruct((seq_len, D), f32),
             jax.ShapeDtypeStruct((seq_len, D), f32),
-            jax.ShapeDtypeStruct((fsdp, own_rows + 16, packed_width), bf16),
-            jax.ShapeDtypeStruct((8, up_width), f32),
-        ],
+        ]
+        + [jax.ShapeDtypeStruct((1, own_rows + 16, packed_width), bf16)] * fsdp,
         scratch_shapes=[
             pltpu.VMEM((seq_len, D), bf16),
             pltpu.VMEM((D, seq_len), bf16),
             pltpu.VMEM((D, up_width), bf16),
             pltpu.VMEM((up_width, D), bf16),
+            pltpu.VMEM((fsdp, own_rows + 16, packed_width), bf16),
+            pltpu.VMEM((8, up_width), f32),
             pltpu.SemaphoreType.DMA((len(pieces), 1 + unit // own_rows)),
+            pltpu.SemaphoreType.DMA((fsdp,)),
         ],
         compiler_params=pltpu.CompilerParams(vmem_limit_bytes=58 * 1024 * 1024),
         cost_estimate=pl.CostEstimate(
@@ -405,17 +451,7 @@
 
 def gather_rows(x, group):
     axis, n, step, _ = group
-    if n != 4:
-        return [(k, 0, swap(x, axis, k * step) if k else x) for k in range(n)]
-    one, two = swap(x, axis, step), swap(x, axis, 2 * step)
-    half = x.shape[0] // 2
-    return [
-        (0, 0, x),
-        (1, 0, one),
-        (2, 0, two),
-        (3, 0, swap(one[:half], axis, 2 * step)),
-        (3, half, swap(two[half:], axis, step)),
-    ]
+    return [(k, 0, swap(x, axis, k * step) if k else x) for k in range(n)]
 
 
 def stacked(pieces):
@@ -544,13 +580,6 @@
         bounds.append(packed[:, at : at + v.shape[0]].reshape(-1).astype(f32))
         at += v.shape[0]
     full_qkv_b, full_out_b, full_up_b, full_down_b, gain_a, shift_a, gain_m, shift_m = bounds
-    w_qkv = jnp.zeros((D, qkv_width), bf16)
-    w_out = jnp.zeros((D, D), bf16)
-    for k, first, piece in attn_got:
-        at = (shard ^ k) * own_rows + first
-        w_qkv = lax.dynamic_update_slice(w_qkv, piece[:, :qkv_width], (at, 0))
-        w_out = lax.dynamic_update_slice(w_out, piece[:, qkv_width:], (at, 0))
-    w_out_rows = jnp.pad(take(w_out, seat, lanes), ((0, spare), (0, 0)))
     b_qkv = by_pair(full_qkv_b[None])
     b_up = up_columns(full_up_b[None])
 
@@ -563,17 +592,19 @@
     def columns(x):
         return jnp.sum(x, 0)
 
-    def vector_row(parts, size):
-        row = jnp.concatenate([v.reshape(fsdp, -1) for v in parts], 1)
-        row = jnp.pad(row, ((0, 0), (0, size - row.shape[1])))[:, None]
-        return jnp.pad(row, ((0, 0), (0, 15), (0, 0))).astype(bf16)
+    def vector_rows(rows, size):
+        out = []
+        for at, v in rows:
+            v = jnp.broadcast_to(v, (fsdp, v.shape[-1])).astype(bf16)
+            out.append(jnp.pad(v, ((0, 0), (at, size - at - v.shape[1])))[:, None])
+        return jnp.pad(jnp.concatenate(out, 1), ((0, 0), (0, 16 - len(rows)), (0, 0)))
 
     normed, _ = normalise(rows_in)
     if seq_len <= 2048:
         affine = jnp.concatenate(
             [gain_a[None], shift_a[None], gain_m[None], shift_m[None], jnp.zeros((4, D), f32)]
         )
-        attn_in, mlp_out, grad_mlp_in, mlp_grads, sums = mlp(
+        attn_in, mlp_out, grad_mlp_in, *mlp_grads = mlp(
             shard.reshape(1).astype(jnp.int32),
             rows_in,
             cot,
@@ -583,10 +614,6 @@
             fsdp,
             unit,
         )
-        row = vector_row(
-            [sums[0], sums[1, :D], sums[2, :D], sums[3, :D] * (1.0 / team)], mlp_width
-        )
-        mlp_grads = lax.dynamic_update_slice(mlp_grads, row, (0, own_rows, 0))
     else:
         w_up = jnp.zeros((D, up_width), bf16)
         w_down = jnp.zeros((fsdp, folds, own_rows, D), bf16)
@@ -609,7 +636,6 @@
         mlp_out = dot(hidden, w_down)
         grad_mlp_in = dot(grad_pre, w_up, NT)
 
-        cot_sum = columns(cot.astype(f32)) * (1.0 / team)
         mlp_grads = jnp.concatenate(
             [up_grad.astype(bf16).reshape(fsdp, own_rows, up_width)]
             + [
@@ -617,53 +643,67 @@
             ],
             2,
         )
-        mlp_grads = jnp.concatenate(
+        rows = vector_rows(
             [
-                mlp_grads,
-                vector_row(
-                    [
-                        columns(grad_pre.astype(f32)),
-                        columns(grad_mlp_in * normed),
-                        columns(grad_mlp_in),
-                        cot_sum,
-                    ],
-                    mlp_width,
-                ),
+                (D, columns(grad_pre.astype(f32)).reshape(fsdp, unit)),
+                (0, columns(grad_mlp_in * normed)),
+                (0, columns(grad_mlp_in)),
+                (0, columns(cot.astype(f32))),
             ],
-            1,
+            mlp_width,
         )
-
-    def spread(mine):
+        mlp_grads = jnp.concatenate([mlp_grads, rows], 1)
+        mlp_grads = [take(mlp_grads, shard ^ k, 1) for k in range(fsdp)]
+
+    def halve(mine):
         cols = mine.shape[1] // seqs
-        return [
-            (s, swap(take(mine, seq ^ s, cols, 1), "ctx", s * team) if s else take(mine, seq, cols, 1))
-            for s in range(seqs)
-        ]
-
-    def joined_columns(pieces):
-        rows, cols = pieces[0][1].shape
+        block = [take(mine, seq ^ k, cols, 1) for k in range(seqs)]
+        got = swap(jnp.stack([block[1], block[3]]), "ctx", team)
+        return block[0], block[2], got
+
+    def quarter(own, far, got):
+        own = own.astype(f32) + got[0].astype(f32)
+        far = far.astype(f32) + got[1].astype(f32)
+        return (own + swap(far.astype(bf16), "ctx", 2 * team).astype(f32)).astype(bf16)
+
+    def widen(part):
+        return jnp.stack([part, swap(part, "ctx", 2 * team)])
+
+    def whole_again(two):
+        got = swap(two, "ctx", team)
+        rows, cols = two.shape[1:]
         whole = jnp.zeros((rows, seqs * cols), bf16)
-        for j, piece in pieces:
-            whole = place(whole, piece, j, 1)
+        for k, piece in ((0, two[0]), (2, two[1]), (1, got[0]), (3, got[1])):
+            whole = place(whole, piece, seq ^ k, 1)
         return stacked(gather(whole, team_group))
 
-    def summed(parts):
-        return sum(part.astype(f32) for _, part in parts).astype(bf16)
-
-    attn_in, cot_held, mlp_grads = lax.optimization_barrier((attn_in, cot, mlp_grads))
-    mlp_pieces = exchange(mlp_grads, fsdp_group)
-    length = lax.dynamic_slice_in_dim(lengths, seq, 1, 0)
+    attn_in, cot_held, mlp_grads, attn_got = lax.optimization_barrier(
+        (attn_in, cot, list(mlp_grads), [piece for _, _, piece in attn_got])
+    )
+    mlp_pieces = [
+        (shard ^ k, swap(x, "fsdp", k) if k else x) for k, x in enumerate(mlp_grads)
+    ]
+    scalars = jnp.stack([lax.dynamic_index_in_dim(lengths, seq, 0, False), shard, seat])
     mixed, grad_proj = attention(
-        length, attn_in, cot_held, w_qkv, b_qkv, w_out_rows, *rope_tables(seq_len)
-    )
-    (mixed, grad_proj), mlp_pieces = after((mixed, grad_proj), mlp_pieces)
+        scalars.astype(jnp.int32), attn_in, cot_held, attn_got, b_qkv, *rope_tables(seq_len), lanes
+    )
+    (mixed, grad_proj, attn_got), mlp_pieces = after((mixed, grad_proj, attn_got), mlp_pieces)
     mlp_mine = total(mlp_pieces).astype(bf16)
     mixed, grad_proj, mlp_mine = lax.optimization_barrier((mixed, grad_proj, mlp_mine))
-    mlp_parts = spread(mlp_mine)
+    mlp_own, mlp_far, mlp_near = halve(mlp_mine)
+
+    w_qkv = jnp.zeros((D, qkv_width), bf16)
+    w_out = jnp.zeros((D, D), bf16)
+    for k, piece in enumerate(attn_got):
+        w_qkv = place(w_qkv, piece[:, :qkv_width], shard ^ k)
+        w_out = place(w_out, piece[:, qkv_width:], shard ^ k)
+    w_out_rows = jnp.pad(take(w_out, seat, lanes), ((0, spare), (0, 0)))
+    delta_out = mlp_out + dot(mixed, w_out_rows)
     mixed_all = stacked(gather(mixed[:, :lanes], team_group)).swapaxes(0, 1).reshape(seq_len, D)
+    grad_proj, mlp_near = lax.optimization_barrier((grad_proj, mlp_near))
+    mlp_part = quarter(mlp_own, mlp_far, mlp_near)
+    grad_attn_in = dot(grad_proj, w_qkv, NT)
     qkv_grad = dot(attn_in, grad_proj, TN)
-    grad_attn_in = dot(grad_proj, w_qkv, NT)
-    delta_out = mlp_out + dot(mixed, w_out_rows)
     out_cols = D // team
     out_grad = dot(mixed_all, take(cot, seat, out_cols, 1), TN)
 
@@ -692,8 +732,13 @@
     attn_grads = jnp.concatenate(
         [
             attn_grads,
-            vector_row(
-                [qkv_b_grad, columns(grad_attn_in * normed), columns(grad_attn_in)], attn_width
+            vector_rows(
+                [
+                    (0, qkv_b_grad.reshape(fsdp, -1)),
+                    (0, columns(grad_attn_in * normed)),
+                    (0, columns(grad_attn_in)),
+                ],
+                attn_width,
             ),
         ],
         1,
@@ -706,8 +751,7 @@
     def returned(pieces):
         return stacked([(j, piece[0]) for j, piece in pieces])
 
-    delta_out, mlp_parts = after(home(delta_out).astype(bf16), mlp_parts)
-    mlp_part = summed(mlp_parts)
+    delta_out, mlp_part = lax.optimization_barrier((home(delta_out).astype(bf16), mlp_part))
     out_pieces = exchange(delta_out, seqs_group)
 
     grad_normed = home(grad_attn_in * gain_a + grad_mlp_in * gain_m)
@@ -723,13 +767,10 @@
         tokens.astype(f32) + returned(out_pieces).astype(f32) + full_out_b + full_down_b
     ).astype(bf16)
 
-    mlp_part, in_pieces = after(mlp_part, in_pieces)
+    mlp_all = whole_again(widen(mlp_part))
+    attn_mine, in_pieces = after(total(attn_pieces).astype(bf16), in_pieces)
     tokens_grad = cotangent.astype(f32) + returned(in_pieces).astype(f32)
-    mlp_whole = gather(mlp_part, seqs_group)
-    attn_mine, mlp_whole = after(total(attn_pieces).astype(bf16), mlp_whole)
-    attn_parts = spread(attn_mine)
-    mlp_all = joined_columns(mlp_whole)
-    attn_all = joined_columns(gather(summed(attn_parts), seqs_group))
+    attn_all = whole_again(widen(quarter(*halve(attn_mine))))
 
     up_mine = jnp.concatenate(
         [
@@ -759,13 +800,13 @@
         1,
     ).astype(f32)
     out_mine = jnp.concatenate([attn_all[t, :own_rows, qkv_width:] for t in range(team)], 1).astype(f32)
-    mlp_vec = mlp_all[:, own_rows].astype(f32)
-    attn_vec = columns(attn_all[:, own_rows].astype(f32))
-    up_b_mine = mlp_vec[:, :unit].reshape(-1)
-    mlp_vec = columns(mlp_vec)[unit:]
-    bias_mine = mlp_vec[2 * own_rows : 3 * own_rows]
-    qkv_b_mine = attn_vec[: 3 * own_rows]
-    attn_vec = attn_vec[3 * own_rows :]
+    mlp_vec = mlp_all[:, own_rows : own_rows + 4].astype(f32)
+    up_b_mine = mlp_vec[:, 0, D : D + unit].reshape(-1)
+    mlp_vec = take(jnp.sum(mlp_vec[:, 1:, :D], 0), shard, own_rows, 1)
+    bias_mine = mlp_vec[2] * (1.0 / team)
+    attn_vec = jnp.sum(attn_all[:, own_rows : own_rows + 3].astype(f32), 0)
+    qkv_b_mine = attn_vec[0, : 3 * own_rows]
+    attn_vec = take(attn_vec[1:, :D], shard, own_rows, 1)
 
     return (
         layer_out,
@@ -778,10 +819,10 @@
         up_b_mine,
         down_mine,
         bias_mine,
-        attn_vec[:own_rows],
-        attn_vec[own_rows : 2 * own_rows],
-        mlp_vec[:own_rows],
-        mlp_vec[own_rows : 2 * own_rows],
+        attn_vec[0],
+        attn_vec[1],
+        mlp_vec[0],
+        mlp_vec[1],
     )
 
 

time: 443 us -> 389 us (0.88)
  local copies, waits for them, and re-layouts: 86.2 us -> 51.8 us
  starting transfers between devices: 70.9 us -> 43.9 us
  waiting for transfers between devices: 124 us -> 132 us
  matrix products: 18.6 us -> 14.1 us
    ppermute x41 -> x35, starting transfers between devices: 70.9 us -> 43.9 us  [swap(): return lax.ppermute(x, axis, [(j, j ^ by) for j in range(n)])]
    dynamic_update_slice x11 -> x0, local copies, waits for them, and re-layouts: 9.78 us -> none  [the longest x5 4.76 us: local(): w_qkv = lax.dynamic_update_slice(w_qkv, piece[:, :qkv_width], (at, 0))]
    ppermute x41 -> x35, waiting for transfers between devices: 124 us -> 132 us  [swap(): return lax.ppermute(x, axis, [(j, j ^ by) for j in range(n)])]
    dynamic_slice x12 -> x8, local copies, waits for them, and re-layouts: 11.7 us -> 3.67 us  [take(): return lax.dynamic_slice_in_dim(x, at * size, size, axis)]
    unnamed x132 -> x123, local copies, waits for them, and re-layouts: 12.4 us -> 4.73 us
    dynamic_update_slice x22 -> x30, local copies, waits for them, and re-layouts: 7.13 us -> 14.2 us  [place(): lax.dynamic_update_slice_in_dim(out, piece, at * piece.shape[axis], axis)]
    slice x10 -> x3, local copies, waits for them, and re-layouts: 7.91 us -> 1.25 us  [the longest x1 0.64 us: local(): attn_vec[1]]
    dot_general x4, matrix products: 18.6 us -> 14.1 us  [dot(): return lax.dot_general(a, b, dims, preferred_element_type=f32)]
  transfers between devices with their start and end apart: 41 -> 35, of which waited for: 15 -> 14; matrix products, arithmetic and copies ran while one was open for 25% -> 22% of each run, Pallas kernels for 23% -> 26%
where the time goes in v3:
time: 389 us; the launch traced here: 383 us
  waiting for transfers between devices  132 us (34%)
  Pallas kernels  101 us (26%)
  local copies, waits for them, and re-layouts  51.8 us (13%)
  starting transfers between devices  43.9 us (11%)
  other arithmetic  36.9 us (9%)
  matrix products  14.1 us (4%)
    ppermute x35, waiting for transfers between devices, swap(): return lax.ppermute(x, axis, [(j, j ^ by) for j in range(n)])  132 us
    pallas_call x1, Pallas kernels, attention(): pl.pallas_call(functools.partial(attention_kernel, seq_len=seq_len, rows=...  60.2 us
    ppermute x35, starting transfers between devices, swap(): return lax.ppermute(x, axis, [(j, j ^ by) for j in range(n)])  43.9 us
    pallas_call x1, Pallas kernels, mlp(): pl.pallas_call(functools.partial(mlp_kernel, layout=layout, fsdp=fsdp, ow...  40.8 us
    dynamic_update_slice x30, local copies, waits for them, and re-layouts, place(): lax.dynamic_update_slice_in_dim(out, piece, at * piece.shape[axis], axis)  14.2 us
    dot_general x4, matrix products, dot(): return lax.dot_general(a, b, dims, preferred_element_type=f32)  14.1 us
  transfers between devices with their start and end apart: 35, of which 14 were waited for; matrix products, arithmetic and copies ran while one was open for 22% of the time, Pallas kernels for 26%

profile of v3, /device:TPU:0, one launch (start us, length us, event | category | flops | bytes accessed | tf_op | source)
XLA Modules:
  0.0 382.8 jit_solution(8365846149319300772)
XLA Ops:
  0.7 5.4 %concatenate.72 = bf16[2496]{0:T(1024)(128)(2,1)S(1)} concatenate(bf16[576]{0:T(1024)(128)(2,1)} %param.21, bf16[192]{0:T(256)(128)(2,1)} %param.23, bf16[768]{0:T(1024)(128)(2,1)} %param.25, bf16[192]{0:T(256)(128)(2,1)} %param.27, bf16[192]{0:T(256)(128)(2,1)} %param.28, bf16[192]{0:T(256)(128)(2,1)} %param.29, bf16[192]{0:T(256)(128)(2,1)} %param.30, bf16[192]{0:T(256)(128)(2,1)} %param.31), dimensions={0} | concatenate | bytes 9984 | tf_op jit(solution)/shard_map/concatenate | solution.py:562
  9.1 2.9 collective-permute-start.4
  12.0 1.5 collective-permute-start.5
  14.6 1.6 collective-permute-start
  16.2 2.7 collective-permute-start.1
  24.9 16.2 %collective-permute-done = bf16[2,192,768]{2,1,0:T(8,128)(2,1)} collective-permute-done((bf16[2,192,768]{2,1,0:T(8,128)(2,1)}, bf16[2,192,768]{2,1,0:T(8,128)(2,1)}, u32[]{:S(2)}, u32[]{:S(2)}) %collective-permute-start) | collective-permute-done | bytes 589856 | tf_op jit(solution)/shard_map/ppermute | solution.py:439
  43.2 15.6 %collective-permute-done.1 = bf16[2,192,768]{2,1,0:T(8,128)(2,1)} collective-permute-done((bf16[2,192,768]{2,1,0:T(8,128)(2,1)S(1)}, bf16[2,192,768]{2,1,0:T(8,128)(2,1)}, u32[]{:S(2)}, u32[]{:S(2)}) %collective-permute-start.1) | collective-permute-done | bytes 589856 | tf_op jit(solution)/shard_map/ppermute | solution.py:439
  61.9 11.6 %collective-permute-done.5.refs_2_ = bf16[224,3072]{1,0:T(8,128)(2,1)} collective-permute-done((bf16[224,3072]{1,0:T(8,128)(2,1)}, bf16[224,3072]{1,0:T(8,128)(2,1)}, u32[]{:S(2)}, u32[]{:S(2)}) %collective-permute-start.5) | collective-permute-done | bytes 1376288 | tf_op jit(solution)/shard_map/ppermute | solution.py:439
  84.8 1.9 select_bitcast_fusion.5
  87.0 1.6 copy.43
  88.8 1.6 copy.44
  90.4 40.8 %mlp.1 = (bf16[1536,768]{1,0:T(8,128)(2,1)}, f32[1536,768]{1,0:T(8,128)}, f32[1536,768]{1,0:T(8,128)}, bf16[1,208,3072]{2,1,0:T(8,128)(2,1)}, bf16[1,208,3072]{2...) custom-call(s32[1]{0:T(128)} %bitcast.5.shard_ref, bf16[1536,768]{1,0:T(8,128)(2,1)} %bitcast.361, ...), custom_call_target="tpu_custom_call" | custom-call | flops 21743271936 | bytes 30000000 | tf_op jit(solution)/shard_map/mlp/pallas_call | solution.py:395
  135.3 1.4 collective-permute-start.12
  136.8 60.2 %attention.1 = (bf16[1536,384]{1,0:T(8,128)(2,1)}, bf16[1536,1152]{1,0:T(8,128)(2,1)}) custom-call(s32[3]{0:T(128)} %pad_add_fusion.scalar_ref, bf16[1536,768]{1,0:T(8,128)(2,1)} %get-tuple-element.75.attn_in_ref, bf16[1536,768]{1,0:T(8,128)(2,1)} %bitcast.359, f32[1,1152]{1,0:T(1,128)} %copy-done.30, f32[1536,128]{1,0:T(8,128)} %constant.84.clone.cos_ref, ...), custom_call_target="tpu_custom_call" | custom-call | flops 14495514624 | bytes 12000000 | tf_op jit(solution)/shard_map/attention/pallas_call | solution.py:226
  197.0 2.5 fusion.18
  199.7 1.6 collective-permute-start.13
  208.6 1.5 slice_dynamic-update-slice_fusion.1
  214.6 4.8 %multiply_reduce_fusion = (bf16[768]{0:T(1024)(128)(2,1)}, bf16[768]{0:T(1024)(128)(2,1)}, bf16[1536,768]{1,0:T(8,128)(2,1)S(1)}) fusion(f32[1536]{0:T(1024)S(1)} %rsqrt.21, f32[1536]{0:T(1024)S(1)} %copy-done.25, bf16[4,2,192,768]{3,2,1,0:T(8,128)(2,1)S(1)} %copy-done.11, f32[1536,768]{1,0:T(8,128)S(1)} %bitcast.376, f32[768]{0:T(1024)S(1)} %copy-done.27, ...), kind=kOutput, calls=%fused_computation.7 | convolution fusion | flops 2729703936 | bytes 14767104 | tf_op jit(solution)/shard_map/dot_general | solution.py:34
  221.4 2.6 collective-permute-start.16
  224.1 4.5 %convolution_convert_fusion = bf16[768,1152]{1,0:T(8,128)(2,1)} fusion(bf16[1536,768]{1,0:T(8,128)(2,1)S(1)} %copy-done.32, bf16[1536,1152]{1,0:T(8,128)(2,1)S(1)} %copy-done.9), kind=kOutput, calls=%fused_computation.10 | convolution fusion | flops 2718793728 | bytes 7667712 | tf_op jit(solution)/shard_map/dot_general | solution.py:34
  232.0 7.4 %collective-permute-done.16 = bf16[208,768]{1,0:T(8,128)(2,1)} collective-permute-done((bf16[208,768]{1,0:T(8,128)(2,1)}, bf16[208,768]{1,0:T(8,128)(2,1)}, u32[]{:S(2)}, u32[]{:S(2)}) %collective-permute-start.16) | collective-permute-done | bytes 319520 | tf_op jit(solution)/shard_map/ppermute | solution.py:439
  239.4 2.0 fusion.23
  241.4 1.9 fusion.15
  244.7 3.4 collective-permute-start.18
  248.7 1.5 select_bitcast_fusion.3
  250.2 1.7 maximum_bitcast_fusion.2
  251.9 4.6 %copy.48 = bf16[1536,2,384]{0,2,1:T(8,128)(2,1)} copy(bf16[1536,2,384]{2,0,1:T(8,128)(2,1)} %maximum_bitcast_fusion.2) | data formatting | bytes 4718592 | tf_op jit(solution)/shard_map/transpose | solution.py:702
  257.4 3.5 convolution_convert_fusion.1
  261.5 26.2 %collective-permute-done.32 = bf16[208,768]{1,0:T(8,128)(2,1)S(1)} collective-permute-done((bf16[208,768]{1,0:T(8,128)(2,1)S(1)}, bf16[208,768]{1,0:T(8,128)(2,1)S(1)}, u32[]{:S(2)}, u32[]{:S(2)}) %collective-permute-start.32) | collective-permute-done | bytes 319520 | tf_op jit(solution)/shard_map/ppermute | solution.py:439
  287.7 1.5 collective-permute-start.23
  290.0 2.2 fusion.16
  293.6 2.0 fusion.13
  295.9 2.0 collective-permute-start.24
  301.0 4.9 %collective-permute-done.23 = bf16[1,208,1536]{2,1,0:T(8,128)(2,1)S(1)} collective-permute-done((bf16[1,208,1536]{2,1,0:T(8,128)(2,1)S(1)}, bf16[1,208,1536]{2,1,0:T(8,128)(2,1)S(1)}, u32[]{:S(2)}, u32[]{:S(2)}) %collective-permute-start.23) | collective-permute-done | bytes 639008 | tf_op jit(solution)/shard_map/ppermute | solution.py:439
  305.9 11.5 %collective-permute-done.22 = bf16[1,208,1536]{2,1,0:T(8,128)(2,1)S(1)} collective-permute-done((bf16[1,208,1536]{2,1,0:T(8,128)(2,1)S(1)}, bf16[1,208,1536]{2,1,0:T(8,128)(2,1)S(1)}, u32[]{:S(2)}, u32[]{:S(2)}) %collective-permute-start.22) | collective-permute-done | bytes 639008 | tf_op jit(solution)/shard_map/ppermute | solution.py:439
  317.5 2.4 collective-permute-start.26
  320.2 1.5 add_convert_fusion.3
  321.7 1.8 collective-permute-done.24
  323.5 6.3 %collective-permute-done.26 = bf16[1,192,768]{2,1,0:T(8,128)(2,1)S(1)} collective-permute-done((bf16[1,192,768]{2,1,0:T(8,128)(2,1)S(1)}, bf16[1,192,768]{2,1,0:T(8,128)(2,1)S(1)}, u32[]{:S(2)}, u32[]{:S(2)}) %collective-permute-start.26) | collective-permute-done | bytes 294944 | tf_op jit(solution)/shard_map/ppermute | solution.py:439
  329.9 6.5 %collective-permute-start.27 = (bf16[2,208,384]{2,1,0:T(8,128)(2,1)S(1)}, bf16[2,208,384]{2,1,0:T(8,128)(2,1)S(1)}, u32[]{:S(2)}, u32[]{:S(2)}) collective-permute-start(bf16[2,208,384]{2,1,0:T(8,128)(2,1)S(1)} %pad_maximum_fusion.5), channel_id=1, source_target_pairs={{0,8},{4,12},{8,0},{12,4},{16,24},{20,28},{24,16},{28,20},{1,9},{5... | collective-permute-start | bytes 958472 | tf_op jit(solution)/shard_map/ppermute | solution.py:439
  336.6 7.2 %collective-permute-done.27 = bf16[2,208,384]{2,1,0:T(8,128)(2,1)S(1)} collective-permute-done((bf16[2,208,384]{2,1,0:T(8,128)(2,1)S(1)}, bf16[2,208,384]{2,1,0:T(8,128)(2,1)S(1)}, u32[]{:S(2)}, u32[]{:S(2)}) %collective-permute-start.27) | collective-permute-done | bytes 319520 | tf_op jit(solution)/shard_map/ppermute | solution.py:439
  343.9 1.8 collective-permute-start.28
  345.8 7.6 %collective-permute-done.28 = bf16[208,384]{1,0:T(8,128)(2,1)S(1)} collective-permute-done((bf16[208,384]{1,0:T(8,128)(2,1)S(1)}, bf16[208,384]{1,0:T(8,128)(2,1)S(1)}, u32[]{:S(2)}, u32[]{:S(2)}) %collective-permute-start.28) | collective-permute-done | bytes 159776 | tf_op jit(solution)/shard_map/ppermute | solution.py:439
  353.7 8.2 %collective-permute-done.29 = bf16[208,384]{1,0:T(8,128)(2,1)S(1)} collective-permute-done((bf16[208,384]{1,0:T(8,128)(2,1)S(1)}, bf16[208,384]{1,0:T(8,128)(2,1)S(1)}, u32[]{:S(2)}, u32[]{:S(2)}) %collective-permute-start.29) | collective-permute-done | bytes 159776 | tf_op jit(solution)/shard_map/ppermute | solution.py:439
  362.0 1.7 convert_add_fusion.2
  363.7 7.7 %collective-permute-done.30 = bf16[2,208,384]{2,1,0:T(8,128)(2,1)S(1)} collective-permute-done((bf16[2,208,384]{2,1,0:T(8,128)(2,1)S(1)}, bf16[2,208,384]{2,1,0:T(8,128)(2,1)S(1)}, u32[]{:S(2)}, u32[]{:S(2)}) %collective-permute-start.30) | collective-permute-done | bytes 319520 | tf_op jit(solution)/shard_map/ppermute | solution.py:439
  372.7 1.7 convert_element_type.392
  375.1 1.6 maximum_convert_fusion
  (313 shorter events, 65.5 us)
Async XLA Ops:
  7.8 5.7 %copy-start.5 = (bf16[4,192,768]{2,1,0:T(8,128)(2,1)S(1)}, bf16[4,192,768]{2,1,0:T(8,128)(2,1)}, u32[]{:S(2)}) copy-start(bf16[4,192,768]{2,1,0:T(8,128)(2,1)} %param.17) | copy-start | bytes 3538948
  7.9 5.7 %copy-start.7 = (bf16[4,192,768]{2,1,0:T(8,128)(2,1)S(1)}, bf16[4,192,768]{2,1,0:T(8,128)(2,1)}, u32[]{:S(2)}) copy-start(bf16[4,192,768]{2,1,0:T(8,128)(2,1)} %param.19) | copy-start | bytes 3538948
  9.1 52.8 %collective-permute-start.4 = (bf16[224,3072]{1,0:T(8,128)(2,1)}, bf16[224,3072]{1,0:T(8,128)(2,1)}, u32[]{:S(2)}, u32[]{:S(2)}) collective-permute-start(bf16[224,3072]{1,0:T(8,128)(2,1)} %fusion.17.refs_0_), channel_id=1, source_target_pairs={{0,1},{1,0},{2,3},{3,2},{4,5},{5,4},{6,7},{7,6},{8,9},{9,8},{10,11... | collective-permute-start | bytes 4128776 | tf_op jit(solution)/shard_map/ppermute | solution.py:439
  12.0 61.4 %collective-permute-start.5 = (bf16[224,3072]{1,0:T(8,128)(2,1)}, bf16[224,3072]{1,0:T(8,128)(2,1)}, u32[]{:S(2)}, u32[]{:S(2)}) collective-permute-start(bf16[224,3072]{1,0:T(8,128)(2,1)} %fusion.17.refs_0_), channel_id=1, source_target_pairs={{0,2},{1,3},{2,0},{3,1},{4,6},{5,7},{6,4},{7,5},{8,10},{9,11},{10,... | collective-permute-start | bytes 4128776 | tf_op jit(solution)/shard_map/ppermute | solution.py:439
  14.6 5.4 %copy-start.15 = (bf16[192,2304]{1,0:T(8,128)(2,1)S(1)}, bf16[192,2304]{1,0:T(8,128)(2,1)}, u32[]{:S(2)}) copy-start(bf16[192,2304]{1,0:T(8,128)(2,1)} %param.20) | copy-start | bytes 2654212
  14.6 26.5 %collective-permute-start = (bf16[2,192,768]{2,1,0:T(8,128)(2,1)}, bf16[2,192,768]{2,1,0:T(8,128)(2,1)}, u32[]{:S(2)}, u32[]{:S(2)}) collective-permute-start(bf16[2,192,768]{2,1,0:T(8,128)(2,1)} %pad_maximum_fusion.2), channel_id=1, source_target_pairs={{0,8},{4,12},{8,0},{12,4},{16,24},{20,28},{24,16},{28,20},{1,9},{5... | collective-permute-start | bytes 1769480 | tf_op jit(solution)/shard_map/ppermute | solution.py:439
  16.2 42.6 %collective-permute-start.1 = (bf16[2,192,768]{2,1,0:T(8,128)(2,1)S(1)}, bf16[2,192,768]{2,1,0:T(8,128)(2,1)}, u32[]{:S(2)}, u32[]{:S(2)}) collective-permute-start(bf16[2,192,768]{2,1,0:T(8,128)(2,1)S(1)} %pad_maximum_fusion.3), channel_id=1, source_target_pairs={{0,16},{4,20},{8,24},{12,28},{16,0},{20,4},{24,8},{28,12},{1,17},{... | collective-permute-start | bytes 1769480 | tf_op jit(solution)/shard_map/ppermute | solution.py:439
  19.7 40.2 %collective-permute-start.2 = (bf16[2,192,768]{2,1,0:T(8,128)(2,1)}, bf16[2,192,768]{2,1,0:T(8,128)(2,1)}, u32[]{:S(2)}, u32[]{:S(2)}) collective-permute-start(bf16[2,192,768]{2,1,0:T(8,128)(2,1)} %pad_maximum_fusion.4), channel_id=1, source_target_pairs={{0,24},{4,28},{8,16},{12,20},{16,8},{20,12},{24,0},{28,4},{1,25},{... | collective-permute-start | bytes 1769480 | tf_op jit(solution)/shard_map/ppermute | solution.py:439
  41.0 32.4 %collective-permute-start.6 = (bf16[224,3072]{1,0:T(8,128)(2,1)}, bf16[224,3072]{1,0:T(8,128)(2,1)S(1)}, u32[]{:S(2)}, u32[]{:S(2)}) collective-permute-start(bf16[224,3072]{1,0:T(8,128)(2,1)} %fusion.17.refs_0_), channel_id=1, source_target_pairs={{0,3},{1,2},{2,1},{3,0},{4,7},{5,6},{6,5},{7,4},{8,11},{9,10},{10,... | collective-permute-start | bytes 4128776 | tf_op jit(solution)/shard_map/ppermute | solution.py:439
  61.1 16.8 %copy-start.17 = (bf16[192,1920]{1,0:T(8,128)(2,1)S(1)}, bf16[192,1920]{1,0:T(8,128)(2,1)}, u32[]{:S(2)}) copy-start(bf16[192,1920]{1,0:T(8,128)(2,1)} %copy-done.16) | copy-start | bytes 2211844
  61.1 23.7 %collective-permute-start.3 = (bf16[4,2,192,768]{3,2,0,1:T(8,128)(2,1)S(1)}, bf16[4,2,192,768]{3,2,0,1:T(8,128)(2,1)}, u32[]{:S(2)}, u32[]{:S(2)}) collective-permute-start(bf16[4,2,192,768]{3,2,0,1:T(8,128)(2,1)S(1)} %bitcast_dynamic-update-slice_fusion), channel_id=1, source_target_pairs={{0,4},{4,0},{8,12},{12,8},{16,20},{20,16},{24,28},{28,24},{1,5},{5... | collective-permute-start | bytes 7077896 | tf_op jit(solution)/shard_map/ppermute | solution.py:439
  77.9 55.3 %collective-permute-start.7 = (bf16[192,1920]{1,0:T(8,128)(2,1)S(1)}, bf16[192,1920]{1,0:T(8,128)(2,1)}, u32[]{:S(2)}, u32[]{:S(2)}) collective-permute-start(bf16[192,1920]{1,0:T(8,128)(2,1)S(1)} %copy-done.17), channel_id=1, source_target_pairs={{0,1},{1,0},{2,3},{3,2},{4,5},{5,4},{6,7},{7,6},{8,9},{9,8},{10,11... | collective-permute-start | bytes 2211848 | tf_op jit(solution)/shard_map/ppermute | solution.py:439
  79.0 54.2 %collective-permute-start.8 = (bf16[192,1920]{1,0:T(8,128)(2,1)S(1)}, bf16[192,1920]{1,0:T(8,128)(2,1)}, u32[]{:S(2)}, u32[]{:S(2)}) collective-permute-start(bf16[192,1920]{1,0:T(8,128)(2,1)S(1)} %copy-done.17), channel_id=1, source_target_pairs={{0,2},{1,3},{2,0},{3,1},{4,6},{5,7},{6,4},{7,5},{8,10},{9,11},{10,... | collective-permute-start | bytes 2211848 | tf_op jit(solution)/shard_map/ppermute | solution.py:439
  80.0 53.2 %collective-permute-start.9 = (bf16[192,1920]{1,0:T(8,128)(2,1)S(1)}, bf16[192,1920]{1,0:T(8,128)(2,1)}, u32[]{:S(2)}, u32[]{:S(2)}) collective-permute-start(bf16[192,1920]{1,0:T(8,128)(2,1)S(1)} %copy-done.17), channel_id=1, source_target_pairs={{0,3},{1,2},{2,1},{3,0},{4,7},{5,6},{6,5},{7,4},{8,11},{9,10},{10,... | collective-permute-start | bytes 2211848 | tf_op jit(solution)/shard_map/ppermute | solution.py:439
  133.2 63.8 %copy-start.13 = (bf16[1,208,3072]{2,1,0:T(8,128)(2,1)S(1)}, bf16[1,208,3072]{2,1,0:T(8,128)(2,1)}, u32[]{:S(2)}) copy-start(bf16[1,208,3072]{2,1,0:T(8,128)(2,1)} %get-tuple-element.89) | copy-start | bytes 3833860
  133.2 63.8 %collective-permute-start.10 = (bf16[1,208,3072]{2,1,0:T(8,128)(2,1)}, bf16[1,208,3072]{2,1,0:T(8,128)(2,1)S(1)}, u32[]{:S(2)}, u32[]{:S(2)}) collective-permute-start(bf16[1,208,3072]{2,1,0:T(8,128)(2,1)} %get-tuple-element.84), channel_id=1, source_target_pairs={{0,1},{1,0},{2,3},{3,2},{4,5},{5,4},{6,7},{7,6},{8,9},{9,8},{10,11... | collective-permute-start | bytes 3833864 | tf_op jit(solution)/shard_map/ppermute | solution.py:439
  134.4 62.6 %collective-permute-start.11 = (bf16[1,208,3072]{2,1,0:T(8,128)(2,1)}, bf16[1,208,3072]{2,1,0:T(8,128)(2,1)}, u32[]{:S(2)}, u32[]{:S(2)}) collective-permute-start(bf16[1,208,3072]{2,1,0:T(8,128)(2,1)} %get-tuple-element.85), channel_id=1, source_target_pairs={{0,2},{1,3},{2,0},{3,1},{4,6},{5,7},{6,4},{7,5},{8,10},{9,11},{10,... | collective-permute-start | bytes 3833864 | tf_op jit(solution)/shard_map/ppermute | solution.py:439
  135.3 61.7 %collective-permute-start.12 = (bf16[1,208,3072]{2,1,0:T(8,128)(2,1)}, bf16[1,208,3072]{2,1,0:T(8,128)(2,1)}, u32[]{:S(2)}, u32[]{:S(2)}) collective-permute-start(bf16[1,208,3072]{2,1,0:T(8,128)(2,1)} %get-tuple-element.86), channel_id=1, source_target_pairs={{0,3},{1,2},{2,1},{3,0},{4,7},{5,6},{6,5},{7,4},{8,11},{9,10},{10,... | collective-permute-start | bytes 3833864 | tf_op jit(solution)/shard_map/ppermute | solution.py:439
  199.5 21.0 %copy-start.4 = (bf16[208,3072]{1,0:T(8,128)(2,1)}, bf16[208,3072]{1,0:T(8,128)(2,1)S(1)}, u32[]{:S(2)}) copy-start(bf16[208,3072]{1,0:T(8,128)(2,1)S(1)} %fusion.18) | copy-start | bytes 3833860
  199.7 13.1 %collective-permute-start.13 = (bf16[2,208,768]{2,1,0:T(8,128)(2,1)S(1)}, bf16[2,208,768]{2,1,0:T(8,128)(2,1)S(1)}, u32[]{:S(2)}, u32[]{:S(2)}) collective-permute-start(bf16[2,208,768]{2,1,0:T(8,128)(2,1)S(1)} %pad_maximum_fusion), channel_id=1, source_target_pairs={{0,8},{4,12},{8,0},{12,4},{16,24},{20,28},{24,16},{28,20},{1,9},{5... | collective-permute-start | bytes 1916936 | tf_op jit(solution)/shard_map/ppermute | solution.py:439
  203.8 44.9 %collective-permute-start.20 = (bf16[1536,384]{1,0:T(8,128)(2,1)S(1)}, bf16[1536,384]{1,0:T(8,128)(2,1)}, u32[]{:S(2)}, u32[]{:S(2)}) collective-permute-start(bf16[1536,384]{1,0:T(8,128)(2,1)S(1)} %copy-done.1), channel_id=1, source_target_pairs={{0,4},{4,0},{8,12},{12,8},{16,20},{20,16},{24,28},{28,24},{1,5},{5... | collective-permute-start | bytes 3538952 | tf_op jit(solution)/shard_map/ppermute | solution.py:439
  206.2 7.2 %slice-start.2 = ((s8[4718592]{0:T(1024)(128)(4,1)}), s8[4194304]{0:T(1024)(128)(4,1)S(1)}, s32[]{:S(2)}) async-start(s8[4718592]{0:T(1024)(128)(4,1)} %bitcast.375), calls=%async_computation.2 | async-start | bytes 8388608
  207.7 5.7 %slice-start.3 = ((s8[4718592]{0:T(1024)(128)(4,1)}), s8[524288]{0:T(1024)(128)(4,1)S(1)}, s32[]{:S(2)}) async-start(s8[4718592]{0:T(1024)(128)(4,1)} %bitcast.375), calls=%async_computation.3 | async-start | bytes 1048576
  211.2 30.2 %collective-permute-start.15 = (bf16[1,4,192,768]{3,2,1,0:T(8,128)(2,1)}, bf16[1,4,192,768]{3,2,1,0:T(8,128)(2,1)}, u32[]{:S(2)}, u32[]{:S(2)}) collective-permute-start(bf16[1,4,192,768]{3,2,1,0:T(8,128)(2,1)} %dynamic-slice_bitcast_fusion), channel_id=1, source_target_pairs={{0,4},{4,0},{8,12},{12,8},{16,20},{20,16},{24,28},{28,24},{1,5},{5... | collective-permute-start | bytes 3538952 | tf_op jit(solution)/shard_map/ppermute | solution.py:439
  212.8 7.7 %copy-start.19 = (bf16[2,208,768]{2,1,0:T(8,128)(2,1)}, bf16[2,208,768]{2,1,0:T(8,128)(2,1)S(1)}, u32[]{:S(2)}) copy-start(bf16[2,208,768]{2,1,0:T(8,128)(2,1)S(1)} %collective-permute-done.13) | copy-start | bytes 1916932
  219.4 4.7 %copy-start.32 = (bf16[1536,768]{1,0:T(8,128)(2,1)S(1)}, bf16[1536,768]{1,0:T(8,128)(2,1)}, u32[]{:S(2)}) copy-start(bf16[1536,768]{1,0:T(8,128)(2,1)} %get-tuple-element.75.attn_in_ref) | copy-start | bytes 7077892
  220.5 68.7 %collective-permute-start.14 = (bf16[1,4,192,768]{3,2,1,0:T(8,128)(2,1)}, bf16[1,4,192,768]{3,2,1,0:T(8,128)(2,1)}, u32[]{:S(2)}, u32[]{:S(2)}) collective-permute-start(bf16[1,4,192,768]{3,2,1,0:T(8,128)(2,1)} %dynamic-slice_bitcast_fusion.1), channel_id=1, source_target_pairs={{0,4},{4,0},{8,12},{12,8},{16,20},{20,16},{24,28},{28,24},{1,5},{5... | collective-permute-start | bytes 3538952 | tf_op jit(solution)/shard_map/ppermute | solution.py:439
  221.4 18.0 %collective-permute-start.16 = (bf16[208,768]{1,0:T(8,128)(2,1)}, bf16[208,768]{1,0:T(8,128)(2,1)}, u32[]{:S(2)}, u32[]{:S(2)}) collective-permute-start(bf16[208,768]{1,0:T(8,128)(2,1)} %fusion.21), channel_id=1, source_target_pairs={{0,16},{4,20},{8,24},{12,28},{16,0},{20,4},{24,8},{28,12},{1,17},{... | collective-permute-start | bytes 958472 | tf_op jit(solution)/shard_map/ppermute | solution.py:439
  244.3 47.9 %collective-permute-start.17 = (bf16[1,192,768]{2,1,0:T(8,128)(2,1)}, bf16[1,192,768]{2,1,0:T(8,128)(2,1)}, u32[]{:S(2)}, u32[]{:S(2)}) collective-permute-start(bf16[1,192,768]{2,1,0:T(8,128)(2,1)} %get-tuple-element.148), channel_id=1, source_target_pairs={{0,8},{4,12},{8,0},{12,4},{16,24},{20,28},{24,16},{28,20},{1,9},{5... | collective-permute-start | bytes 884744 | tf_op jit(solution)/shard_map/ppermute | solution.py:439
  244.7 50.9 %collective-permute-start.18 = (bf16[1,192,768]{2,1,0:T(8,128)(2,1)}, bf16[1,192,768]{2,1,0:T(8,128)(2,1)}, u32[]{:S(2)}, u32[]{:S(2)}) collective-permute-start(bf16[1,192,768]{2,1,0:T(8,128)(2,1)} %get-tuple-element.147), channel_id=1, source_target_pairs={{0,16},{4,20},{8,24},{12,28},{16,0},{20,4},{24,8},{28,12},{1,17},{... | collective-permute-start | bytes 884744 | tf_op jit(solution)/shard_map/ppermute | solution.py:439
  248.1 47.7 %collective-permute-start.19 = (bf16[1,192,768]{2,1,0:T(8,128)(2,1)}, bf16[1,192,768]{2,1,0:T(8,128)(2,1)}, u32[]{:S(2)}, u32[]{:S(2)}) collective-permute-start(bf16[1,192,768]{2,1,0:T(8,128)(2,1)} %get-tuple-element.146), channel_id=1, source_target_pairs={{0,24},{4,28},{8,16},{12,20},{16,8},{20,12},{24,0},{28,4},{1,25},{... | collective-permute-start | bytes 884744 | tf_op jit(solution)/shard_map/ppermute | solution.py:439
  256.4 31.2 %collective-permute-start.32 = (bf16[208,768]{1,0:T(8,128)(2,1)S(1)}, bf16[208,768]{1,0:T(8,128)(2,1)S(1)}, u32[]{:S(2)}, u32[]{:S(2)}) collective-permute-start(bf16[208,768]{1,0:T(8,128)(2,1)S(1)} %copy-done.10), channel_id=1, source_target_pairs={{0,16},{4,20},{8,24},{12,28},{16,0},{20,4},{24,8},{28,12},{1,17},{... | collective-permute-start | bytes 958472 | tf_op jit(solution)/shard_map/ppermute | solution.py:439
  261.3 28.7 %copy-start.3 = (bf16[1536,768]{1,0:T(8,128)(2,1)S(1)}, bf16[1536,768]{1,0:T(8,128)(2,1)}, u32[]{:S(2)}) copy-start(bf16[1536,768]{1,0:T(8,128)(2,1)} %copy-done.2) | copy-start | bytes 7077892
  287.7 18.3 %collective-permute-start.23 = (bf16[1,208,1536]{2,1,0:T(8,128)(2,1)S(1)}, bf16[1,208,1536]{2,1,0:T(8,128)(2,1)S(1)}, u32[]{:S(2)}, u32[]{:S(2)}) collective-permute-start(bf16[1,208,1536]{2,1,0:T(8,128)(2,1)S(1)} %get-tuple-element.130), channel_id=1, source_target_pairs={{0,3},{1,2},{2,1},{3,0},{4,7},{5,6},{6,5},{7,4},{8,11},{9,10},{10,... | collective-permute-start | bytes 1916936 | tf_op jit(solution)/shard_map/ppermute | solution.py:439
  289.3 28.2 %collective-permute-start.22 = (bf16[1,208,1536]{2,1,0:T(8,128)(2,1)S(1)}, bf16[1,208,1536]{2,1,0:T(8,128)(2,1)S(1)}, u32[]{:S(2)}, u32[]{:S(2)}) collective-permute-start(bf16[1,208,1536]{2,1,0:T(8,128)(2,1)S(1)} %get-tuple-element.131), channel_id=1, source_target_pairs={{0,2},{1,3},{2,0},{3,1},{4,6},{5,7},{6,4},{7,5},{8,10},{9,11},{10,... | collective-permute-start | bytes 1916936 | tf_op jit(solution)/shard_map/ppermute | solution.py:439
  292.3 27.6 %collective-permute-start.21 = (bf16[1,208,1536]{2,1,0:T(8,128)(2,1)S(1)}, bf16[1,208,1536]{2,1,0:T(8,128)(2,1)S(1)}, u32[]{:S(2)}, u32[]{:S(2)}) collective-permute-start(bf16[1,208,1536]{2,1,0:T(8,128)(2,1)S(1)} %get-tuple-element.129), channel_id=1, source_target_pairs={{0,1},{1,0},{2,3},{3,2},{4,5},{5,4},{6,7},{7,6},{8,9},{9,8},{10,11... | collective-permute-start | bytes 1916936 | tf_op jit(solution)/shard_map/ppermute | solution.py:439
  295.7 40.9 %collective-permute-start.33 = (bf16[2,208,768]{2,1,0:T(8,128)(2,1)S(1)}, bf16[2,208,768]{2,1,0:T(8,128)(2,1)S(1)}, u32[]{:S(2)}, u32[]{:S(2)}) collective-permute-start(bf16[2,208,768]{2,1,0:T(8,128)(2,1)S(1)} %pad_maximum_fusion.1), channel_id=1, source_target_pairs={{0,8},{4,12},{8,0},{12,4},{16,24},{20,28},{24,16},{28,20},{1,9},{5... | collective-permute-start | bytes 1916936 | tf_op jit(solution)/shard_map/ppermute | solution.py:439
  295.9 27.6 %collective-permute-start.24 = (bf16[1,192,768]{2,1,0:T(8,128)(2,1)S(1)}, bf16[1,192,768]{2,1,0:T(8,128)(2,1)S(1)}, u32[]{:S(2)}, u32[]{:S(2)}) collective-permute-start(bf16[1,192,768]{2,1,0:T(8,128)(2,1)S(1)} %get-tuple-element.144), channel_id=1, source_target_pairs={{0,8},{4,12},{8,0},{12,4},{16,24},{20,28},{24,16},{28,20},{1,9},{5... | collective-permute-start | bytes 884744 | tf_op jit(solution)/shard_map/ppermute | solution.py:439
  305.9 17.6 %collective-permute-start.25 = (bf16[1,192,768]{2,1,0:T(8,128)(2,1)S(1)}, bf16[1,192,768]{2,1,0:T(8,128)(2,1)S(1)}, u32[]{:S(2)}, u32[]{:S(2)}) collective-permute-start(bf16[1,192,768]{2,1,0:T(8,128)(2,1)S(1)} %get-tuple-element.143), channel_id=1, source_target_pairs={{0,16},{4,20},{8,24},{12,28},{16,0},{20,4},{24,8},{28,12},{1,17},{... | collective-permute-start | bytes 884744 | tf_op jit(solution)/shard_map/ppermute | solution.py:439
  317.5 12.3 %collective-permute-start.26 = (bf16[1,192,768]{2,1,0:T(8,128)(2,1)S(1)}, bf16[1,192,768]{2,1,0:T(8,128)(2,1)S(1)}, u32[]{:S(2)}, u32[]{:S(2)}) collective-permute-start(bf16[1,192,768]{2,1,0:T(8,128)(2,1)S(1)} %get-tuple-element.142), channel_id=1, source_target_pairs={{0,24},{4,28},{8,16},{12,20},{16,8},{20,12},{24,0},{28,4},{1,25},{... | collective-permute-start | bytes 884744 | tf_op jit(solution)/shard_map/ppermute | solution.py:439
  329.9 13.9 %collective-permute-start.27 = (bf16[2,208,384]{2,1,0:T(8,128)(2,1)S(1)}, bf16[2,208,384]{2,1,0:T(8,128)(2,1)S(1)}, u32[]{:S(2)}, u32[]{:S(2)}) collective-permute-start(bf16[2,208,384]{2,1,0:T(8,128)(2,1)S(1)} %pad_maximum_fusion.5), channel_id=1, source_target_pairs={{0,8},{4,12},{8,0},{12,4},{16,24},{20,28},{24,16},{28,20},{1,9},{5... | collective-permute-start | bytes 958472 | tf_op jit(solution)/shard_map/ppermute | solution.py:439
  343.9 9.5 %collective-permute-start.28 = (bf16[208,384]{1,0:T(8,128)(2,1)S(1)}, bf16[208,384]{1,0:T(8,128)(2,1)S(1)}, u32[]{:S(2)}, u32[]{:S(2)}) collective-permute-start(bf16[208,384]{1,0:T(8,128)(2,1)S(1)} %fusion.29), channel_id=1, source_target_pairs={{0,16},{4,20},{8,24},{12,28},{16,0},{20,4},{24,8},{28,12},{1,17},{... | collective-permute-start | bytes 479240 | tf_op jit(solution)/shard_map/ppermute | solution.py:439
  345.7 25.9 %collective-permute-start.34 = (bf16[208,3072]{1,0:T(8,128)(2,1)S(1)}, bf16[208,3072]{1,0:T(8,128)(2,1)S(1)}, u32[]{:S(2)}, u32[]{:S(2)}) collective-permute-start(bf16[208,3072]{1,0:T(8,128)(2,1)S(1)} %fusion.27), channel_id=1, source_target_pairs={{0,4},{4,0},{8,12},{12,8},{16,20},{20,16},{24,28},{28,24},{1,5},{5... | collective-permute-start | bytes 3833864 | tf_op jit(solution)/shard_map/ppermute | solution.py:439
  353.5 8.5 %copy-start.8 = (bf16[4,192,768]{2,1,0:T(8,128)(2,1)S(1)}, bf16[4,192,768]{2,1,0:T(8,128)(2,1)}, u32[]{:S(2)}) copy-start(bf16[4,192,768]{2,1,0:T(8,128)(2,1)} %param.19) | copy-start | bytes 3538948
  353.6 8.3 %collective-permute-start.29 = (bf16[208,384]{1,0:T(8,128)(2,1)S(1)}, bf16[208,384]{1,0:T(8,128)(2,1)S(1)}, u32[]{:S(2)}, u32[]{:S(2)}) collective-permute-start(bf16[208,384]{1,0:T(8,128)(2,1)S(1)} %get-tuple-element.121), channel_id=1, source_target_pairs={{0,16},{4,20},{8,24},{12,28},{16,0},{20,4},{24,8},{28,12},{1,17},{... | collective-permute-start | bytes 479240 | tf_op jit(solution)/shard_map/ppermute | solution.py:439
  361.9 9.5 %collective-permute-start.30 = (bf16[2,208,384]{2,1,0:T(8,128)(2,1)S(1)}, bf16[2,208,384]{2,1,0:T(8,128)(2,1)S(1)}, u32[]{:S(2)}, u32[]{:S(2)}) collective-permute-start(bf16[2,208,384]{2,1,0:T(8,128)(2,1)S(1)} %pad_maximum_fusion.6), channel_id=1, source_target_pairs={{0,8},{4,12},{8,0},{12,4},{16,24},{20,28},{24,16},{28,20},{1,9},{5... | collective-permute-start | bytes 958472 | tf_op jit(solution)/shard_map/ppermute | solution.py:439
  371.5 5.1 %collective-permute-start.31 = (bf16[208,1536]{1,0:T(8,128)(2,1)S(1)}, bf16[208,1536]{1,0:T(8,128)(2,1)}, u32[]{:S(2)}, u32[]{:S(2)}) collective-permute-start(bf16[208,1536]{1,0:T(8,128)(2,1)S(1)} %fusion.32), channel_id=1, source_target_pairs={{0,4},{4,0},{8,12},{12,8},{16,20},{20,16},{24,28},{28,24},{1,5},{5... | collective-permute-start | bytes 1916936 | tf_op jit(solution)/shard_map/ppermute | solution.py:439
  372.5 9.3 %copy-start.26 = (f32[1,192]{1,0:T(1,128)}, f32[1,192]{1,0:T(1,128)S(1)}, u32[]{:S(2)}) copy-start(f32[1,192]{1,0:T(1,128)S(1)} %get-tuple-element.181) | copy-start | bytes 2308
  (24 other events, 58.7 us)

commit v4 on v3

--- a/solution.py
+++ b/solution.py
@@ -540,10 +540,11 @@
     own_rows = D // fsdp
     folds = unit // own_rows
 
-    both = []
-    for s in range(seqs):
-        block = jnp.concatenate([take(tokens, seq ^ s, 1), take(cotangent, seq ^ s, 1)])
-        both.append((seq ^ s, swap(block, "ctx", s * team) if s else block))
+    blocks = [
+        jnp.concatenate([take(tokens, seq ^ s, 1), take(cotangent, seq ^ s, 1)]) for s in range(seqs)
+    ]
+    both = [(seq ^ s, swap(x, "ctx", s * team) if s else x) for s, x in enumerate(blocks)]
+    blocks, up_weight, down_weight = lax.optimization_barrier((blocks, up_weight, down_weight))
     half = stacked(both)
     joined = gather(half, team_group)
     tok_half = half[:, 0]
@@ -699,13 +700,14 @@
         w_out = place(w_out, piece[:, qkv_width:], shard ^ k)
     w_out_rows = jnp.pad(take(w_out, seat, lanes), ((0, spare), (0, 0)))
     delta_out = mlp_out + dot(mixed, w_out_rows)
-    mixed_all = stacked(gather(mixed[:, :lanes], team_group)).swapaxes(0, 1).reshape(seq_len, D)
+    mixed_got = gather(mixed[:, :lanes], team_group)
     grad_proj, mlp_near = lax.optimization_barrier((grad_proj, mlp_near))
     mlp_part = quarter(mlp_own, mlp_far, mlp_near)
     grad_attn_in = dot(grad_proj, w_qkv, NT)
     qkv_grad = dot(attn_in, grad_proj, TN)
     out_cols = D // team
-    out_grad = dot(mixed_all, take(cot, seat, out_cols, 1), TN)
+    cot_cols = take(cot, seat, out_cols, 1)
+    out_grad = stacked([(j, dot(m, cot_cols, TN).astype(bf16)) for j, m in mixed_got])
 
     qkv_b_grad = columns(grad_proj.astype(f32))
     qkv_b_grad = jnp.concatenate(
@@ -767,10 +769,12 @@
         tokens.astype(f32) + returned(out_pieces).astype(f32) + full_out_b + full_down_b
     ).astype(bf16)
 
-    mlp_all = whole_again(widen(mlp_part))
-    attn_mine, in_pieces = after(total(attn_pieces).astype(bf16), in_pieces)
+    mlp_two, attn_pieces = after(widen(mlp_part), attn_pieces)
+    attn_mine = total(attn_pieces).astype(bf16)
+    attn_own, attn_far, attn_near = halve(attn_mine)
+    mlp_all = whole_again(mlp_two)
     tokens_grad = cotangent.astype(f32) + returned(in_pieces).astype(f32)
-    attn_all = whole_again(widen(quarter(*halve(attn_mine))))
+    attn_all = whole_again(widen(quarter(attn_own, attn_far, attn_near)))
 
     up_mine = jnp.concatenate(
         [

time: 389 us -> 374 us (0.961)
  waiting for transfers between devices: 132 us -> 122 us
  starting transfers between devices: 43.9 us -> 50.7 us
  local copies, waits for them, and re-layouts: 51.8 us -> 45 us
  other arithmetic: 36.9 us -> 32.3 us
    ppermute x35, waiting for transfers between devices: 132 us -> 122 us  [swap(): return lax.ppermute(x, axis, [(j, j ^ by) for j in range(n)])]
    ppermute x35, starting transfers between devices: 43.9 us -> 50.7 us  [swap(): return lax.ppermute(x, axis, [(j, j ^ by) for j in range(n)])]
    transpose x1 -> x0, local copies, waits for them, and re-layouts: 4.55 us -> none  [local(): stacked(gather(mixed[:, :lanes], team_group)).swapaxes(0, 1)]
    unnamed x123 -> x127, local copies, waits for them, and re-layouts: 4.73 us -> 8.26 us
    dynamic_update_slice x30 -> x29, local copies, waits for them, and re-layouts: 14.2 us -> 10.7 us  [place(): lax.dynamic_update_slice_in_dim(out, piece, at * piece.shape[axis], axis)]
    dot_general x4 -> x5, matrix products: 14.1 us -> 14.4 us  [dot(): return lax.dot_general(a, b, dims, preferred_element_type=f32)]
  transfers between devices with their start and end apart: 35 -> 35, of which waited for: 14 -> 11; matrix products, arithmetic and copies ran while one was open for 22% -> 21% of each run, Pallas kernels for 26% -> 27%
where the time goes in v4:
time: 374 us; the launch traced here: 368 us
  waiting for transfers between devices  122 us (33%)
  Pallas kernels  101 us (27%)
  starting transfers between devices  50.7 us (14%)
  local copies, waits for them, and re-layouts  45 us (12%)
  other arithmetic  32.3 us (9%)
  matrix products  14.4 us (4%)
    ppermute x35, waiting for transfers between devices, swap(): return lax.ppermute(x, axis, [(j, j ^ by) for j in range(n)])  122 us
    pallas_call x1, Pallas kernels, attention(): pl.pallas_call(functools.partial(attention_kernel, seq_len=seq_len, rows=...  60.1 us
    ppermute x35, starting transfers between devices, swap(): return lax.ppermute(x, axis, [(j, j ^ by) for j in range(n)])  50.7 us
    pallas_call x1, Pallas kernels, mlp(): pl.pallas_call(functools.partial(mlp_kernel, layout=layout, fsdp=fsdp, ow...  40.8 us
    dot_general x5, matrix products, dot(): return lax.dot_general(a, b, dims, preferred_element_type=f32)  14.4 us
    dynamic_update_slice x29, local copies, waits for them, and re-layouts, place(): lax.dynamic_update_slice_in_dim(out, piece, at * piece.shape[axis], axis)  10.7 us
    unnamed x127, local copies, waits for them, and re-layouts  8.26 us
  transfers between devices with their start and end apart: 35, of which 11 were waited for; matrix products, arithmetic and copies ran while one was open for 21% of the time, Pallas kernels for 27%

profile of v4, /device:TPU:0, one launch (start us, length us, event | category | flops | bytes accessed | tf_op | source)
XLA Modules:
  0.0 367.8 jit_solution(2051251682743788529)
XLA Ops:
  0.7 1.8 constant_dynamic-slice_fusion.37
  3.3 3.1 collective-permute-start
  6.5 2.7 collective-permute-start.1
  10.0 2.8 concatenate.72
  16.3 1.7 collective-permute-start.4
  18.0 1.5 collective-permute-start.5
  24.4 7.6 %collective-permute-done = bf16[2,192,768]{2,1,0:T(8,128)(2,1)} collective-permute-done((bf16[2,192,768]{2,1,0:T(8,128)(2,1)}, bf16[2,192,768]{2,1,0:T(8,128)(2,1)}, u32[]{:S(2)}, u32[]{:S(2)}) %collective-permute-start) | collective-permute-done | bytes 589856 | tf_op jit(solution)/shard_map/ppermute | solution.py:439
  32.0 2.6 collective-permute-start.6
  35.7 13.4 %collective-permute-done.1 = bf16[2,192,768]{2,1,0:T(8,128)(2,1)} collective-permute-done((bf16[2,192,768]{2,1,0:T(8,128)(2,1)S(1)}, bf16[2,192,768]{2,1,0:T(8,128)(2,1)}, u32[]{:S(2)}, u32[]{:S(2)}) %collective-permute-start.1) | collective-permute-done | bytes 589856 | tf_op jit(solution)/shard_map/ppermute | solution.py:439
  52.2 26.5 %collective-permute-done.5.refs_2_ = bf16[224,3072]{1,0:T(8,128)(2,1)} collective-permute-done((bf16[224,3072]{1,0:T(8,128)(2,1)}, bf16[224,3072]{1,0:T(8,128)(2,1)}, u32[]{:S(2)}, u32[]{:S(2)}) %collective-permute-start.5) | collective-permute-done | bytes 1376288 | tf_op jit(solution)/shard_map/ppermute | solution.py:439
  85.2 1.4 collective-permute-start.9
  90.0 1.9 select_bitcast_fusion.3
  92.2 1.6 copy.42
  94.0 1.6 copy.43
  95.6 40.8 %mlp.1 = (bf16[1536,768]{1,0:T(8,128)(2,1)}, f32[1536,768]{1,0:T(8,128)}, f32[1536,768]{1,0:T(8,128)}, bf16[1,208,3072]{2,1,0:T(8,128)(2,1)}, bf16[1,208,3072]{2...) custom-call(s32[1]{0:T(128)} %bitcast.5.shard_ref, bf16[1536,768]{1,0:T(8,128)(2,1)} %bitcast.352, ...), custom_call_target="tpu_custom_call" | custom-call | flops 21743271936 | bytes 30000000 | tf_op jit(solution)/shard_map/mlp/pallas_call | solution.py:395
  140.6 1.4 collective-permute-start.12
  142.0 60.1 %attention.1 = (bf16[1536,384]{1,0:T(8,128)(2,1)}, bf16[1536,1152]{1,0:T(8,128)(2,1)}) custom-call(s32[3]{0:T(128)} %pad_add_fusion.scalar_ref, bf16[1536,768]{1,0:T(8,128)(2,1)} %get-tuple-element.79.attn_in_ref, bf16[1536,768]{1,0:T(8,128)(2,1)} %bitcast.341, f32[1,1152]{1,0:T(1,128)} %copy-done.32, f32[1536,128]{1,0:T(8,128)} %constant.88.clone.cos_ref, ...), custom_call_target="tpu_custom_call" | custom-call | flops 14495514624 | bytes 12000000 | tf_op jit(solution)/shard_map/attention/pallas_call | solution.py:226
  202.2 2.5 fusion.18
  215.9 1.4 copy-done
  217.3 1.6 convolution_convert_fusion.2
  221.8 4.8 %multiply_reduce_fusion = (bf16[768]{0:T(1024)(128)(2,1)}, bf16[768]{0:T(1024)(128)(2,1)}, bf16[1536,768]{1,0:T(8,128)(2,1)S(1)}) fusion(f32[1536]{0:T(1024)S(1)} %rsqrt.21, f32[1536]{0:T(1024)S(1)} %copy-done.23, bf16[4,2,192,768]{3,2,1,0:T(8,128)(2,1)S(1)} %copy-done.10, f32[1536,768]{1,0:T(8,128)S(1)} %bitcast.366, f32[768]{0:T(1024)S(1)} %copy-done.25, ...), kind=kOutput, calls=%fused_computation.7 | convolution fusion | flops 2729703936 | bytes 14767104 | tf_op jit(solution)/shard_map/dot_general | solution.py:34
  229.0 2.9 collective-permute-start.16
  231.9 4.5 %convolution_convert_fusion = bf16[768,1152]{1,0:T(8,128)(2,1)} fusion(bf16[1536,768]{1,0:T(8,128)(2,1)S(1)} %copy-done.34, bf16[1536,1152]{1,0:T(8,128)(2,1)S(1)} %copy-done.9), kind=kOutput, calls=%fused_computation.10 | convolution fusion | flops 2718793728 | bytes 7667712 | tf_op jit(solution)/shard_map/dot_general | solution.py:34
  239.3 7.6 %collective-permute-done.16 = bf16[208,768]{1,0:T(8,128)(2,1)} collective-permute-done((bf16[208,768]{1,0:T(8,128)(2,1)}, bf16[208,768]{1,0:T(8,128)(2,1)}, u32[]{:S(2)}, u32[]{:S(2)}) %collective-permute-start.16) | collective-permute-done | bytes 319520 | tf_op jit(solution)/shard_map/ppermute | solution.py:439
  248.1 2.0 fusion.15
  250.7 3.4 collective-permute-start.18
  254.2 2.2 select_bitcast_fusion.9
  258.1 22.8 %collective-permute-done.23 = bf16[208,768]{1,0:T(8,128)(2,1)S(1)} collective-permute-done((bf16[208,768]{1,0:T(8,128)(2,1)S(1)}, bf16[208,768]{1,0:T(8,128)(2,1)S(1)}, u32[]{:S(2)}, u32[]{:S(2)}) %collective-permute-start.23) | collective-permute-done | bytes 319520 | tf_op jit(solution)/shard_map/ppermute | solution.py:439
  280.9 1.5 collective-permute-start.26
  283.6 2.2 fusion.16
  285.8 2.5 collective-permute-start.19
  288.3 2.3 fusion.13
  290.6 4.5 %collective-permute-done.19 = bf16[1,192,768]{2,1,0:T(8,128)(2,1)S(1)} collective-permute-done((bf16[1,192,768]{2,1,0:T(8,128)(2,1)S(1)}, bf16[1,192,768]{2,1,0:T(8,128)(2,1)S(1)}, u32[]{:S(2)}, u32[]{:S(2)}) %collective-permute-start.19) | collective-permute-done | bytes 294944 | tf_op jit(solution)/shard_map/ppermute | solution.py:439
  295.3 4.1 %collective-permute-start.20 = (bf16[1,192,768]{2,1,0:T(8,128)(2,1)S(1)}, bf16[1,192,768]{2,1,0:T(8,128)(2,1)S(1)}, u32[]{:S(2)}, u32[]{:S(2)}) collective-permute-start(bf16[1,192,768]{2,1,0:T(8,128)(2,1)S(1)} %get-tuple-element.147), channel_id=1, source_target_pairs={{0,8},{4,12},{8,0},{12,4},{16,24},{20,28},{24,16},{28,20},{1,9},{5... | collective-permute-start | bytes 884744 | tf_op jit(solution)/shard_map/ppermute | solution.py:439
  299.4 2.4 collective-permute-start.22
  301.8 8.0 %collective-permute-done.26 = bf16[1,208,1536]{2,1,0:T(8,128)(2,1)S(1)} collective-permute-done((bf16[1,208,1536]{2,1,0:T(8,128)(2,1)S(1)}, bf16[1,208,1536]{2,1,0:T(8,128)(2,1)S(1)}, u32[]{:S(2)}, u32[]{:S(2)}) %collective-permute-start.26) | collective-permute-done | bytes 639008 | tf_op jit(solution)/shard_map/ppermute | solution.py:439
  310.3 2.0 collective-permute-start.33
  313.7 1.5 add_convert_fusion.3
  315.2 11.2 %collective-permute-done.28 = bf16[2,208,384]{2,1,0:T(8,128)(2,1)S(1)} collective-permute-done((bf16[2,208,384]{2,1,0:T(8,128)(2,1)S(1)}, bf16[2,208,384]{2,1,0:T(8,128)(2,1)S(1)}, u32[]{:S(2)}, u32[]{:S(2)}) %collective-permute-start.28) | collective-permute-done | bytes 319520 | tf_op jit(solution)/shard_map/ppermute | solution.py:439
  326.4 2.5 collective-permute-start.29
  329.0 10.9 %collective-permute-done.29 = bf16[208,384]{1,0:T(8,128)(2,1)S(1)} collective-permute-done((bf16[208,384]{1,0:T(8,128)(2,1)S(1)}, bf16[208,384]{1,0:T(8,128)(2,1)S(1)}, u32[]{:S(2)}, u32[]{:S(2)}) %collective-permute-start.29) | collective-permute-done | bytes 159776 | tf_op jit(solution)/shard_map/ppermute | solution.py:439
  340.0 3.4 collective-permute-start.30
  343.6 4.4 %collective-permute-done.30 = bf16[208,384]{1,0:T(8,128)(2,1)S(1)} collective-permute-done((bf16[208,384]{1,0:T(8,128)(2,1)S(1)}, bf16[208,384]{1,0:T(8,128)(2,1)S(1)}, u32[]{:S(2)}, u32[]{:S(2)}) %collective-permute-start.30) | collective-permute-done | bytes 159776 | tf_op jit(solution)/shard_map/ppermute | solution.py:439
  348.0 2.2 collective-permute-start.31
  350.3 4.9 %collective-permute-done.31 = bf16[2,208,384]{2,1,0:T(8,128)(2,1)S(1)} collective-permute-done((bf16[2,208,384]{2,1,0:T(8,128)(2,1)S(1)}, bf16[2,208,384]{2,1,0:T(8,128)(2,1)S(1)}, u32[]{:S(2)}, u32[]{:S(2)}) %collective-permute-start.31) | collective-permute-done | bytes 319520 | tf_op jit(solution)/shard_map/ppermute | solution.py:439
  355.3 1.7 convert_add_fusion.2
  362.9 1.7 convert_element_type.396
  365.2 1.6 maximum_convert_fusion
  (317 shorter events, 61.9 us)
Async XLA Ops:
  3.3 6.7 %copy-start.27 = (bf16[576]{0:T(1024)(128)(2,1)S(1)}, bf16[576]{0:T(1024)(128)(2,1)}, u32[]{:S(2)}) copy-start(bf16[576]{0:T(1024)(128)(2,1)} %param.21) | copy-start | bytes 3460
  3.3 6.7 %copy-start.28 = (bf16[768]{0:T(1024)(128)(2,1)S(1)}, bf16[768]{0:T(1024)(128)(2,1)}, u32[]{:S(2)}) copy-start(bf16[768]{0:T(1024)(128)(2,1)} %param.25) | copy-start | bytes 4612
  3.3 6.7 %copy-start.29 = (bf16[192]{0:T(256)(128)(2,1)S(1)}, bf16[192]{0:T(256)(128)(2,1)}, u32[]{:S(2)}) copy-start(bf16[192]{0:T(256)(128)(2,1)} %param.23) | copy-start | bytes 1156
  3.3 6.7 %copy-start.30 = (bf16[192]{0:T(256)(128)(2,1)S(1)}, bf16[192]{0:T(256)(128)(2,1)}, u32[]{:S(2)}) copy-start(bf16[192]{0:T(256)(128)(2,1)} %param.27) | copy-start | bytes 1156
  3.3 9.5 %copy-start.14 = (bf16[192,3072]{1,0:T(8,128)(2,1)S(1)}, bf16[192,3072]{1,0:T(8,128)(2,1)}, u32[]{:S(2)}) copy-start(bf16[192,3072]{1,0:T(8,128)(2,1)} %param.24) | copy-start | bytes 3538948
  3.3 28.6 %collective-permute-start = (bf16[2,192,768]{2,1,0:T(8,128)(2,1)}, bf16[2,192,768]{2,1,0:T(8,128)(2,1)}, u32[]{:S(2)}, u32[]{:S(2)}) collective-permute-start(bf16[2,192,768]{2,1,0:T(8,128)(2,1)} %pad_maximum_fusion.3), channel_id=1, source_target_pairs={{0,8},{4,12},{8,0},{12,4},{16,24},{20,28},{24,16},{28,20},{1,9},{5... | collective-permute-start | bytes 1769480 | tf_op jit(solution)/shard_map/ppermute | solution.py:439
  6.5 42.6 %collective-permute-start.1 = (bf16[2,192,768]{2,1,0:T(8,128)(2,1)S(1)}, bf16[2,192,768]{2,1,0:T(8,128)(2,1)}, u32[]{:S(2)}, u32[]{:S(2)}) collective-permute-start(bf16[2,192,768]{2,1,0:T(8,128)(2,1)S(1)} %pad_maximum_fusion.4), channel_id=1, source_target_pairs={{0,16},{4,20},{8,24},{12,28},{16,0},{20,4},{24,8},{28,12},{1,17},{... | collective-permute-start | bytes 1769480 | tf_op jit(solution)/shard_map/ppermute | solution.py:439
  10.0 40.2 %collective-permute-start.2 = (bf16[2,192,768]{2,1,0:T(8,128)(2,1)}, bf16[2,192,768]{2,1,0:T(8,128)(2,1)}, u32[]{:S(2)}, u32[]{:S(2)}) collective-permute-start(bf16[2,192,768]{2,1,0:T(8,128)(2,1)} %pad_maximum_fusion.5), channel_id=1, source_target_pairs={{0,24},{4,28},{8,16},{12,20},{16,8},{20,12},{24,0},{28,4},{1,25},{... | collective-permute-start | bytes 1769480 | tf_op jit(solution)/shard_map/ppermute | solution.py:439
  16.3 35.9 %collective-permute-start.4 = (bf16[224,3072]{1,0:T(8,128)(2,1)}, bf16[224,3072]{1,0:T(8,128)(2,1)}, u32[]{:S(2)}, u32[]{:S(2)}) collective-permute-start(bf16[224,3072]{1,0:T(8,128)(2,1)} %fusion.17.refs_0_), channel_id=1, source_target_pairs={{0,1},{1,0},{2,3},{3,2},{4,5},{5,4},{6,7},{7,6},{8,9},{9,8},{10,11... | collective-permute-start | bytes 4128776 | tf_op jit(solution)/shard_map/ppermute | solution.py:439
  18.0 60.7 %collective-permute-start.5 = (bf16[224,3072]{1,0:T(8,128)(2,1)}, bf16[224,3072]{1,0:T(8,128)(2,1)}, u32[]{:S(2)}, u32[]{:S(2)}) collective-permute-start(bf16[224,3072]{1,0:T(8,128)(2,1)} %fusion.17.refs_0_), channel_id=1, source_target_pairs={{0,2},{1,3},{2,0},{3,1},{4,6},{5,7},{6,4},{7,5},{8,10},{9,11},{10,... | collective-permute-start | bytes 4128776 | tf_op jit(solution)/shard_map/ppermute | solution.py:439
  32.0 46.7 %collective-permute-start.6 = (bf16[224,3072]{1,0:T(8,128)(2,1)}, bf16[224,3072]{1,0:T(8,128)(2,1)S(1)}, u32[]{:S(2)}, u32[]{:S(2)}) collective-permute-start(bf16[224,3072]{1,0:T(8,128)(2,1)} %fusion.17.refs_0_), channel_id=1, source_target_pairs={{0,3},{1,2},{2,1},{3,0},{4,7},{5,6},{6,5},{7,4},{8,11},{9,10},{10,... | collective-permute-start | bytes 4128776 | tf_op jit(solution)/shard_map/ppermute | solution.py:439
  51.3 31.8 %copy-start.17 = (bf16[192,1920]{1,0:T(8,128)(2,1)S(1)}, bf16[192,1920]{1,0:T(8,128)(2,1)}, u32[]{:S(2)}) copy-start(bf16[192,1920]{1,0:T(8,128)(2,1)} %copy-done.16) | copy-start | bytes 2211844
  51.3 38.7 %collective-permute-start.3 = (bf16[4,2,192,768]{3,2,0,1:T(8,128)(2,1)S(1)}, bf16[4,2,192,768]{3,2,0,1:T(8,128)(2,1)}, u32[]{:S(2)}, u32[]{:S(2)}) collective-permute-start(bf16[4,2,192,768]{3,2,0,1:T(8,128)(2,1)S(1)} %bitcast_dynamic-update-slice_fusion), channel_id=1, source_target_pairs={{0,4},{4,0},{8,12},{12,8},{16,20},{20,16},{24,28},{28,24},{1,5},{5... | collective-permute-start | bytes 7077896 | tf_op jit(solution)/shard_map/ppermute | solution.py:439
  83.1 55.3 %collective-permute-start.7 = (bf16[192,1920]{1,0:T(8,128)(2,1)S(1)}, bf16[192,1920]{1,0:T(8,128)(2,1)}, u32[]{:S(2)}, u32[]{:S(2)}) collective-permute-start(bf16[192,1920]{1,0:T(8,128)(2,1)S(1)} %copy-done.17), channel_id=1, source_target_pairs={{0,1},{1,0},{2,3},{3,2},{4,5},{5,4},{6,7},{7,6},{8,9},{9,8},{10,11... | collective-permute-start | bytes 2211848 | tf_op jit(solution)/shard_map/ppermute | solution.py:439
  84.2 54.2 %collective-permute-start.8 = (bf16[192,1920]{1,0:T(8,128)(2,1)S(1)}, bf16[192,1920]{1,0:T(8,128)(2,1)}, u32[]{:S(2)}, u32[]{:S(2)}) collective-permute-start(bf16[192,1920]{1,0:T(8,128)(2,1)S(1)} %copy-done.17), channel_id=1, source_target_pairs={{0,2},{1,3},{2,0},{3,1},{4,6},{5,7},{6,4},{7,5},{8,10},{9,11},{10,... | collective-permute-start | bytes 2211848 | tf_op jit(solution)/shard_map/ppermute | solution.py:439
  85.2 53.3 %collective-permute-start.9 = (bf16[192,1920]{1,0:T(8,128)(2,1)S(1)}, bf16[192,1920]{1,0:T(8,128)(2,1)}, u32[]{:S(2)}, u32[]{:S(2)}) collective-permute-start(bf16[192,1920]{1,0:T(8,128)(2,1)S(1)} %copy-done.17), channel_id=1, source_target_pairs={{0,3},{1,2},{2,1},{3,0},{4,7},{5,6},{6,5},{7,4},{8,11},{9,10},{10,... | collective-permute-start | bytes 2211848 | tf_op jit(solution)/shard_map/ppermute | solution.py:439
  138.5 63.7 %copy-start.12 = (bf16[1,208,3072]{2,1,0:T(8,128)(2,1)S(1)}, bf16[1,208,3072]{2,1,0:T(8,128)(2,1)}, u32[]{:S(2)}) copy-start(bf16[1,208,3072]{2,1,0:T(8,128)(2,1)} %get-tuple-element.93) | copy-start | bytes 3833860
  138.5 63.7 %collective-permute-start.10 = (bf16[1,208,3072]{2,1,0:T(8,128)(2,1)}, bf16[1,208,3072]{2,1,0:T(8,128)(2,1)S(1)}, u32[]{:S(2)}, u32[]{:S(2)}) collective-permute-start(bf16[1,208,3072]{2,1,0:T(8,128)(2,1)} %get-tuple-element.88), channel_id=1, source_target_pairs={{0,1},{1,0},{2,3},{3,2},{4,5},{5,4},{6,7},{7,6},{8,9},{9,8},{10,11... | collective-permute-start | bytes 3833864 | tf_op jit(solution)/shard_map/ppermute | solution.py:439
  139.7 62.5 %collective-permute-start.11 = (bf16[1,208,3072]{2,1,0:T(8,128)(2,1)}, bf16[1,208,3072]{2,1,0:T(8,128)(2,1)}, u32[]{:S(2)}, u32[]{:S(2)}) collective-permute-start(bf16[1,208,3072]{2,1,0:T(8,128)(2,1)} %get-tuple-element.89), channel_id=1, source_target_pairs={{0,2},{1,3},{2,0},{3,1},{4,6},{5,7},{6,4},{7,5},{8,10},{9,11},{10,... | collective-permute-start | bytes 3833864 | tf_op jit(solution)/shard_map/ppermute | solution.py:439
  140.6 61.6 %collective-permute-start.12 = (bf16[1,208,3072]{2,1,0:T(8,128)(2,1)}, bf16[1,208,3072]{2,1,0:T(8,128)(2,1)}, u32[]{:S(2)}, u32[]{:S(2)}) collective-permute-start(bf16[1,208,3072]{2,1,0:T(8,128)(2,1)} %get-tuple-element.90), channel_id=1, source_target_pairs={{0,3},{1,2},{2,1},{3,0},{4,7},{5,6},{6,5},{7,4},{8,11},{9,10},{10,... | collective-permute-start | bytes 3833864 | tf_op jit(solution)/shard_map/ppermute | solution.py:439
  204.7 23.4 %copy-start.6 = (bf16[208,3072]{1,0:T(8,128)(2,1)}, bf16[208,3072]{1,0:T(8,128)(2,1)S(1)}, u32[]{:S(2)}) copy-start(bf16[208,3072]{1,0:T(8,128)(2,1)S(1)} %fusion.18) | copy-start | bytes 3833860
  204.9 15.1 %collective-permute-start.13 = (bf16[2,208,768]{2,1,0:T(8,128)(2,1)S(1)}, bf16[2,208,768]{2,1,0:T(8,128)(2,1)S(1)}, u32[]{:S(2)}, u32[]{:S(2)}) collective-permute-start(bf16[2,208,768]{2,1,0:T(8,128)(2,1)S(1)} %pad_maximum_fusion), channel_id=1, source_target_pairs={{0,8},{4,12},{8,0},{12,4},{16,24},{20,28},{24,16},{28,20},{1,9},{5... | collective-permute-start | bytes 1916936 | tf_op jit(solution)/shard_map/ppermute | solution.py:439
  210.9 43.3 %collective-permute-start.24 = (bf16[1536,384]{1,0:T(8,128)(2,1)S(1)}, bf16[1536,384]{1,0:T(8,128)(2,1)}, u32[]{:S(2)}, u32[]{:S(2)}) collective-permute-start(bf16[1536,384]{1,0:T(8,128)(2,1)S(1)} %copy-done.3), channel_id=1, source_target_pairs={{0,4},{4,0},{8,12},{12,8},{16,20},{20,16},{24,28},{28,24},{1,5},{5... | collective-permute-start | bytes 3538952 | tf_op jit(solution)/shard_map/ppermute | solution.py:439
  212.1 8.5 %slice-start.2 = ((s8[4718592]{0:T(1024)(128)(4,1)}), s8[4194304]{0:T(1024)(128)(4,1)S(1)}, s32[]{:S(2)}) async-start(s8[4718592]{0:T(1024)(128)(4,1)} %bitcast.365), calls=%async_computation.2 | async-start | bytes 8388608
  213.5 7.1 %slice-start.3 = ((s8[4718592]{0:T(1024)(128)(4,1)}), s8[524288]{0:T(1024)(128)(4,1)S(1)}, s32[]{:S(2)}) async-start(s8[4718592]{0:T(1024)(128)(4,1)} %bitcast.365), calls=%async_computation.3 | async-start | bytes 1048576
  215.5 32.6 %collective-permute-start.15 = (bf16[1,4,192,768]{3,2,1,0:T(8,128)(2,1)}, bf16[1,4,192,768]{3,2,1,0:T(8,128)(2,1)}, u32[]{:S(2)}, u32[]{:S(2)}) collective-permute-start(bf16[1,4,192,768]{3,2,1,0:T(8,128)(2,1)} %dynamic-slice_bitcast_fusion), channel_id=1, source_target_pairs={{0,4},{4,0},{8,12},{12,8},{16,20},{20,16},{24,28},{28,24},{1,5},{5... | collective-permute-start | bytes 3538952 | tf_op jit(solution)/shard_map/ppermute | solution.py:439
  220.0 8.2 %copy-start.19 = (bf16[2,208,768]{2,1,0:T(8,128)(2,1)}, bf16[2,208,768]{2,1,0:T(8,128)(2,1)S(1)}, u32[]{:S(2)}) copy-start(bf16[2,208,768]{2,1,0:T(8,128)(2,1)S(1)} %collective-permute-done.13) | copy-start | bytes 1916932
  227.8 54.7 %collective-permute-start.14 = (bf16[1,4,192,768]{3,2,1,0:T(8,128)(2,1)}, bf16[1,4,192,768]{3,2,1,0:T(8,128)(2,1)}, u32[]{:S(2)}, u32[]{:S(2)}) collective-permute-start(bf16[1,4,192,768]{3,2,1,0:T(8,128)(2,1)} %dynamic-slice_bitcast_fusion.1), channel_id=1, source_target_pairs={{0,4},{4,0},{8,12},{12,8},{16,20},{20,16},{24,28},{28,24},{1,5},{5... | collective-permute-start | bytes 3538952 | tf_op jit(solution)/shard_map/ppermute | solution.py:439
  229.0 17.9 %collective-permute-start.16 = (bf16[208,768]{1,0:T(8,128)(2,1)}, bf16[208,768]{1,0:T(8,128)(2,1)}, u32[]{:S(2)}, u32[]{:S(2)}) collective-permute-start(bf16[208,768]{1,0:T(8,128)(2,1)} %fusion.21), channel_id=1, source_target_pairs={{0,16},{4,20},{8,24},{12,28},{16,0},{20,4},{24,8},{28,12},{1,17},{... | collective-permute-start | bytes 958472 | tf_op jit(solution)/shard_map/ppermute | solution.py:439
  250.2 35.6 %collective-permute-start.17 = (bf16[1,192,768]{2,1,0:T(8,128)(2,1)S(1)}, bf16[1,192,768]{2,1,0:T(8,128)(2,1)S(1)}, u32[]{:S(2)}, u32[]{:S(2)}) collective-permute-start(bf16[1,192,768]{2,1,0:T(8,128)(2,1)S(1)} %get-tuple-element.151), channel_id=1, source_target_pairs={{0,8},{4,12},{8,0},{12,4},{16,24},{20,28},{24,16},{28,20},{1,9},{5... | collective-permute-start | bytes 884744 | tf_op jit(solution)/shard_map/ppermute | solution.py:439
  250.7 39.9 %collective-permute-start.18 = (bf16[1,192,768]{2,1,0:T(8,128)(2,1)S(1)}, bf16[1,192,768]{2,1,0:T(8,128)(2,1)S(1)}, u32[]{:S(2)}, u32[]{:S(2)}) collective-permute-start(bf16[1,192,768]{2,1,0:T(8,128)(2,1)S(1)} %get-tuple-element.150), channel_id=1, source_target_pairs={{0,16},{4,20},{8,24},{12,28},{16,0},{20,4},{24,8},{28,12},{1,17},{... | collective-permute-start | bytes 884744 | tf_op jit(solution)/shard_map/ppermute | solution.py:439
  254.1 26.7 %collective-permute-start.23 = (bf16[208,768]{1,0:T(8,128)(2,1)S(1)}, bf16[208,768]{1,0:T(8,128)(2,1)S(1)}, u32[]{:S(2)}, u32[]{:S(2)}) collective-permute-start(bf16[208,768]{1,0:T(8,128)(2,1)S(1)} %fusion.23), channel_id=1, source_target_pairs={{0,16},{4,20},{8,24},{12,28},{16,0},{20,4},{24,8},{28,12},{1,17},{... | collective-permute-start | bytes 958472 | tf_op jit(solution)/shard_map/ppermute | solution.py:439
  256.7 26.9 %copy-start.5 = (bf16[1536,768]{1,0:T(8,128)(2,1)S(1)}, bf16[1536,768]{1,0:T(8,128)(2,1)}, u32[]{:S(2)}) copy-start(bf16[1536,768]{1,0:T(8,128)(2,1)} %copy-done.4) | copy-start | bytes 7077892
  256.9 42.5 %collective-permute-start.25 = (bf16[1,208,1536]{2,1,0:T(8,128)(2,1)S(1)}, bf16[1,208,1536]{2,1,0:T(8,128)(2,1)S(1)}, u32[]{:S(2)}, u32[]{:S(2)}) collective-permute-start(bf16[1,208,1536]{2,1,0:T(8,128)(2,1)S(1)} %get-tuple-element.135), channel_id=1, source_target_pairs={{0,1},{1,0},{2,3},{3,2},{4,5},{5,4},{6,7},{7,6},{8,9},{9,8},{10,11... | collective-permute-start | bytes 1916936 | tf_op jit(solution)/shard_map/ppermute | solution.py:439
  280.9 28.9 %collective-permute-start.26 = (bf16[1,208,1536]{2,1,0:T(8,128)(2,1)S(1)}, bf16[1,208,1536]{2,1,0:T(8,128)(2,1)S(1)}, u32[]{:S(2)}, u32[]{:S(2)}) collective-permute-start(bf16[1,208,1536]{2,1,0:T(8,128)(2,1)S(1)} %get-tuple-element.134), channel_id=1, source_target_pairs={{0,2},{1,3},{2,0},{3,1},{4,6},{5,7},{6,4},{7,5},{8,10},{9,11},{10,... | collective-permute-start | bytes 1916936 | tf_op jit(solution)/shard_map/ppermute | solution.py:439
  282.5 27.3 %collective-permute-start.27 = (bf16[1,208,1536]{2,1,0:T(8,128)(2,1)S(1)}, bf16[1,208,1536]{2,1,0:T(8,128)(2,1)S(1)}, u32[]{:S(2)}, u32[]{:S(2)}) collective-permute-start(bf16[1,208,1536]{2,1,0:T(8,128)(2,1)S(1)} %get-tuple-element.133), channel_id=1, source_target_pairs={{0,3},{1,2},{2,1},{3,0},{4,7},{5,6},{6,5},{7,4},{8,11},{9,10},{10,... | collective-permute-start | bytes 1916936 | tf_op jit(solution)/shard_map/ppermute | solution.py:439
  285.8 9.3 %collective-permute-start.19 = (bf16[1,192,768]{2,1,0:T(8,128)(2,1)S(1)}, bf16[1,192,768]{2,1,0:T(8,128)(2,1)S(1)}, u32[]{:S(2)}, u32[]{:S(2)}) collective-permute-start(bf16[1,192,768]{2,1,0:T(8,128)(2,1)S(1)} %get-tuple-element.149), channel_id=1, source_target_pairs={{0,24},{4,28},{8,16},{12,20},{16,8},{20,12},{24,0},{28,4},{1,25},{... | collective-permute-start | bytes 884744 | tf_op jit(solution)/shard_map/ppermute | solution.py:439
  295.3 48.2 %collective-permute-start.20 = (bf16[1,192,768]{2,1,0:T(8,128)(2,1)S(1)}, bf16[1,192,768]{2,1,0:T(8,128)(2,1)S(1)}, u32[]{:S(2)}, u32[]{:S(2)}) collective-permute-start(bf16[1,192,768]{2,1,0:T(8,128)(2,1)S(1)} %get-tuple-element.147), channel_id=1, source_target_pairs={{0,8},{4,12},{8,0},{12,4},{16,24},{20,28},{24,16},{28,20},{1,9},{5... | collective-permute-start | bytes 884744 | tf_op jit(solution)/shard_map/ppermute | solution.py:439
  299.4 50.8 %collective-permute-start.21 = (bf16[1,192,768]{2,1,0:T(8,128)(2,1)S(1)}, bf16[1,192,768]{2,1,0:T(8,128)(2,1)S(1)}, u32[]{:S(2)}, u32[]{:S(2)}) collective-permute-start(bf16[1,192,768]{2,1,0:T(8,128)(2,1)S(1)} %get-tuple-element.146), channel_id=1, source_target_pairs={{0,16},{4,20},{8,24},{12,28},{16,0},{20,4},{24,8},{28,12},{1,17},{... | collective-permute-start | bytes 884744 | tf_op jit(solution)/shard_map/ppermute | solution.py:439
  299.4 50.8 %collective-permute-start.22 = (bf16[1,192,768]{2,1,0:T(8,128)(2,1)S(1)}, bf16[1,192,768]{2,1,0:T(8,128)(2,1)S(1)}, u32[]{:S(2)}, u32[]{:S(2)}) collective-permute-start(bf16[1,192,768]{2,1,0:T(8,128)(2,1)S(1)} %get-tuple-element.145), channel_id=1, source_target_pairs={{0,24},{4,28},{8,16},{12,20},{16,8},{20,12},{24,0},{28,4},{1,25},{... | collective-permute-start | bytes 884744 | tf_op jit(solution)/shard_map/ppermute | solution.py:439
  310.2 16.1 %collective-permute-start.28 = (bf16[2,208,384]{2,1,0:T(8,128)(2,1)S(1)}, bf16[2,208,384]{2,1,0:T(8,128)(2,1)S(1)}, u32[]{:S(2)}, u32[]{:S(2)}) collective-permute-start(bf16[2,208,384]{2,1,0:T(8,128)(2,1)S(1)} %pad_maximum_fusion.7), channel_id=1, source_target_pairs={{0,8},{4,12},{8,0},{12,4},{16,24},{20,28},{24,16},{28,20},{1,9},{5... | collective-permute-start | bytes 958472 | tf_op jit(solution)/shard_map/ppermute | solution.py:439
  310.3 46.7 %collective-permute-start.33 = (bf16[2,208,768]{2,1,0:T(8,128)(2,1)S(1)}, bf16[2,208,768]{2,1,0:T(8,128)(2,1)S(1)}, u32[]{:S(2)}, u32[]{:S(2)}) collective-permute-start(bf16[2,208,768]{2,1,0:T(8,128)(2,1)S(1)} %pad_maximum_fusion.1), channel_id=1, source_target_pairs={{0,8},{4,12},{8,0},{12,4},{16,24},{20,28},{24,16},{28,20},{1,9},{5... | collective-permute-start | bytes 1916936 | tf_op jit(solution)/shard_map/ppermute | solution.py:439
  326.4 13.5 %collective-permute-start.29 = (bf16[208,384]{1,0:T(8,128)(2,1)S(1)}, bf16[208,384]{1,0:T(8,128)(2,1)S(1)}, u32[]{:S(2)}, u32[]{:S(2)}) collective-permute-start(bf16[208,384]{1,0:T(8,128)(2,1)S(1)} %fusion.29), channel_id=1, source_target_pairs={{0,16},{4,20},{8,24},{12,28},{16,0},{20,4},{24,8},{28,12},{1,17},{... | collective-permute-start | bytes 479240 | tf_op jit(solution)/shard_map/ppermute | solution.py:439
  340.0 7.9 %collective-permute-start.30 = (bf16[208,384]{1,0:T(8,128)(2,1)S(1)}, bf16[208,384]{1,0:T(8,128)(2,1)S(1)}, u32[]{:S(2)}, u32[]{:S(2)}) collective-permute-start(bf16[208,384]{1,0:T(8,128)(2,1)S(1)} %get-tuple-element.125), channel_id=1, source_target_pairs={{0,16},{4,20},{8,24},{12,28},{16,0},{20,4},{24,8},{28,12},{1,17},{... | collective-permute-start | bytes 479240 | tf_op jit(solution)/shard_map/ppermute | solution.py:439
  348.0 7.3 %copy-start.8 = (bf16[4,192,768]{2,1,0:T(8,128)(2,1)S(1)}, bf16[4,192,768]{2,1,0:T(8,128)(2,1)}, u32[]{:S(2)}) copy-start(bf16[4,192,768]{2,1,0:T(8,128)(2,1)} %param.19) | copy-start | bytes 3538948
  348.0 7.1 %collective-permute-start.31 = (bf16[2,208,384]{2,1,0:T(8,128)(2,1)S(1)}, bf16[2,208,384]{2,1,0:T(8,128)(2,1)S(1)}, u32[]{:S(2)}, u32[]{:S(2)}) collective-permute-start(bf16[2,208,384]{2,1,0:T(8,128)(2,1)S(1)} %pad_maximum_fusion.8), channel_id=1, source_target_pairs={{0,8},{4,12},{8,0},{12,4},{16,24},{20,28},{24,16},{28,20},{1,9},{5... | collective-permute-start | bytes 958472 | tf_op jit(solution)/shard_map/ppermute | solution.py:439
  355.2 2.4 collective-permute-start.32
  357.0 4.7 %collective-permute-start.34 = (bf16[208,3072]{1,0:T(8,128)(2,1)S(1)}, bf16[208,3072]{1,0:T(8,128)(2,1)S(1)}, u32[]{:S(2)}, u32[]{:S(2)}) collective-permute-start(bf16[208,3072]{1,0:T(8,128)(2,1)S(1)} %fusion.26), channel_id=1, source_target_pairs={{0,4},{4,0},{8,12},{12,8},{16,20},{20,16},{24,28},{28,24},{1,5},{5... | collective-permute-start | bytes 3833864 | tf_op jit(solution)/shard_map/ppermute | solution.py:439
  (26 other events, 72.4 us)

commit v5 on v4

--- a/solution.py
+++ b/solution.py
@@ -544,7 +544,6 @@
         jnp.concatenate([take(tokens, seq ^ s, 1), take(cotangent, seq ^ s, 1)]) for s in range(seqs)
     ]
     both = [(seq ^ s, swap(x, "ctx", s * team) if s else x) for s, x in enumerate(blocks)]
-    blocks, up_weight, down_weight = lax.optimization_barrier((blocks, up_weight, down_weight))
     half = stacked(both)
     joined = gather(half, team_group)
     tok_half = half[:, 0]
@@ -745,7 +744,6 @@
         ],
         1,
     )
-    attn_pieces = exchange(attn_grads, fsdp_group)
 
     def home(x):
         return scatter_sum(x.astype(bf16).reshape(seqs, team, width, D).swapaxes(0, 1), team_group)
@@ -757,21 +755,24 @@
     out_pieces = exchange(delta_out, seqs_group)
 
     grad_normed = home(grad_attn_in * gain_a + grad_mlp_in * gain_m)
+    attn_grads, grad_normed = lax.optimization_barrier((attn_grads, grad_normed))
+    attn_pieces = exchange(attn_grads, fsdp_group)
     normed_half, inv_half = normalise(tok_half)
     delta_in = inv_half * (
         grad_normed
         - jnp.mean(grad_normed, -1, keepdims=True)
         - normed_half * jnp.mean(grad_normed * normed_half, -1, keepdims=True)
     )
-    delta_in, out_pieces = after(delta_in.astype(bf16), out_pieces)
+    mlp_part, attn_pieces = after(mlp_part, attn_pieces)
+    mlp_two = widen(mlp_part)
+    attn_own, attn_far, attn_near = halve(total(attn_pieces).astype(bf16))
+    delta_in, attn_near = lax.optimization_barrier((delta_in.astype(bf16), attn_near))
+    delta_in, out_pieces = after(delta_in, out_pieces)
     in_pieces = exchange(delta_in, seqs_group)
     layer_out = (
         tokens.astype(f32) + returned(out_pieces).astype(f32) + full_out_b + full_down_b
     ).astype(bf16)
 
-    mlp_two, attn_pieces = after(widen(mlp_part), attn_pieces)
-    attn_mine = total(attn_pieces).astype(bf16)
-    attn_own, attn_far, attn_near = halve(attn_mine)
     mlp_all = whole_again(mlp_two)
     tokens_grad = cotangent.astype(f32) + returned(in_pieces).astype(f32)
     attn_all = whole_again(widen(quarter(attn_own, attn_far, attn_near)))

time: 374 us -> 368 us (0.984)
  starting transfers between devices: 50.7 us -> 38.8 us
  waiting for transfers between devices: 122 us -> 127 us
  matrix products: 14.4 us -> 18.5 us
    ppermute x35, starting transfers between devices: 50.7 us -> 38.8 us  [swap(): return lax.ppermute(x, axis, [(j, j ^ by) for j in range(n)])]
    ppermute x35, waiting for transfers between devices: 122 us -> 127 us  [swap(): return lax.ppermute(x, axis, [(j, j ^ by) for j in range(n)])]
    dot_general x5, matrix products: 14.4 us -> 18.5 us  [dot(): return lax.dot_general(a, b, dims, preferred_element_type=f32)]
    unnamed x127 -> x115, local copies, waits for them, and re-layouts: 8.26 us -> 8.11 us
  transfers between devices with their start and end apart: 35 -> 35, of which waited for: 11 -> 12; matrix products, arithmetic and copies ran while one was open for 21% -> 19% of each run, Pallas kernels for 27% -> 28%
where the time goes in v5:
time: 368 us; the launch traced here: 362 us
  waiting for transfers between devices  127 us (35%)
  Pallas kernels  101 us (27%)
  local copies, waits for them, and re-layouts  43.8 us (12%)
  starting transfers between devices  38.8 us (11%)
  other arithmetic  29.8 us (8%)
  matrix products  18.5 us (5%)
    ppermute x35, waiting for transfers between devices, swap(): return lax.ppermute(x, axis, [(j, j ^ by) for j in range(n)])  127 us
    pallas_call x1, Pallas kernels, attention(): pl.pallas_call(functools.partial(attention_kernel, seq_len=seq_len, rows=...  60.1 us
    pallas_call x1, Pallas kernels, mlp(): pl.pallas_call(functools.partial(mlp_kernel, layout=layout, fsdp=fsdp, ow...  40.9 us
    ppermute x35, starting transfers between devices, swap(): return lax.ppermute(x, axis, [(j, j ^ by) for j in range(n)])  38.8 us
    dot_general x5, matrix products, dot(): return lax.dot_general(a, b, dims, preferred_element_type=f32)  18.5 us
    dynamic_update_slice x29, local copies, waits for them, and re-layouts, place(): lax.dynamic_update_slice_in_dim(out, piece, at * piece.shape[axis], axis)  10.7 us
    unnamed x115, local copies, waits for them, and re-layouts  8.11 us
  transfers between devices with their start and end apart: 35, of which 12 were waited for; matrix products, arithmetic and copies ran while one was open for 19% of the time, Pallas kernels for 28%

profile of v5, /device:TPU:0, one launch (start us, length us, event | category | flops | bytes accessed | tf_op | source)
XLA Modules:
  0.0 361.7 jit_solution(10693425389147160608)
XLA Ops:
  0.7 5.4 %concatenate.72 = bf16[2496]{0:T(1024)(128)(2,1)S(1)} concatenate(bf16[576]{0:T(1024)(128)(2,1)} %param.21, bf16[192]{0:T(256)(128)(2,1)} %param.23, bf16[768]{0:T(1024)(128)(2,1)} %param.25, bf16[192]{0:T(256)(128)(2,1)} %param.27, bf16[192]{0:T(256)(128)(2,1)} %param.28, bf16[192]{0:T(256)(128)(2,1)} %param.29, bf16[192]{0:T(256)(128)(2,1)} %param.30, bf16[192]{0:T(256)(128)(2,1)} %param.31), dimensions={0} | concatenate | bytes 9984 | tf_op jit(solution)/shard_map/concatenate | solution.py:562
  6.1 1.4 fusion.56
  7.9 1.2 fusion.16.refs_0_
  9.1 2.9 collective-permute-start.4
  12.0 1.5 collective-permute-start.5
  14.6 1.6 collective-permute-start
  16.2 2.7 collective-permute-start.1
  23.6 1.2 pad_add_fusion.scalar_ref
  24.8 16.2 %collective-permute-done = bf16[2,192,768]{2,1,0:T(8,128)(2,1)} collective-permute-done((bf16[2,192,768]{2,1,0:T(8,128)(2,1)}, bf16[2,192,768]{2,1,0:T(8,128)(2,1)}, u32[]{:S(2)}, u32[]{:S(2)}) %collective-permute-start) | collective-permute-done | bytes 589856 | tf_op jit(solution)/shard_map/ppermute | solution.py:439
  43.2 15.6 %collective-permute-done.1 = bf16[2,192,768]{2,1,0:T(8,128)(2,1)} collective-permute-done((bf16[2,192,768]{2,1,0:T(8,128)(2,1)S(1)}, bf16[2,192,768]{2,1,0:T(8,128)(2,1)}, u32[]{:S(2)}, u32[]{:S(2)}) %collective-permute-start.1) | collective-permute-done | bytes 589856 | tf_op jit(solution)/shard_map/ppermute | solution.py:439
  61.9 11.6 %collective-permute-done.5.refs_2_ = bf16[224,3072]{1,0:T(8,128)(2,1)} collective-permute-done((bf16[224,3072]{1,0:T(8,128)(2,1)}, bf16[224,3072]{1,0:T(8,128)(2,1)}, u32[]{:S(2)}, u32[]{:S(2)}) %collective-permute-start.5) | collective-permute-done | bytes 1376288 | tf_op jit(solution)/shard_map/ppermute | solution.py:439
  80.0 1.4 collective-permute-start.9
  84.8 1.9 select_bitcast_fusion.3
  87.0 1.6 copy.42
  88.8 1.6 copy.43
  90.4 40.9 %mlp.1 = (bf16[1536,768]{1,0:T(8,128)(2,1)}, f32[1536,768]{1,0:T(8,128)}, f32[1536,768]{1,0:T(8,128)}, bf16[1,208,3072]{2,1,0:T(8,128)(2,1)}, bf16[1,208,3072]{2...) custom-call(s32[1]{0:T(128)} %bitcast.5.shard_ref, bf16[1536,768]{1,0:T(8,128)(2,1)} %bitcast.346, ...), custom_call_target="tpu_custom_call" | custom-call | flops 21743271936 | bytes 30000000 | tf_op jit(solution)/shard_map/mlp/pallas_call | solution.py:395
  133.9 1.2 collective-permute-start.10
  136.0 1.4 collective-permute-start.12
  137.5 60.1 %attention.1 = (bf16[1536,384]{1,0:T(8,128)(2,1)}, bf16[1536,1152]{1,0:T(8,128)(2,1)}) custom-call(s32[3]{0:T(128)} %pad_add_fusion.scalar_ref, bf16[1536,768]{1,0:T(8,128)(2,1)} %get-tuple-element.79.attn_in_ref, bf16[1536,768]{1,0:T(8,128)(2,1)} %bitcast.335, f32[1,1152]{1,0:T(1,128)} %copy-done.28, f32[1536,128]{1,0:T(8,128)} %constant.88.clone.cos_ref, ...), custom_call_target="tpu_custom_call" | custom-call | flops 14495514624 | bytes 12000000 | tf_op jit(solution)/shard_map/attention/pallas_call | solution.py:226
  197.6 2.5 fusion.17
  201.2 1.6 collective-permute-start.13
  208.6 1.4 fusion.24
  212.5 1.3 copy-done
  213.8 1.5 convolution_convert_fusion.2
  219.0 4.7 %convolution_convert_fusion = bf16[768,1152]{1,0:T(8,128)(2,1)} fusion(bf16[1536,768]{1,0:T(8,128)(2,1)S(1)} %copy-done.30, bf16[1536,1152]{1,0:T(8,128)(2,1)S(1)} %copy-done.10), kind=kOutput, calls=%fused_computation.10 | convolution fusion | flops 2718793728 | bytes 7667712 | tf_op jit(solution)/shard_map/dot_general | solution.py:34
  225.6 2.7 collective-permute-start.17
  228.3 8.7 %multiply_reduce_fusion = (bf16[768]{0:T(1024)(128)(2,1)S(1)}, bf16[768]{0:T(1024)(128)(2,1)S(1)}, bf16[1536,768]{1,0:T(8,128)(2,1)S(1)}) fusion(f32[1536]{0:T(1024)} %rsqrt.21, f32[1536]{0:T(1024)} %div.34, bf16[4,2,192,768]{3,2,1,0:T(8,128)(2,1)} %copy.42, f32[1536,768]{1,0:T(8,128)} %get-tuple-element.105, f32[768]{0:T(1024)} %reshape.344, ...), kind=kOutput, calls=%fused_computation.9 | convolution fusion | flops 2729703936 | bytes 14767104 | tf_op jit(solution)/shard_map/dot_general | solution.py:34
  237.5 5.8 %collective-permute-done.17 = bf16[208,768]{1,0:T(8,128)(2,1)S(1)} collective-permute-done((bf16[208,768]{1,0:T(8,128)(2,1)S(1)}, bf16[208,768]{1,0:T(8,128)(2,1)S(1)}, u32[]{:S(2)}, u32[]{:S(2)}) %collective-permute-start.17) | collective-permute-done | bytes 319520 | tf_op jit(solution)/shard_map/ppermute | solution.py:439
  244.5 1.6 fusion.15
  246.3 3.2 collective-permute-start.23
  249.6 2.2 select_bitcast_fusion.9
  252.6 1.2 collective-permute-start.18
  254.7 1.4 collective-permute-start.20
  257.0 13.0 %collective-permute-done.18 = bf16[1,208,1536]{2,1,0:T(8,128)(2,1)S(1)} collective-permute-done((bf16[1,208,1536]{2,1,0:T(8,128)(2,1)S(1)}, bf16[1,208,1536]{2,1,0:T(8,128)(2,1)S(1)}, u32[]{:S(2)}, u32[]{:S(2)}) %collective-permute-start.18) | collective-permute-done | bytes 639008 | tf_op jit(solution)/shard_map/ppermute | solution.py:439
  271.1 10.0 %collective-permute-done.19 = bf16[1,208,1536]{2,1,0:T(8,128)(2,1)S(1)} collective-permute-done((bf16[1,208,1536]{2,1,0:T(8,128)(2,1)S(1)}, bf16[1,208,1536]{2,1,0:T(8,128)(2,1)S(1)}, u32[]{:S(2)}, u32[]{:S(2)}) %collective-permute-start.19) | collective-permute-done | bytes 639008 | tf_op jit(solution)/shard_map/ppermute | solution.py:439
  281.1 1.6 collective-permute-done.20
  284.6 1.7 collective-permute-start.32
  286.6 9.2 %collective-permute-done.21 = bf16[2,208,384]{2,1,0:T(8,128)(2,1)S(1)} collective-permute-done((bf16[2,208,384]{2,1,0:T(8,128)(2,1)S(1)}, bf16[2,208,384]{2,1,0:T(8,128)(2,1)S(1)}, u32[]{:S(2)}, u32[]{:S(2)}) %collective-permute-start.21) | collective-permute-done | bytes 319520 | tf_op jit(solution)/shard_map/ppermute | solution.py:439
  296.0 3.3 collective-permute-start.26
  301.0 2.2 collective-permute-done.32
  305.3 1.5 add_convert_fusion.3
  306.8 25.7 %collective-permute-done.28 = bf16[208,384]{1,0:T(8,128)(2,1)S(1)} collective-permute-done((bf16[208,384]{1,0:T(8,128)(2,1)S(1)}, bf16[208,384]{1,0:T(8,128)(2,1)S(1)}, u32[]{:S(2)}, u32[]{:S(2)}) %collective-permute-start.28) | collective-permute-done | bytes 159776 | tf_op jit(solution)/shard_map/ppermute | solution.py:439
  332.8 7.4 %collective-permute-done.29 = bf16[208,384]{1,0:T(8,128)(2,1)S(1)} collective-permute-done((bf16[208,384]{1,0:T(8,128)(2,1)S(1)}, bf16[208,384]{1,0:T(8,128)(2,1)S(1)}, u32[]{:S(2)}, u32[]{:S(2)}) %collective-permute-start.29) | collective-permute-done | bytes 159776 | tf_op jit(solution)/shard_map/ppermute | solution.py:439
  340.5 8.6 %collective-permute-done.30 = bf16[2,208,384]{2,1,0:T(8,128)(2,1)S(1)} collective-permute-done((bf16[2,208,384]{2,1,0:T(8,128)(2,1)S(1)}, bf16[2,208,384]{2,1,0:T(8,128)(2,1)S(1)}, u32[]{:S(2)}, u32[]{:S(2)}) %collective-permute-start.30) | collective-permute-done | bytes 319520 | tf_op jit(solution)/shard_map/ppermute | solution.py:439
  349.2 1.6 convert_add_fusion.2
  352.1 1.3 convert_element_type.392
  356.8 1.7 convert_element_type.396
  359.1 1.6 maximum_convert_fusion
  (303 shorter events, 57.1 us)
Async XLA Ops:
  7.8 5.7 %copy-start.6 = (bf16[4,192,768]{2,1,0:T(8,128)(2,1)S(1)}, bf16[4,192,768]{2,1,0:T(8,128)(2,1)}, u32[]{:S(2)}) copy-start(bf16[4,192,768]{2,1,0:T(8,128)(2,1)} %param.17) | copy-start | bytes 3538948
  7.9 5.7 %copy-start.8 = (bf16[4,192,768]{2,1,0:T(8,128)(2,1)S(1)}, bf16[4,192,768]{2,1,0:T(8,128)(2,1)}, u32[]{:S(2)}) copy-start(bf16[4,192,768]{2,1,0:T(8,128)(2,1)} %param.19) | copy-start | bytes 3538948
  9.1 52.8 %collective-permute-start.4 = (bf16[224,3072]{1,0:T(8,128)(2,1)}, bf16[224,3072]{1,0:T(8,128)(2,1)}, u32[]{:S(2)}, u32[]{:S(2)}) collective-permute-start(bf16[224,3072]{1,0:T(8,128)(2,1)} %fusion.16.refs_0_), channel_id=1, source_target_pairs={{0,1},{1,0},{2,3},{3,2},{4,5},{5,4},{6,7},{7,6},{8,9},{9,8},{10,11... | collective-permute-start | bytes 4128776 | tf_op jit(solution)/shard_map/ppermute | solution.py:439
  12.0 61.4 %collective-permute-start.5 = (bf16[224,3072]{1,0:T(8,128)(2,1)}, bf16[224,3072]{1,0:T(8,128)(2,1)}, u32[]{:S(2)}, u32[]{:S(2)}) collective-permute-start(bf16[224,3072]{1,0:T(8,128)(2,1)} %fusion.16.refs_0_), channel_id=1, source_target_pairs={{0,2},{1,3},{2,0},{3,1},{4,6},{5,7},{6,4},{7,5},{8,10},{9,11},{10,... | collective-permute-start | bytes 4128776 | tf_op jit(solution)/shard_map/ppermute | solution.py:439
  14.6 5.4 %copy-start.15 = (bf16[192,2304]{1,0:T(8,128)(2,1)S(1)}, bf16[192,2304]{1,0:T(8,128)(2,1)}, u32[]{:S(2)}) copy-start(bf16[192,2304]{1,0:T(8,128)(2,1)} %param.20) | copy-start | bytes 2654212
  14.6 26.5 %collective-permute-start = (bf16[2,192,768]{2,1,0:T(8,128)(2,1)}, bf16[2,192,768]{2,1,0:T(8,128)(2,1)}, u32[]{:S(2)}, u32[]{:S(2)}) collective-permute-start(bf16[2,192,768]{2,1,0:T(8,128)(2,1)} %pad_maximum_fusion.2), channel_id=1, source_target_pairs={{0,8},{4,12},{8,0},{12,4},{16,24},{20,28},{24,16},{28,20},{1,9},{5... | collective-permute-start | bytes 1769480 | tf_op jit(solution)/shard_map/ppermute | solution.py:439
  16.2 42.6 %collective-permute-start.1 = (bf16[2,192,768]{2,1,0:T(8,128)(2,1)S(1)}, bf16[2,192,768]{2,1,0:T(8,128)(2,1)}, u32[]{:S(2)}, u32[]{:S(2)}) collective-permute-start(bf16[2,192,768]{2,1,0:T(8,128)(2,1)S(1)} %pad_maximum_fusion.3), channel_id=1, source_target_pairs={{0,16},{4,20},{8,24},{12,28},{16,0},{20,4},{24,8},{28,12},{1,17},{... | collective-permute-start | bytes 1769480 | tf_op jit(solution)/shard_map/ppermute | solution.py:439
  19.7 40.2 %collective-permute-start.2 = (bf16[2,192,768]{2,1,0:T(8,128)(2,1)}, bf16[2,192,768]{2,1,0:T(8,128)(2,1)}, u32[]{:S(2)}, u32[]{:S(2)}) collective-permute-start(bf16[2,192,768]{2,1,0:T(8,128)(2,1)} %pad_maximum_fusion.4), channel_id=1, source_target_pairs={{0,24},{4,28},{8,16},{12,20},{16,8},{20,12},{24,0},{28,4},{1,25},{... | collective-permute-start | bytes 1769480 | tf_op jit(solution)/shard_map/ppermute | solution.py:439
  41.0 32.4 %collective-permute-start.6 = (bf16[224,3072]{1,0:T(8,128)(2,1)}, bf16[224,3072]{1,0:T(8,128)(2,1)S(1)}, u32[]{:S(2)}, u32[]{:S(2)}) collective-permute-start(bf16[224,3072]{1,0:T(8,128)(2,1)} %fusion.16.refs_0_), channel_id=1, source_target_pairs={{0,3},{1,2},{2,1},{3,0},{4,7},{5,6},{6,5},{7,4},{8,11},{9,10},{10,... | collective-permute-start | bytes 4128776 | tf_op jit(solution)/shard_map/ppermute | solution.py:439
  61.1 16.8 %copy-start.17 = (bf16[192,1920]{1,0:T(8,128)(2,1)S(1)}, bf16[192,1920]{1,0:T(8,128)(2,1)}, u32[]{:S(2)}) copy-start(bf16[192,1920]{1,0:T(8,128)(2,1)} %copy-done.16) | copy-start | bytes 2211844
  61.1 23.7 %collective-permute-start.3 = (bf16[4,2,192,768]{3,2,0,1:T(8,128)(2,1)S(1)}, bf16[4,2,192,768]{3,2,0,1:T(8,128)(2,1)}, u32[]{:S(2)}, u32[]{:S(2)}) collective-permute-start(bf16[4,2,192,768]{3,2,0,1:T(8,128)(2,1)S(1)} %bitcast_dynamic-update-slice_fusion), channel_id=1, source_target_pairs={{0,4},{4,0},{8,12},{12,8},{16,20},{20,16},{24,28},{28,24},{1,5},{5... | collective-permute-start | bytes 7077896 | tf_op jit(solution)/shard_map/ppermute | solution.py:439
  77.9 56.0 %collective-permute-start.7 = (bf16[192,1920]{1,0:T(8,128)(2,1)S(1)}, bf16[192,1920]{1,0:T(8,128)(2,1)}, u32[]{:S(2)}, u32[]{:S(2)}) collective-permute-start(bf16[192,1920]{1,0:T(8,128)(2,1)S(1)} %copy-done.17), channel_id=1, source_target_pairs={{0,1},{1,0},{2,3},{3,2},{4,5},{5,4},{6,7},{7,6},{8,9},{9,8},{10,11... | collective-permute-start | bytes 2211848 | tf_op jit(solution)/shard_map/ppermute | solution.py:439
  79.0 54.9 %collective-permute-start.8 = (bf16[192,1920]{1,0:T(8,128)(2,1)S(1)}, bf16[192,1920]{1,0:T(8,128)(2,1)}, u32[]{:S(2)}, u32[]{:S(2)}) collective-permute-start(bf16[192,1920]{1,0:T(8,128)(2,1)S(1)} %copy-done.17), channel_id=1, source_target_pairs={{0,2},{1,3},{2,0},{3,1},{4,6},{5,7},{6,4},{7,5},{8,10},{9,11},{10,... | collective-permute-start | bytes 2211848 | tf_op jit(solution)/shard_map/ppermute | solution.py:439
  80.0 53.9 %collective-permute-start.9 = (bf16[192,1920]{1,0:T(8,128)(2,1)S(1)}, bf16[192,1920]{1,0:T(8,128)(2,1)}, u32[]{:S(2)}, u32[]{:S(2)}) collective-permute-start(bf16[192,1920]{1,0:T(8,128)(2,1)S(1)} %copy-done.17), channel_id=1, source_target_pairs={{0,3},{1,2},{2,1},{3,0},{4,7},{5,6},{6,5},{7,4},{8,11},{9,10},{10,... | collective-permute-start | bytes 2211848 | tf_op jit(solution)/shard_map/ppermute | solution.py:439
  133.9 63.7 %copy-start.13 = (bf16[1,208,3072]{2,1,0:T(8,128)(2,1)S(1)}, bf16[1,208,3072]{2,1,0:T(8,128)(2,1)}, u32[]{:S(2)}) copy-start(bf16[1,208,3072]{2,1,0:T(8,128)(2,1)} %get-tuple-element.93) | copy-start | bytes 3833860
  133.9 63.7 %collective-permute-start.10 = (bf16[1,208,3072]{2,1,0:T(8,128)(2,1)}, bf16[1,208,3072]{2,1,0:T(8,128)(2,1)S(1)}, u32[]{:S(2)}, u32[]{:S(2)}) collective-permute-start(bf16[1,208,3072]{2,1,0:T(8,128)(2,1)} %get-tuple-element.88), channel_id=1, source_target_pairs={{0,1},{1,0},{2,3},{3,2},{4,5},{5,4},{6,7},{7,6},{8,9},{9,8},{10,11... | collective-permute-start | bytes 3833864 | tf_op jit(solution)/shard_map/ppermute | solution.py:439
  135.1 62.5 %collective-permute-start.11 = (bf16[1,208,3072]{2,1,0:T(8,128)(2,1)}, bf16[1,208,3072]{2,1,0:T(8,128)(2,1)}, u32[]{:S(2)}, u32[]{:S(2)}) collective-permute-start(bf16[1,208,3072]{2,1,0:T(8,128)(2,1)} %get-tuple-element.89), channel_id=1, source_target_pairs={{0,2},{1,3},{2,0},{3,1},{4,6},{5,7},{6,4},{7,5},{8,10},{9,11},{10,... | collective-permute-start | bytes 3833864 | tf_op jit(solution)/shard_map/ppermute | solution.py:439
  136.0 61.6 %collective-permute-start.12 = (bf16[1,208,3072]{2,1,0:T(8,128)(2,1)}, bf16[1,208,3072]{2,1,0:T(8,128)(2,1)}, u32[]{:S(2)}, u32[]{:S(2)}) collective-permute-start(bf16[1,208,3072]{2,1,0:T(8,128)(2,1)} %get-tuple-element.90), channel_id=1, source_target_pairs={{0,3},{1,2},{2,1},{3,0},{4,7},{5,6},{6,5},{7,4},{8,11},{9,10},{10,... | collective-permute-start | bytes 3833864 | tf_op jit(solution)/shard_map/ppermute | solution.py:439
  201.2 15.2 %collective-permute-start.13 = (bf16[2,208,768]{2,1,0:T(8,128)(2,1)S(1)}, bf16[2,208,768]{2,1,0:T(8,128)(2,1)S(1)}, u32[]{:S(2)}, u32[]{:S(2)}) collective-permute-start(bf16[2,208,768]{2,1,0:T(8,128)(2,1)S(1)} %pad_maximum_fusion), channel_id=1, source_target_pairs={{0,8},{4,12},{8,0},{12,4},{16,24},{20,28},{24,16},{28,20},{1,9},{5... | collective-permute-start | bytes 1916936 | tf_op jit(solution)/shard_map/ppermute | solution.py:439
  202.8 46.8 %collective-permute-start.14 = (bf16[1536,384]{1,0:T(8,128)(2,1)S(1)}, bf16[1536,384]{1,0:T(8,128)(2,1)}, u32[]{:S(2)}, u32[]{:S(2)}) collective-permute-start(bf16[1536,384]{1,0:T(8,128)(2,1)S(1)} %copy-done.4), channel_id=1, source_target_pairs={{0,4},{4,0},{8,12},{12,8},{16,20},{20,16},{24,28},{28,24},{1,5},{5... | collective-permute-start | bytes 3538952 | tf_op jit(solution)/shard_map/ppermute | solution.py:439
  210.9 4.5 %copy-start.2 = (bf16[1536,768]{1,0:T(8,128)(2,1)}, bf16[1536,768]{1,0:T(8,128)(2,1)S(1)}, u32[]{:S(2)}) copy-start(bf16[1536,768]{1,0:T(8,128)(2,1)S(1)} %add_convert_fusion) | copy-start | bytes 7077892
  212.0 4.5 %copy-start.10 = (bf16[1536,1152]{1,0:T(8,128)(2,1)S(1)}, bf16[1536,1152]{1,0:T(8,128)(2,1)}, u32[]{:S(2)}) copy-start(bf16[1536,1152]{1,0:T(8,128)(2,1)} %get-tuple-element.99) | copy-start | bytes 10616836
  212.0 32.5 %collective-permute-start.16 = (bf16[1,4,192,768]{3,2,1,0:T(8,128)(2,1)}, bf16[1,4,192,768]{3,2,1,0:T(8,128)(2,1)}, u32[]{:S(2)}, u32[]{:S(2)}) collective-permute-start(bf16[1,4,192,768]{3,2,1,0:T(8,128)(2,1)} %dynamic-slice_bitcast_fusion), channel_id=1, source_target_pairs={{0,4},{4,0},{8,12},{12,8},{16,20},{20,16},{24,28},{28,24},{1,5},{5... | collective-permute-start | bytes 3538952 | tf_op jit(solution)/shard_map/ppermute | solution.py:439
  225.6 17.8 %collective-permute-start.17 = (bf16[208,768]{1,0:T(8,128)(2,1)S(1)}, bf16[208,768]{1,0:T(8,128)(2,1)S(1)}, u32[]{:S(2)}, u32[]{:S(2)}) collective-permute-start(bf16[208,768]{1,0:T(8,128)(2,1)S(1)} %fusion.20), channel_id=1, source_target_pairs={{0,16},{4,20},{8,24},{12,28},{16,0},{20,4},{24,8},{28,12},{1,17},{... | collective-permute-start | bytes 958472 | tf_op jit(solution)/shard_map/ppermute | solution.py:439
  228.3 8.8 %copy-start.23 = (bf16[4,576]{1,0:T(4,128)(2,1)S(1)}, bf16[4,576]{1,0:T(4,128)(2,1)}, u32[]{:S(2)}) copy-start(bf16[4,576]{1,0:T(4,128)(2,1)} %convert_element_type.341) | copy-start | bytes 13828
  237.0 6.3 %copy-start.20 = (bf16[2,208,768]{2,1,0:T(8,128)(2,1)S(1)}, bf16[2,208,768]{2,1,0:T(8,128)(2,1)}, u32[]{:S(2)}) copy-start(bf16[2,208,768]{2,1,0:T(8,128)(2,1)} %copy-done.19) | copy-start | bytes 1916932
  237.1 7.3 %copy-start.3 = (bf16[1536,768]{1,0:T(8,128)(2,1)S(1)}, bf16[1536,768]{1,0:T(8,128)(2,1)}, u32[]{:S(2)}) copy-start(bf16[1536,768]{1,0:T(8,128)(2,1)} %copy-done.2) | copy-start | bytes 7077892
  237.2 14.9 %collective-permute-start.15 = (bf16[1,4,192,768]{3,2,1,0:T(8,128)(2,1)S(1)}, bf16[1,4,192,768]{3,2,1,0:T(8,128)(2,1)S(1)}, u32[]{:S(2)}, u32[]{:S(2)}) collective-permute-start(bf16[1,4,192,768]{3,2,1,0:T(8,128)(2,1)S(1)} %dynamic-slice_bitcast_fusion.1), channel_id=1, source_target_pairs={{0,4},{4,0},{8,12},{12,8},{16,20},{20,16},{24,28},{28,24},{1,5},{5... | collective-permute-start | bytes 3538952 | tf_op jit(solution)/shard_map/ppermute | solution.py:439
  244.5 5.1 %copy-start.14 = (bf16[384,384]{1,0:T(8,128)(2,1)S(1)}, bf16[384,384]{1,0:T(8,128)(2,1)}, u32[]{:S(2)}) copy-start(bf16[384,384]{1,0:T(8,128)(2,1)} %convolution_convert_fusion.2) | copy-start | bytes 884740
  246.3 49.5 %collective-permute-start.22 = (bf16[1,192,768]{2,1,0:T(8,128)(2,1)S(1)}, bf16[1,192,768]{2,1,0:T(8,128)(2,1)S(1)}, u32[]{:S(2)}, u32[]{:S(2)}) collective-permute-start(bf16[1,192,768]{2,1,0:T(8,128)(2,1)S(1)} %get-tuple-element.155), channel_id=1, source_target_pairs={{0,8},{4,12},{8,0},{12,4},{16,24},{20,28},{24,16},{28,20},{1,9},{5... | collective-permute-start | bytes 884744 | tf_op jit(solution)/shard_map/ppermute | solution.py:439
  246.3 49.4 %collective-permute-start.23 = (bf16[1,192,768]{2,1,0:T(8,128)(2,1)S(1)}, bf16[1,192,768]{2,1,0:T(8,128)(2,1)S(1)}, u32[]{:S(2)}, u32[]{:S(2)}) collective-permute-start(bf16[1,192,768]{2,1,0:T(8,128)(2,1)S(1)} %get-tuple-element.154), channel_id=1, source_target_pairs={{0,16},{4,20},{8,24},{12,28},{16,0},{20,4},{24,8},{28,12},{1,17},{... | collective-permute-start | bytes 884744 | tf_op jit(solution)/shard_map/ppermute | solution.py:439
  252.6 17.4 %collective-permute-start.18 = (bf16[1,208,1536]{2,1,0:T(8,128)(2,1)S(1)}, bf16[1,208,1536]{2,1,0:T(8,128)(2,1)S(1)}, u32[]{:S(2)}, u32[]{:S(2)}) collective-permute-start(bf16[1,208,1536]{2,1,0:T(8,128)(2,1)S(1)} %get-tuple-element.139), channel_id=1, source_target_pairs={{0,1},{1,0},{2,3},{3,2},{4,5},{5,4},{6,7},{7,6},{8,9},{9,8},{10,11... | collective-permute-start | bytes 1916936 | tf_op jit(solution)/shard_map/ppermute | solution.py:439
  253.8 27.3 %collective-permute-start.19 = (bf16[1,208,1536]{2,1,0:T(8,128)(2,1)S(1)}, bf16[1,208,1536]{2,1,0:T(8,128)(2,1)S(1)}, u32[]{:S(2)}, u32[]{:S(2)}) collective-permute-start(bf16[1,208,1536]{2,1,0:T(8,128)(2,1)S(1)} %get-tuple-element.138), channel_id=1, source_target_pairs={{0,2},{1,3},{2,0},{3,1},{4,6},{5,7},{6,4},{7,5},{8,10},{9,11},{10,... | collective-permute-start | bytes 1916936 | tf_op jit(solution)/shard_map/ppermute | solution.py:439
  254.7 28.0 %collective-permute-start.20 = (bf16[1,208,1536]{2,1,0:T(8,128)(2,1)S(1)}, bf16[1,208,1536]{2,1,0:T(8,128)(2,1)S(1)}, u32[]{:S(2)}, u32[]{:S(2)}) collective-permute-start(bf16[1,208,1536]{2,1,0:T(8,128)(2,1)S(1)} %get-tuple-element.137), channel_id=1, source_target_pairs={{0,3},{1,2},{2,1},{3,0},{4,7},{5,6},{6,5},{7,4},{8,11},{9,10},{10,... | collective-permute-start | bytes 1916936 | tf_op jit(solution)/shard_map/ppermute | solution.py:439
  270.0 25.7 %collective-permute-start.24 = (bf16[1,192,768]{2,1,0:T(8,128)(2,1)S(1)}, bf16[1,192,768]{2,1,0:T(8,128)(2,1)S(1)}, u32[]{:S(2)}, u32[]{:S(2)}) collective-permute-start(bf16[1,192,768]{2,1,0:T(8,128)(2,1)S(1)} %get-tuple-element.153), channel_id=1, source_target_pairs={{0,24},{4,28},{8,16},{12,20},{16,8},{20,12},{24,0},{28,4},{1,25},{... | collective-permute-start | bytes 884744 | tf_op jit(solution)/shard_map/ppermute | solution.py:439
  283.1 12.6 %collective-permute-start.21 = (bf16[2,208,384]{2,1,0:T(8,128)(2,1)S(1)}, bf16[2,208,384]{2,1,0:T(8,128)(2,1)S(1)}, u32[]{:S(2)}, u32[]{:S(2)}) collective-permute-start(bf16[2,208,384]{2,1,0:T(8,128)(2,1)S(1)} %pad_maximum_fusion.6), channel_id=1, source_target_pairs={{0,8},{4,12},{8,0},{12,4},{16,24},{20,28},{24,16},{28,20},{1,9},{5... | collective-permute-start | bytes 958472 | tf_op jit(solution)/shard_map/ppermute | solution.py:439
  284.6 18.5 %collective-permute-start.32 = (bf16[208,768]{1,0:T(8,128)(2,1)S(1)}, bf16[208,768]{1,0:T(8,128)(2,1)S(1)}, u32[]{:S(2)}, u32[]{:S(2)}) collective-permute-start(bf16[208,768]{1,0:T(8,128)(2,1)S(1)} %fusion.22), channel_id=1, source_target_pairs={{0,16},{4,20},{8,24},{12,28},{16,0},{20,4},{24,8},{28,12},{1,17},{... | collective-permute-start | bytes 958472 | tf_op jit(solution)/shard_map/ppermute | solution.py:439
  295.9 36.8 %collective-permute-start.25 = (bf16[1,192,768]{2,1,0:T(8,128)(2,1)S(1)}, bf16[1,192,768]{2,1,0:T(8,128)(2,1)S(1)}, u32[]{:S(2)}, u32[]{:S(2)}) collective-permute-start(bf16[1,192,768]{2,1,0:T(8,128)(2,1)S(1)} %get-tuple-element.151), channel_id=1, source_target_pairs={{0,8},{4,12},{8,0},{12,4},{16,24},{20,28},{24,16},{28,20},{1,9},{5... | collective-permute-start | bytes 884744 | tf_op jit(solution)/shard_map/ppermute | solution.py:439
  296.0 44.3 %collective-permute-start.26 = (bf16[1,192,768]{2,1,0:T(8,128)(2,1)S(1)}, bf16[1,192,768]{2,1,0:T(8,128)(2,1)S(1)}, u32[]{:S(2)}, u32[]{:S(2)}) collective-permute-start(bf16[1,192,768]{2,1,0:T(8,128)(2,1)S(1)} %get-tuple-element.150), channel_id=1, source_target_pairs={{0,16},{4,20},{8,24},{12,28},{16,0},{20,4},{24,8},{28,12},{1,17},{... | collective-permute-start | bytes 884744 | tf_op jit(solution)/shard_map/ppermute | solution.py:439
  299.3 41.0 %collective-permute-start.27 = (bf16[1,192,768]{2,1,0:T(8,128)(2,1)S(1)}, bf16[1,192,768]{2,1,0:T(8,128)(2,1)S(1)}, u32[]{:S(2)}, u32[]{:S(2)}) collective-permute-start(bf16[1,192,768]{2,1,0:T(8,128)(2,1)S(1)} %get-tuple-element.149), channel_id=1, source_target_pairs={{0,24},{4,28},{8,16},{12,20},{16,8},{20,12},{24,0},{28,4},{1,25},{... | collective-permute-start | bytes 884744 | tf_op jit(solution)/shard_map/ppermute | solution.py:439
  300.4 32.0 %collective-permute-start.28 = (bf16[208,384]{1,0:T(8,128)(2,1)S(1)}, bf16[208,384]{1,0:T(8,128)(2,1)S(1)}, u32[]{:S(2)}, u32[]{:S(2)}) collective-permute-start(bf16[208,384]{1,0:T(8,128)(2,1)S(1)} %fusion.29), channel_id=1, source_target_pairs={{0,16},{4,20},{8,24},{12,28},{16,0},{20,4},{24,8},{28,12},{1,17},{... | collective-permute-start | bytes 479240 | tf_op jit(solution)/shard_map/ppermute | solution.py:439
  303.2 47.7 %collective-permute-start.33 = (bf16[2,208,768]{2,1,0:T(8,128)(2,1)S(1)}, bf16[2,208,768]{2,1,0:T(8,128)(2,1)S(1)}, u32[]{:S(2)}, u32[]{:S(2)}) collective-permute-start(bf16[2,208,768]{2,1,0:T(8,128)(2,1)S(1)} %pad_maximum_fusion.1), channel_id=1, source_target_pairs={{0,8},{4,12},{8,0},{12,4},{16,24},{20,28},{24,16},{28,20},{1,9},{5... | collective-permute-start | bytes 1916936 | tf_op jit(solution)/shard_map/ppermute | solution.py:439
  332.6 7.6 %collective-permute-start.29 = (bf16[208,384]{1,0:T(8,128)(2,1)S(1)}, bf16[208,384]{1,0:T(8,128)(2,1)S(1)}, u32[]{:S(2)}, u32[]{:S(2)}) collective-permute-start(bf16[208,384]{1,0:T(8,128)(2,1)S(1)} %get-tuple-element.129), channel_id=1, source_target_pairs={{0,16},{4,20},{8,24},{12,28},{16,0},{20,4},{24,8},{28,12},{1,17},{... | collective-permute-start | bytes 479240 | tf_op jit(solution)/shard_map/ppermute | solution.py:439
  340.2 9.0 %copy-start.9 = (bf16[4,192,768]{2,1,0:T(8,128)(2,1)S(1)}, bf16[4,192,768]{2,1,0:T(8,128)(2,1)}, u32[]{:S(2)}) copy-start(bf16[4,192,768]{2,1,0:T(8,128)(2,1)} %param.19) | copy-start | bytes 3538948
  340.2 8.8 %collective-permute-start.30 = (bf16[2,208,384]{2,1,0:T(8,128)(2,1)S(1)}, bf16[2,208,384]{2,1,0:T(8,128)(2,1)S(1)}, u32[]{:S(2)}, u32[]{:S(2)}) collective-permute-start(bf16[2,208,384]{2,1,0:T(8,128)(2,1)S(1)} %pad_maximum_fusion.7), channel_id=1, source_target_pairs={{0,8},{4,12},{8,0},{12,4},{16,24},{20,28},{24,16},{28,20},{1,9},{5... | collective-permute-start | bytes 958472 | tf_op jit(solution)/shard_map/ppermute | solution.py:439
  349.2 2.4 collective-permute-start.31
  351.0 4.6 %collective-permute-start.34 = (bf16[208,3072]{1,0:T(8,128)(2,1)S(1)}, bf16[208,3072]{1,0:T(8,128)(2,1)S(1)}, u32[]{:S(2)}, u32[]{:S(2)}) collective-permute-start(bf16[208,3072]{1,0:T(8,128)(2,1)S(1)} %fusion.26), channel_id=1, source_target_pairs={{0,4},{4,0},{8,12},{12,8},{16,20},{20,16},{24,28},{28,24},{1,5},{5... | collective-permute-start | bytes 3833864 | tf_op jit(solution)/shard_map/ppermute | solution.py:439
  356.6 4.1 %copy-start.26 = (f32[1,192]{1,0:T(1,128)}, f32[1,192]{1,0:T(1,128)S(1)}, u32[]{:S(2)}) copy-start(f32[1,192]{1,0:T(1,128)S(1)} %get-tuple-element.190) | copy-start | bytes 2308
  (20 other events, 40.2 us)
